TPU v7x, 512 devices: a whole 4x8x8 slice. The times are simulated.
512 devices in a mesh: grid: 64 (over x, y_hi, z), orb: 8 (over y_lo, core).
Axes of the slice: x: 4, y: 8 (y_hi: 2, y_lo: 4; y = y_hi * 4 + y_lo), z: 8, core: 2. Of those that a mesh axis runs over, the one named last changes fastest.
Arguments:
- orbitals: float32 [32, 1024, 32, 256], P('orb', 'grid'), may hold values from -6 to 6
- potential: float32 [1024, 32, 256], P('grid'), may hold values from -1 to 1
- lower_cut: float32 [1], replicated, may hold values from 0.5 to 1.5
- upper_bound: float32 [1], replicated, may hold values from 11 to 12
- rotation: float32 [32, 16], P('orb'), may hold values from -1 to 1
Outputs:
- filtered: float32 [32, 1024, 32, 256], P('orb', 'grid')
- rotated: float32 [16, 1024, 32, 256], P(None, 'grid', 'orb')
All inputs are finite; a program needn't handle non-finite values.
Results may differ from a plain program's by a relative error of at most 0.00011.
Values sent between devices are 32-bit elements; how exact they have to be, the bound alone decides.
No kernel may reach another device: no remote copies, remote signals or barrier semaphores. Data moves between devices by JAX's collectives and lax.ppermute only.
A program may use at most 64 MiB of HBM per device.

v0:
```python
import jax
import jax.numpy as jnp
from jax import lax
from jax.sharding import PartitionSpec as P

R = 2


STENCIL_WEIGHTS = (-5.0 / 2.0, 4.0 / 3.0, -1.0 / 12.0)
SPACING = 1.0


def padded(block, sides, width):
    for axis, dim in sides:
        count = lax.axis_size(axis)
        forward = [(i, i + 1) for i in range(count - 1)]
        forward.append((count - 1, 0))
        backward = [(target, source) for source, target in forward]
        low = lax.ppermute(
            lax.slice_in_dim(block, block.shape[dim] - width, None, axis=dim), axis, forward
        )
        high = lax.ppermute(lax.slice_in_dim(block, 0, width, axis=dim), axis, backward)
        block = jnp.concatenate([low, block, high], axis=dim)
    return block


def apply_hamilton(extended, local_potential, margin):
    planes = extended.shape[1] - 2 * margin
    interior = extended[:, margin : margin + planes]
    summed = 3.0 * STENCIL_WEIGHTS[0] * interior
    for offset in range(1, R + 1):
        beside_all = (
            extended[:, margin + offset : margin + offset + planes]
            + extended[:, margin - offset : margin - offset + planes]
        )
        beside_all = beside_all + jnp.roll(interior, offset, 2) + jnp.roll(interior, -offset, 2)
        beside_all = beside_all + jnp.roll(interior, offset, 3) + jnp.roll(interior, -offset, 3)
        summed = summed + STENCIL_WEIGHTS[offset] * beside_all
    return -0.5 * summed / (SPACING * SPACING) + local_potential * interior


def extend_planes(field):
    return padded(field, (("grid", 1),), R)


def body(orbitals, potential, lower_cut, upper_bound, rotation):
    middle = (upper_bound[0] + lower_cut[0]) * 0.5
    half_width = (upper_bound[0] - lower_cut[0]) * 0.5
    first = (apply_hamilton(extend_planes(orbitals), potential, R) - middle * orbitals) / half_width
    filtered = (
        2.0 * (apply_hamilton(extend_planes(first), potential, R) - middle * first) / half_width
        - orbitals
    )
    regrouped = lax.all_to_all(filtered, "orb", split_axis=2, concat_axis=0, tiled=True)
    full_rows = lax.all_gather(rotation, "orb", axis=0, tiled=True)
    flat = regrouped.reshape(regrouped.shape[0], -1)
    rotated = jnp.dot(
        full_rows.T, flat, precision=lax.Precision.HIGHEST, preferred_element_type=jnp.float32
    )
    return (filtered, rotated.reshape((full_rows.shape[1],) + regrouped.shape[1:]))


def solution(mesh):
    in_specs = (P("orb", "grid", None, None), P("grid", None, None), P(), P(), P("orb", None))
    out_specs = (P("orb", "grid", None, None), P(None, "grid", "orb", None))
    return jax.shard_map(body, mesh=mesh, in_specs=in_specs, out_specs=out_specs, check_vma=False)
```

profile of v0, /device:TPU:1, one launch (start us, length us, event | category | flops | bytes accessed | tf_op | source)
XLA Modules:
  0.0 166.4 jit_solution(26727825742083862)
XLA Ops:
  0.6 1.1 fusion.55
  1.7 4.8 %collective-permute-start.1 = (f32[4,2,32,256]{3,2,1,0:T(8,128)S(1)}, f32[4,2,32,256]{3,2,1,0:T(8,128)S(1)}, u32[]{:S(2)}, u32[]{:S(2)}) collective-permute-start(f32[4,2,32,256]{3,2,1,0:T(8,128)S(1)} %get-tuple-element.39), channel_id=1, source_target_pairs={{0,8},{8,16},{16,24},{24,32},{32,40},{40,48},{48,56},{56,64},{64,7... | collective-permute-start | bytes 786440 | tf_op jit(solution)/shard_map/ppermute | solution.py:19
  6.5 0.0 copy-start
  6.6 16.2 %collective-permute-start = (f32[4,2,32,256]{3,2,1,0:T(8,128)S(1)}, f32[4,2,32,256]{3,2,1,0:T(8,128)S(1)}, u32[]{:S(2)}, u32[]{:S(2)}) collective-permute-start(f32[4,2,32,256]{3,2,1,0:T(8,128)S(1)} %get-tuple-element.38), channel_id=1, source_target_pairs={{8,0},{16,8},{24,16},{32,24},{40,32},{48,40},{56,48},{64,56},{72,6... | collective-permute-start | bytes 786440 | tf_op jit(solution)/shard_map/ppermute | solution.py:22
  22.7 3.1 %fusion.47 = (f32[4,16,32,254]{3,2,1,0:T(8,128)S(1)}, f32[4,16,32,254]{3,2,1,0:T(8,128)S(1)}) fusion(f32[4,16,32,256]{3,2,1,0:T(8,128)} %param.5), kind=kLoop, calls=%fused_computation.61 | loop fusion | bytes 8323072 | tf_op jit(solution)/shard_map/jit(_roll_static)/slice | solution.py:37
  25.8 0.0 copy-done
  25.8 0.5 fusion.49
  26.4 2.8 %fusion.51 = (f32[4,16,32,255]{3,2,1,0:T(8,128)}, f32[4,16,32,255]{3,2,1,0:T(8,128)}) fusion(f32[4,16,32,256]{3,2,1,0:T(8,128)S(1)} %copy-done), kind=kLoop, calls=%fused_computation.65 | loop fusion | bytes 8355840 | tf_op jit(solution)/shard_map/jit(_roll_static)/slice | solution.py:37
  29.1 2.4 %fusion.53 = (f32[4,16,31,256]{3,2,1,0:T(8,128)}, f32[4,16,31,256]{3,2,1,0:T(8,128)}) fusion(f32[4,16,32,256]{3,2,1,0:T(8,128)S(1)} %copy-done), kind=kLoop, calls=%fused_computation.67 | loop fusion | bytes 8126464 | tf_op jit(solution)/shard_map/jit(_roll_static)/slice | solution.py:36
  31.6 1.5 fusion.48
  33.0 1.7 %fusion.52 = (f32[4,16,32,1]{3,2,1,0:T(8,128)}, f32[4,16,32,1]{3,2,1,0:T(8,128)}) fusion(f32[4,16,32,256]{3,2,1,0:T(8,128)S(1)} %copy-done), kind=kLoop, calls=%fused_computation.66 | loop fusion | bytes 32768 | tf_op jit(solution)/shard_map/jit(_roll_static)/slice | solution.py:37
  34.7 0.1 fusion.54
  36.1 0.1 fusion.50
  36.2 0.0 collective-permute-done.1
  36.2 0.0 copy-start.2
  36.2 0.5 constant_dynamic-update-slice_fusion.1
  36.8 0.0 collective-permute-done
  36.8 0.4 copy-done.2
  37.3 6.6 %fusion.31 = f32[4,16,32,256]{3,2,1,0:T(8,128)S(1)} fusion(f32[4,18,32,256]{3,2,1,0:T(8,128)S(1)} %get-tuple-element.41, f32[4,18,32,256]{3,2,1,0:T(8,128)S(1)} %constant_dynamic-update-slice_fusion, f32[4,16,31,256]{3,2,1,0:T(8,128)} %get-tuple-element.35, f32[4,16,1,256]{3,2,1,0:T(1,128)S(1)} %get-tuple-element.37, ...), kind=kLoop, calls=%fused_computation.39 | loop fusion | flops 15204352 | bytes 29884424 | tf_op jit(solution)/shard_map/div | solution.py:49
  43.9 0.8 fusion.42
  44.7 2.4 %fusion.44 = (f32[4,16,31,256]{3,2,1,0:T(8,128)}, f32[4,16,31,256]{3,2,1,0:T(8,128)}) fusion(f32[4,16,32,256]{3,2,1,0:T(8,128)S(1)} %fusion.31), kind=kLoop, calls=%fused_computation.58 | loop fusion | bytes 8126464 | tf_op jit(solution)/shard_map/jit(_roll_static)/slice | solution.py:36
  47.2 2.8 %fusion.38 = (f32[4,16,32,254]{3,2,1,0:T(8,128)}, f32[4,16,32,254]{3,2,1,0:T(8,128)}) fusion(f32[4,16,32,256]{3,2,1,0:T(8,128)S(1)} %fusion.31), kind=kLoop, calls=%fused_computation.52 | loop fusion | bytes 8323072 | tf_op jit(solution)/shard_map/jit(_roll_static)/slice | solution.py:37
  50.0 2.4 %fusion.40 = (f32[4,16,30,256]{3,2,1,0:T(8,128)}, f32[4,16,30,256]{3,2,1,0:T(8,128)}) fusion(f32[4,16,32,256]{3,2,1,0:T(8,128)S(1)} %fusion.31), kind=kLoop, calls=%fused_computation.54 | loop fusion | bytes 7864320 | tf_op jit(solution)/shard_map/jit(_roll_static)/slice | solution.py:36
  52.4 1.7 %fusion.43 = (f32[4,16,32,1]{3,2,1,0:T(8,128)}, f32[4,16,32,1]{3,2,1,0:T(8,128)}) fusion(f32[4,16,32,256]{3,2,1,0:T(8,128)S(1)} %fusion.31), kind=kLoop, calls=%fused_computation.57 | loop fusion | bytes 32768 | tf_op jit(solution)/shard_map/jit(_roll_static)/slice | solution.py:37
  54.0 0.0 copy-start.3
  54.1 1.7 %fusion.39 = (f32[4,16,32,2]{3,2,1,0:T(8,128)}, f32[4,16,32,2]{3,2,1,0:T(8,128)}) fusion(f32[4,16,32,256]{3,2,1,0:T(8,128)S(1)} %fusion.31), kind=kLoop, calls=%fused_computation.53 | loop fusion | bytes 65536 | tf_op jit(solution)/shard_map/jit(_roll_static)/slice | solution.py:37
  55.8 8.2 %collective-permute-start.2 = (f32[4,2,32,256]{3,2,1,0:T(8,128)S(1)}, f32[4,2,32,256]{3,2,1,0:T(8,128)S(1)}, u32[]{:S(2)}, u32[]{:S(2)}) collective-permute-start(f32[4,2,32,256]{3,2,1,0:T(8,128)S(1)} %get-tuple-element.20), channel_id=1, source_target_pairs={{8,0},{16,8},{24,16},{32,24},{40,32},{48,40},{56,48},{64,56},{72,6... | collective-permute-start | bytes 786440 | tf_op jit(solution)/shard_map/ppermute | solution.py:22
  64.1 1.9 %collective-permute-start.3 = (f32[4,2,32,256]{3,2,1,0:T(8,128)S(1)}, f32[4,2,32,256]{3,2,1,0:T(8,128)S(1)}, u32[]{:S(2)}, u32[]{:S(2)}) collective-permute-start(f32[4,2,32,256]{3,2,1,0:T(8,128)S(1)} %get-tuple-element.21), channel_id=1, source_target_pairs={{0,8},{8,16},{16,24},{24,32},{32,40},{40,48},{48,56},{56,64},{64,7... | collective-permute-start | bytes 786440 | tf_op jit(solution)/shard_map/ppermute | solution.py:19
  66.0 0.1 fusion.45
  66.1 0.1 fusion.41
  66.2 7.6 %collective-permute-done.2 = f32[4,2,32,256]{3,2,1,0:T(8,128)S(1)} collective-permute-done((f32[4,2,32,256]{3,2,1,0:T(8,128)S(1)}, f32[4,2,32,256]{3,2,1,0:T(8,128)S(1)}, u32[]{:S(2)}, u32[]{:S(2)}) %collective-permute-start.2) | collective-permute-done | bytes 262176 | tf_op jit(solution)/shard_map/ppermute | solution.py:22
  73.8 0.0 copy-start.4
  73.8 12.3 %collective-permute-done.3 = f32[4,2,32,256]{3,2,1,0:T(8,128)S(1)} collective-permute-done((f32[4,2,32,256]{3,2,1,0:T(8,128)S(1)}, f32[4,2,32,256]{3,2,1,0:T(8,128)S(1)}, u32[]{:S(2)}, u32[]{:S(2)}) %collective-permute-start.3) | collective-permute-done | bytes 262176 | tf_op jit(solution)/shard_map/ppermute | solution.py:19
  86.1 0.0 copy-start.5
  86.1 0.0 copy-done.4
  86.1 0.7 copy-done.5
  86.8 0.0 copy-done.3
  86.8 8.1 %fusion.14 = f32[4,16,32,256]{3,2,1,0:T(8,128)S(1)} fusion(f32[4,16,32,256]{3,2,1,0:T(8,128)S(1)} %copy-done, f32[4,2,32,256]{3,2,1,0:T(8,128)} %copy-done.5, f32[4,16,32,256]{3,2,1,0:T(8,128)S(1)} %fusion.31, f32[4,2,32,256]{3,2,1,0:T(8,128)} %copy-done.4, f32[4,16,31,256]{3,2,1,0:T(8,128)} %get-tuple-element.17, ...), kind=kLoop, calls=%fused_computation.19 | loop fusion | flops 18350080 | bytes 24117256 | tf_op jit(solution)/shard_map/sub | solution.py:51
  95.0 0.0 copy-start.1
  95.0 1.3 copy-done.1
  96.3 2.6 %copy.35 = f32[4,16,32,256]{3,1,0,2:T(8,128)} copy(f32[4,16,32,256]{3,2,1,0:T(8,128)S(1)} %fusion.14) | data formatting | bytes 4194304 | tf_op jit(solution)/shard_map/sub | solution.py:51
  98.8 0.0 copy-start.6
  98.8 4.3 %all-to-all-start = ((f32[4,16,32,256]{3,1,0,2:T(8,128)}), f32[4,16,32,256]{3,1,0,2:T(8,128)S(1)}, u32[]{:S(2)}, u32[]{:S(2)}) async-start(f32[4,16,32,256]{3,1,0,2:T(8,128)} %copy.35), calls=%async_computation | async-start | bytes 4194304 | tf_op jit(solution)/shard_map/all_to_all | solution.py:54
  103.1 0.0 copy-done.6
  103.2 54.8 %all-gather = f32[8,4,16]{2,1,0:T(4,128)S(1)} all-gather(f32[1,4,16]{2,1,0:T(4,128)S(1)} %bitcast.15), channel_id=1, replica_groups=mesh['grid'=64,'orb'=8] {'orb'}, dimensions={0}, use_global_device_ids=true | all-gather | bytes 2304 | tf_op jit(solution)/shard_map/all_gather | solution.py:55
  158.0 0.0 all-to-all-done
  158.0 3.1 %copy.38 = f32[4,16,8,4,256]{4,3,1,0,2:T(4,128)} copy(f32[4,16,8,4,256]{4,1,0,3,2:T(8,128)S(1)} %bitcast.12) | data formatting | bytes 4194304 | tf_op jit(solution)/shard_map/all_to_all | solution.py:54
  161.1 2.3 %reshape.18 = f32[32,16384]{1,0:T(8,128)S(1)} reshape(f32[8,4,16,4,256]{4,3,2,1,0:T(4,128)} %bitcast.13) | data formatting | bytes 4194304 | tf_op jit(solution)/shard_map/reshape | solution.py:56
  163.5 1.2 convolution_bitcast_fusion
  164.7 1.7 %reshape.19 = f32[16,16,4,256]{3,2,1,0:T(4,128)} reshape(f32[16,16384]{1,0:T(8,128)S(1)} %convolution_bitcast_fusion) | data formatting | bytes 2097152 | tf_op jit(solution)/shard_map/reshape | solution.py:60
  (3 shorter events, 0.1 us)
Async XLA Ops:
  1.7 34.5 %collective-permute-start.1 = (f32[4,2,32,256]{3,2,1,0:T(8,128)S(1)}, f32[4,2,32,256]{3,2,1,0:T(8,128)S(1)}, u32[]{:S(2)}, u32[]{:S(2)}) collective-permute-start(f32[4,2,32,256]{3,2,1,0:T(8,128)S(1)} %get-tuple-element.39), channel_id=1, source_target_pairs={{0,8},{8,16},{16,24},{24,32},{32,40},{40,48},{48,56},{56,64},{64,7... | collective-permute-start | bytes 786440 | tf_op jit(solution)/shard_map/ppermute | solution.py:19
  6.5 19.3 %copy-start = (f32[4,16,32,256]{3,2,1,0:T(8,128)S(1)}, f32[4,16,32,256]{3,2,1,0:T(8,128)}, u32[]{:S(2)}) copy-start(f32[4,16,32,256]{3,2,1,0:T(8,128)} %param.5) | copy-start | bytes 6291460
  6.6 30.2 %collective-permute-start = (f32[4,2,32,256]{3,2,1,0:T(8,128)S(1)}, f32[4,2,32,256]{3,2,1,0:T(8,128)S(1)}, u32[]{:S(2)}, u32[]{:S(2)}) collective-permute-start(f32[4,2,32,256]{3,2,1,0:T(8,128)S(1)} %get-tuple-element.38), channel_id=1, source_target_pairs={{8,0},{16,8},{24,16},{32,24},{40,32},{48,40},{56,48},{64,56},{72,6... | collective-permute-start | bytes 786440 | tf_op jit(solution)/shard_map/ppermute | solution.py:22
  36.2 1.0 copy-start.2
  54.0 32.8 %copy-start.3 = (f32[16,32,256]{2,1,0:T(8,128)S(1)}, f32[16,32,256]{2,1,0:T(8,128)}, u32[]{:S(2)}) copy-start(f32[16,32,256]{2,1,0:T(8,128)} %param.6) | copy-start | bytes 1572868
  55.8 18.0 %collective-permute-start.2 = (f32[4,2,32,256]{3,2,1,0:T(8,128)S(1)}, f32[4,2,32,256]{3,2,1,0:T(8,128)S(1)}, u32[]{:S(2)}, u32[]{:S(2)}) collective-permute-start(f32[4,2,32,256]{3,2,1,0:T(8,128)S(1)} %get-tuple-element.20), channel_id=1, source_target_pairs={{8,0},{16,8},{24,16},{32,24},{40,32},{48,40},{56,48},{64,56},{72,6... | collective-permute-start | bytes 786440 | tf_op jit(solution)/shard_map/ppermute | solution.py:22
  64.1 22.1 %collective-permute-start.3 = (f32[4,2,32,256]{3,2,1,0:T(8,128)S(1)}, f32[4,2,32,256]{3,2,1,0:T(8,128)S(1)}, u32[]{:S(2)}, u32[]{:S(2)}) collective-permute-start(f32[4,2,32,256]{3,2,1,0:T(8,128)S(1)} %get-tuple-element.21), channel_id=1, source_target_pairs={{0,8},{8,16},{16,24},{24,32},{32,40},{40,48},{48,56},{56,64},{64,7... | collective-permute-start | bytes 786440 | tf_op jit(solution)/shard_map/ppermute | solution.py:19
  73.8 12.3 %copy-start.4 = (f32[4,2,32,256]{3,2,1,0:T(8,128)}, f32[4,2,32,256]{3,2,1,0:T(8,128)S(1)}, u32[]{:S(2)}) copy-start(f32[4,2,32,256]{3,2,1,0:T(8,128)S(1)} %collective-permute-done.2) | copy-start | bytes 786436
  86.1 0.7 copy-start.5
  95.0 1.3 copy-start.1
  98.8 4.3 %copy-start.6 = (f32[4,16]{1,0:T(4,128)S(1)}, f32[4,16]{1,0:T(4,128)}, u32[]{:S(2)}) copy-start(f32[4,16]{1,0:T(4,128)} %param.9) | copy-start | bytes 772
  98.8 59.2 %all-to-all-start = ((f32[4,16,32,256]{3,1,0,2:T(8,128)}), f32[4,16,32,256]{3,1,0,2:T(8,128)S(1)}, u32[]{:S(2)}, u32[]{:S(2)}) async-start(f32[4,16,32,256]{3,1,0,2:T(8,128)} %copy.35), calls=%async_computation | async-start | bytes 4194304 | tf_op jit(solution)/shard_map/all_to_all | solution.py:54
where the time goes:
time: 167 us; the launch traced here: 166 us
  blocking collectives  54.8 us (33%)
  local copies, waits for them, and re-layouts  38.1 us (23%)
  starting transfers between devices  35.5 us (21%)
  waiting for transfers between devices  19.9 us (12%)
  other arithmetic  14.7 us (9%)
  between operations  2.14 us (1%)
    all_gather x1, blocking collectives, body(): full_rows = lax.all_gather(rotation, 'orb', axis=0, tiled=True)  54.8 us
    ppermute x2, starting transfers between devices, padded(): lax.ppermute(lax.slice_in_dim(block, 0, width, axis=dim), axis, backward)  24.4 us
    slice x8, local copies, waits for them, and re-layouts, apply_hamilton(): jnp.roll(interior, -offset, 3)  16 us
    ppermute x2, waiting for transfers between devices, padded(): lax.ppermute(lax.slice_in_dim(block, block.shape[dim] - width, None, axis...  12.3 us
    slice x8, local copies, waits for them, and re-layouts, apply_hamilton(): jnp.roll(interior, -offset, 2)  8.16 us
    sub x1, other arithmetic, body(): 2.0 * (apply_hamilton(extend_planes(first), potential, R) - middle * first)  8.11 us
    ppermute x2, waiting for transfers between devices, padded(): lax.ppermute(lax.slice_in_dim(block, 0, width, axis=dim), axis, backward)  7.6 us
    ppermute x2, starting transfers between devices, padded(): lax.ppermute(lax.slice_in_dim(block, block.shape[dim] - width, None, axis...  6.75 us
  transfers between devices with their start and end apart: 5, of which 2 were waited for; matrix products, arithmetic and copies ran while one was open for 8% of the time, Pallas kernels for 0%

commit v1 on v0

v1 whole, which is shorter than its diff:
```python
import jax
import jax.numpy as jnp
from jax import lax
from jax.experimental import pallas as pl
from jax.experimental.pallas import tpu as pltpu
from jax.sharding import PartitionSpec as P

W0, W1, W2 = -5.0 / 2.0, 4.0 / 3.0, -1.0 / 12.0
F32 = jnp.float32
ORBS, PLANES, ROWS, COLS = 4, 16, 32, 256
REACH = 4
PEERS, NCOL = 8, 16
LIMIT = 48 * 1024 * 1024


def coefficients(lower_ref, upper_ref):
    middle = (upper_ref[0] + lower_ref[0]) * 0.5
    inverse = 1.0 / ((upper_ref[0] - lower_ref[0]) * 0.5)
    return (-1.5 * W0 - middle) * inverse, inverse, -0.5 * W1 * inverse


def scaled_hamilton(planes, local, coef):
    base, inverse, near = coef
    below2, below1, f, above1, above2 = planes
    s1 = below1 + above1
    s2 = below2 + above2
    s1 = s1 + (pltpu.roll(f, 1, 0) + pltpu.roll(f, ROWS - 1, 0))
    s2 = s2 + (pltpu.roll(f, 2, 0) + pltpu.roll(f, ROWS - 2, 0))
    s1 = s1 + (pltpu.roll(f, 1, 1) + pltpu.roll(f, COLS - 1, 1))
    s2 = s2 + (pltpu.roll(f, 2, 1) + pltpu.roll(f, COLS - 2, 1))
    return f * (base + inverse * local) + near * (s1 + (W2 / W1) * s2)


def first_planes(count, source, local, store, coef):
    def step(p, carry):
        store(p, scaled_hamilton([source(p + d) for d in range(5)], local(p), coef))
        return carry

    lax.fori_loop(0, count, step, 0, unroll=2)


def filtered_plane(q, first, original, local, coef):
    g = scaled_hamilton([first(q + d) for d in range(5)], local, coef)
    return 2.0 * g - original


def pack_pair(mine, slots_ref, row, g0, g1):
    low = lax.broadcasted_iota(jnp.int32, (8, 128), 0) < 4
    for k in range(ROWS // 8):
        for h in range(COLS // 128):
            a = g0[8 * k : 8 * k + 8, 128 * h : 128 * h + 128]
            b = g1[8 * k : 8 * k + 8, 128 * h : 128 * h + 128]
            at = slice(row + 8 * h, row + 8 * h + 8)
            slots_ref[jnp.bitwise_xor(mine, 2 * k), at, :] = jnp.where(low, a, pltpu.roll(b, 4, 0))
            slots_ref[jnp.bitwise_xor(mine, 2 * k + 1), at, :] = jnp.where(
                low, pltpu.roll(a, 4, 0), b
            )


def inner_kernel(
    lower_ref, upper_ref, orb_ref, pot_ref, rot_ref, out_ref, first_ref, send_ref, slots_ref
):
    coef = coefficients(lower_ref, upper_ref)
    orbital = pl.program_id(0)

    def store(p, value):
        first_ref[0, p] = value

    first_planes(12, lambda p: orb_ref[0, p], lambda p: pot_ref[p + 2], store, coef)
    for t in range(4):
        pair = []
        for q in (2 * t, 2 * t + 1):
            g = filtered_plane(
                q, lambda p: first_ref[0, p], orb_ref[0, q + 4], pot_ref[q + 4], coef
            )
            out_ref[0, q + 4] = g
            pair.append(g)
        pack_pair(0, slots_ref, t * 16, *pair)
    for slot in range(PEERS):
        send_ref[slot, pl.ds(pl.multiple_of(orbital * 64, 64), 64), :] = slots_ref[slot]
        send_ref[slot, 256:264, :] = rot_ref[...]


def outer_kernel(
    mine_ref, lower_ref, upper_ref, orb_ref, pot_ref, stored_ref, low_ref, low_pot_ref,
    high_ref, high_pot_ref, _, *rest,
):
    out_ref, sends, (ext_ref, local_ref, first_ref, slots_ref) = rest[0], rest[1:-4], rest[-4:]
    coef = coefficients(lower_ref, upper_ref)
    mine, side = mine_ref[0], pl.program_id(1)

    @pl.when(side == 0)
    def _():
        ext_ref[0:4] = low_ref[...]
        ext_ref[4:8] = orb_ref[0]
        local_ref[0:2] = low_pot_ref[...]
        local_ref[2:4] = pot_ref[0:2]
        first_ref[4:8] = stored_ref[0]

    @pl.when(side == 1)
    def _():
        ext_ref[0:4] = orb_ref[0]
        ext_ref[4:8] = high_ref[...]
        local_ref[0:2] = pot_ref[14:16]
        local_ref[2:4] = high_pot_ref[...]
        first_ref[0:4] = stored_ref[0]

    def store(p, value):
        first_ref[4 * side + p] = value

    first_planes(4, lambda p: ext_ref[p], lambda p: local_ref[p], store, coef)
    for t in range(2):
        pair = []
        for q in (2 * t, 2 * t + 1):
            g = filtered_plane(
                q, lambda p: first_ref[p], ext_ref[q + 4 - 4 * side], pot_ref[q + 12 * side], coef
            )
            out_ref[0, q] = g
            pair.append(g)
        pack_pair(mine, slots_ref, t * 16, *pair)
    for slot, send_ref in enumerate(sends):
        send_ref[...] = slots_ref[slot]


def rotate_tiles(u, tile, weight, out_ref):
    width = 8
    for first in range(0, NCOL, width):
        sums = [jnp.zeros((8, 128), F32)] * (4 * width)
        for slot in range(PEERS):
            for i in range(ORBS):
                rows = [pl.multiple_of(i * 64 + u * 32 + 8 * n, 8) for n in range(4)]
                values = [tile(slot, pl.ds(row, 8)) for row in rows]
                for j in range(width):
                    factor = weight(slot, i * NCOL + first + j)
                    for n in range(4):
                        sums[4 * j + n] = sums[4 * j + n] + factor * values[n]
        for j in range(width):
            for n in range(4):
                t, h = divmod(n, 2)
                columns = slice(128 * h, 128 * h + 128)
                out_ref[first + j, 2 * t, :, columns] = sums[4 * j + n][0:4]
                out_ref[first + j, 2 * t + 1, :, columns] = sums[4 * j + n][4:8]


def rotate_inner_kernel(rot_ref, recv_ref, out_ref):
    rotate_tiles(
        pl.program_id(0),
        lambda slot, rows: recv_ref[slot, rows, :],
        lambda slot, n: rot_ref[slot, n],
        out_ref,
    )


def rotate_outer_kernel(mine_ref, rot_ref, *rest):
    received, out_ref, mine = rest[:PEERS], rest[-1], mine_ref[0]
    rotate_tiles(
        pl.program_id(0),
        lambda slot, rows: received[slot][rows, :],
        lambda slot, n: rot_ref[jnp.bitwise_xor(mine, slot), n],
        out_ref,
    )


SMEM = pl.BlockSpec(memory_space=pltpu.SMEM)
ANY = pl.BlockSpec(memory_space=pl.ANY)


def params():
    return pltpu.CompilerParams(vmem_limit_bytes=LIMIT)


def cost(flops, moved):
    return pl.CostEstimate(flops=flops, bytes_accessed=moved, transcendentals=0)


def body(orbitals, potential, lower_cut, upper_bound, rotation):
    count = lax.axis_size("grid")
    forward = [(i, (i + 1) % count) for i in range(count)]
    backward = [(target, source) for source, target in forward]
    plane = (ROWS, COLS)

    def packed(first_plane, first_local):
        own = orbitals[:, first_plane : first_plane + REACH].reshape((ORBS * REACH,) + plane)
        return jnp.concatenate([own, potential[first_local : first_local + 2]], axis=0)

    low = lax.ppermute(packed(PLANES - REACH, PLANES - 2), "grid", forward)
    high = lax.ppermute(packed(0, 0), "grid", backward)

    orb_hbm = pltpu.with_memory_space_constraint(orbitals, pltpu.HBM)
    pot_hbm = pltpu.with_memory_space_constraint(potential, pltpu.HBM)
    rot_tile = jnp.pad(rotation.reshape(1, ORBS * NCOL), ((0, 7), (0, 128 - ORBS * NCOL)))
    mine = lax.axis_index("orb").astype(jnp.int32).reshape(1)
    filtered_shape = pltpu.HBM((ORBS, PLANES) + plane, F32)

    def regroup(sends):
        got = [sends[0]] + [None] * (PEERS - 1)
        for k in (4, 5, 6, 7, 2, 3, 1):
            got[k] = lax.ppermute(sends[k], "orb", [(o, o ^ k) for o in range(PEERS)])
        return got

    filtered, stored, send = pl.pallas_call(
        inner_kernel,
        grid=(ORBS,),
        in_specs=[
            SMEM,
            SMEM,
            pl.BlockSpec((1, PLANES) + plane, lambda i: (i, 0, 0, 0)),
            pl.BlockSpec((PLANES,) + plane, lambda i: (0, 0, 0)),
            pl.BlockSpec((8, 128), lambda i: (0, 0)),
        ],
        out_specs=[
            pl.BlockSpec((1, PLANES) + plane, lambda i: (i, 0, 0, 0)),
            pl.BlockSpec((1, 12) + plane, lambda i: (i, 0, 0, 0)),
            pl.BlockSpec((PEERS, 264, 128), lambda i: (0, 0, 0)),
        ],
        out_shape=[
            filtered_shape,
            pltpu.HBM((ORBS, 12) + plane, F32),
            pltpu.HBM((PEERS, 264, 128), F32),
        ],
        scratch_shapes=[pltpu.VMEM((PEERS, 64, 128), F32)],
        compiler_params=params(),
        cost_estimate=cost(1_000_000, 1_000_000),
        name="filter_inner",
    )(lower_cut, upper_bound, orb_hbm, pot_hbm, rot_tile)
    received = lax.all_to_all(send, "orb", split_axis=0, concat_axis=0, tiled=True)
    stored = pltpu.with_memory_space_constraint(stored, pltpu.HBM)

    filtered, *sends_outer = pl.pallas_call(
        outer_kernel,
        grid=(ORBS, 2),
        in_specs=[
            SMEM,
            SMEM,
            SMEM,
            pl.BlockSpec((1, 4) + plane, lambda i, s: (i, 3 * s, 0, 0)),
            pl.BlockSpec((PLANES,) + plane, lambda i, s: (0, 0, 0)),
            pl.BlockSpec((1, 4) + plane, lambda i, s: (i, 2 * s, 0, 0)),
            pl.BlockSpec((4,) + plane, lambda i, s: (i, 0, 0)),
            pl.BlockSpec((2,) + plane, lambda i, s: (8, 0, 0)),
            pl.BlockSpec((4,) + plane, lambda i, s: (i, 0, 0)),
            pl.BlockSpec((2,) + plane, lambda i, s: (8, 0, 0)),
            ANY,
        ],
        out_specs=[pl.BlockSpec((1, 4) + plane, lambda i, s: (i, 3 * s, 0, 0))]
        + [pl.BlockSpec((32, 128), lambda i, s: (2 * i + s, 0))] * PEERS,
        out_shape=[filtered_shape] + [jax.ShapeDtypeStruct((256, 128), F32)] * PEERS,
        scratch_shapes=[
            pltpu.VMEM((8,) + plane, F32),
            pltpu.VMEM((4,) + plane, F32),
            pltpu.VMEM((8,) + plane, F32),
            pltpu.VMEM((PEERS, 32, 128), F32),
        ],
        input_output_aliases={10: 0},
        compiler_params=params(),
        cost_estimate=cost(400_000_000_000, 400_000_000),
        name="filter_outer",
    )(mine, lower_cut, upper_bound, orb_hbm, pot_hbm, stored, low, low, high, high, filtered)
    received_outer = regroup(sends_outer)

    weights = received[:, 256, : ORBS * NCOL]
    rotated_shape = jax.ShapeDtypeStruct((NCOL, PLANES, 4, COLS), F32)
    vmem = pl.BlockSpec(memory_space=pltpu.VMEM)
    rotated = pl.pallas_call(
        rotate_inner_kernel,
        grid=(2,),
        in_specs=[SMEM, vmem],
        out_specs=pl.BlockSpec((NCOL, 4, 4, COLS), lambda u: (0, 1 + u, 0, 0)),
        out_shape=rotated_shape,
        compiler_params=params(),
        cost_estimate=cost(8_000_000, 1_600_000),
        name="rotate_inner",
    )(weights, received)
    rotated = pl.pallas_call(
        rotate_outer_kernel,
        grid=(2,),
        in_specs=[SMEM, SMEM] + [vmem] * PEERS + [ANY],
        out_specs=pl.BlockSpec((NCOL, 4, 4, COLS), lambda u: (0, 3 * u, 0, 0)),
        out_shape=rotated_shape,
        input_output_aliases={PEERS + 2: 0},
        compiler_params=params(),
        cost_estimate=cost(8_000_000, 1_600_000),
        name="rotate_outer",
    )(mine, weights, *received_outer, rotated)
    return (filtered, rotated)


def solution(mesh):
    in_specs = (P("orb", "grid", None, None), P("grid", None, None), P(), P(), P("orb", None))
    out_specs = (P("orb", "grid", None, None), P(None, "grid", "orb", None))
    return jax.shard_map(body, mesh=mesh, in_specs=in_specs, out_specs=out_specs, check_vma=False)
```

time: 167 us -> 98.7 us (0.59)
  the two profiles are of different devices: /device:TPU:1 before, /device:TPU:17 now
where the time goes in v1:
time: 98.7 us; the launch traced here: 97.9 us
  starting transfers between devices  47.3 us (48%)
  waiting for transfers between devices  24 us (24%)
  Pallas kernels  21.4 us (22%)
  local copies, waits for them, and re-layouts  3.05 us (3%)
  between operations  2.07 us (2%)
    ppermute x7, starting transfers between devices, regroup(): got[k] = lax.ppermute(sends[k], 'orb', [(o, o ^ k) for o in range(PEERS)])  22.2 us
    ppermute x7, waiting for transfers between devices, regroup(): got[k] = lax.ppermute(sends[k], 'orb', [(o, o ^ k) for o in range(PEERS)])  15.7 us
    ppermute x1, starting transfers between devices, body(): high = lax.ppermute(packed(0, 0), 'grid', backward)  14.2 us
    ppermute x1, waiting for transfers between devices, body(): low = lax.ppermute(packed(PLANES - REACH, PLANES - 2), 'grid', forward)  8.24 us
    pallas_call x1, Pallas kernels, body(): pl.pallas_call(outer_kernel, grid=(ORBS, 2), in_specs=[SMEM, SMEM, SMEM,...  7.98 us
    pallas_call x1, Pallas kernels, body(): pl.pallas_call(inner_kernel, grid=(ORBS,), in_specs=[SMEM, SMEM, pl.Block...  7.5 us
    all_to_all x1, starting transfers between devices, body(): lax.all_to_all(send, 'orb', split_axis=0, concat_axis=0, tiled=True)  6.88 us
    ppermute x1, starting transfers between devices, body(): low = lax.ppermute(packed(PLANES - REACH, PLANES - 2), 'grid', forward)  4 us
  transfers between devices with their start and end apart: 10, of which 5 were waited for; matrix products, arithmetic and copies ran while one was open for 1% of the time, Pallas kernels for 19%

profile of v1, /device:TPU:17, one launch (start us, length us, event | category | flops | bytes accessed | tf_op | source)
XLA Modules:
  0.0 97.9 jit_solution(9750034466827811163)
XLA Ops:
  0.6 0.9 fusion.1
  1.5 0.0 copy-start
  1.5 1.3 %fusion = (f32[4,4,32,256]{3,2,1,0:T(8,128)S(1)}, f32[4,4,32,256]{3,2,1,0:T(8,128)S(1)}) fusion(f32[4,16,32,256]{3,2,1,0:T(8,128)} %orb_ref.3), kind=kLoop, calls=%fused_computation.2 | loop fusion | bytes 2097152 | tf_op jit(solution)/shard_map/slice | solution.py:183
  2.9 4.0 %collective-permute-start = (f32[18,32,256]{2,1,0:T(8,128)S(1)}, f32[18,32,256]{2,1,0:T(8,128)S(1)}, u32[]{:S(2)}, u32[]{:S(2)}) collective-permute-start(f32[18,32,256]{2,1,0:T(8,128)S(1)} %pad_maximum_fusion), channel_id=1, source_target_pairs={{0,8},{8,16},{16,24},{24,32},{32,40},{40,48},{48,56},{56,64},{64,7... | collective-permute-start | bytes 1769480 | tf_op jit(solution)/shard_map/ppermute | solution.py:186
  7.0 14.2 %collective-permute-start.1 = (f32[18,32,256]{2,1,0:T(8,128)S(1)}, f32[18,32,256]{2,1,0:T(8,128)S(1)}, u32[]{:S(2)}, u32[]{:S(2)}) collective-permute-start(f32[18,32,256]{2,1,0:T(8,128)S(1)} %pad_maximum_fusion.1), channel_id=1, source_target_pairs={{8,0},{16,8},{24,16},{32,24},{40,32},{48,40},{56,48},{64,56},{72,6... | collective-permute-start | bytes 1769480 | tf_op jit(solution)/shard_map/ppermute | solution.py:187
  22.5 0.0 copy-done
  22.5 0.1 reshape.17
  22.6 7.5 %filter_inner.1 = (f32[4,16,32,256]{3,2,1,0:T(8,128)}, f32[4,12,32,256]{3,2,1,0:T(8,128)}, f32[8,264,128]{2,1,0:T(8,128)}) custom-call(f32[1]{0:T(128)S(6)} %copy.15.lower_ref, f32[1]{0:T(128)S(6)} %copy.16.upper_ref, f32[4,16,32,256]{3,2,1,0:T(8,128)} %orb_ref.3, f32[16,32,256]{2,1,0:T(8,128)} %pot_ref.3, f32[8,128]{1,0:T(8,128)S(1)} %pad.4.rot_ref), custom_call_target="tpu_custom_call" | custom-call | flops 1000000 | bytes 1000000 | tf_op jit(solution)/shard_map/filter_inner/pallas_call | solution.py:201
  30.1 6.9 %all-to-all-start = ((f32[8,264,128]{2,1,0:T(8,128)}), f32[8,264,128]{2,1,0:T(8,128)}, u32[]{:S(2)}, u32[]{:S(2)}) async-start(f32[8,264,128]{2,1,0:T(8,128)} %get-tuple-element.17), calls=%async_computation | async-start | bytes 2162688 | tf_op jit(solution)/shard_map/all_to_all | solution.py:226
  37.0 8.2 %collective-permute-done.low_ref.low_pot_ref = f32[18,32,256]{2,1,0:T(8,128)S(1)} collective-permute-done((f32[18,32,256]{2,1,0:T(8,128)S(1)}, f32[18,32,256]{2,1,0:T(8,128)S(1)}, u32[]{:S(2)}, u32[]{:S(2)}) %collective-permute-start) | collective-permute-done | bytes 589856 | tf_op jit(solution)/shard_map/ppermute | solution.py:186
  45.2 0.0 collective-permute-done.1.high_ref.high_pot_ref
  45.2 8.0 %filter_outer.1 = (f32[4,16,32,256]{3,2,1,0:T(8,128)}, f32[256,128]{1,0:T(8,128)S(1)}, f32[256,128]{1,0:T(8,128)S(1)}, f32[256,128]{1,0:T(8,128)S(1)}, f32[256,1...) custom-call(s32[1]{0:T(128)} %bitcast.mine_ref, ...), custom_call_target="tpu_custom_call", output_to_operand_aliasing={{0}: (10, {})} | custom-call | flops 399999991808 | bytes 400000000 | tf_op jit(solution)/shard_map/filter_outer/pallas_call | solution.py:229
  53.2 4.6 %collective-permute-start.2 = (f32[256,128]{1,0:T(8,128)S(1)}, f32[256,128]{1,0:T(8,128)S(1)}, u32[]{:S(2)}, u32[]{:S(2)}) collective-permute-start(f32[256,128]{1,0:T(8,128)S(1)} %get-tuple-element.19), channel_id=1, source_target_pairs={{0,1},{1,0},{2,3},{3,2},{4,5},{5,4},{6,7},{7,6},{8,9},{9,8},{10,11... | collective-permute-start | bytes 393224 | tf_op jit(solution)/shard_map/ppermute | solution.py:198
  57.8 1.9 %collective-permute-start.3 = (f32[256,128]{1,0:T(8,128)S(1)}, f32[256,128]{1,0:T(8,128)S(1)}, u32[]{:S(2)}, u32[]{:S(2)}) collective-permute-start(f32[256,128]{1,0:T(8,128)S(1)} %get-tuple-element.20), channel_id=1, source_target_pairs={{0,2},{1,3},{2,0},{3,1},{4,6},{5,7},{6,4},{7,5},{8,10},{9,11},{10,... | collective-permute-start | bytes 393224 | tf_op jit(solution)/shard_map/ppermute | solution.py:198
  59.8 3.5 %collective-permute-start.4 = (f32[256,128]{1,0:T(8,128)S(1)}, f32[256,128]{1,0:T(8,128)S(1)}, u32[]{:S(2)}, u32[]{:S(2)}) collective-permute-start(f32[256,128]{1,0:T(8,128)S(1)} %get-tuple-element.21), channel_id=1, source_target_pairs={{0,3},{1,2},{2,1},{3,0},{4,7},{5,6},{6,5},{7,4},{8,11},{9,10},{10,... | collective-permute-start | bytes 393224 | tf_op jit(solution)/shard_map/ppermute | solution.py:198
  63.3 4.3 %collective-permute-start.5 = (f32[256,128]{1,0:T(8,128)S(1)}, f32[256,128]{1,0:T(8,128)S(1)}, u32[]{:S(2)}, u32[]{:S(2)}) collective-permute-start(f32[256,128]{1,0:T(8,128)S(1)} %get-tuple-element.22), channel_id=1, source_target_pairs={{0,4},{1,5},{2,6},{3,7},{4,0},{5,1},{6,2},{7,3},{8,12},{9,13},{10,... | collective-permute-start | bytes 393224 | tf_op jit(solution)/shard_map/ppermute | solution.py:198
  67.6 2.3 %collective-permute-start.6 = (f32[256,128]{1,0:T(8,128)S(1)}, f32[256,128]{1,0:T(8,128)S(1)}, u32[]{:S(2)}, u32[]{:S(2)}) collective-permute-start(f32[256,128]{1,0:T(8,128)S(1)} %get-tuple-element.23), channel_id=1, source_target_pairs={{0,5},{1,4},{2,7},{3,6},{4,1},{5,0},{6,3},{7,2},{8,13},{9,12},{10,... | collective-permute-start | bytes 393224 | tf_op jit(solution)/shard_map/ppermute | solution.py:198
  69.9 0.0 collective-permute-done.2.rest_1_
  69.9 3.2 %collective-permute-start.7 = (f32[256,128]{1,0:T(8,128)S(1)}, f32[256,128]{1,0:T(8,128)S(1)}, u32[]{:S(2)}, u32[]{:S(2)}) collective-permute-start(f32[256,128]{1,0:T(8,128)S(1)} %get-tuple-element.24), channel_id=1, source_target_pairs={{0,6},{1,7},{2,4},{3,5},{4,2},{5,3},{6,0},{7,1},{8,14},{9,15},{10,... | collective-permute-start | bytes 393224 | tf_op jit(solution)/shard_map/ppermute | solution.py:198
  73.1 0.0 collective-permute-done.3.rest_2_
  73.1 2.4 %collective-permute-start.8 = (f32[256,128]{1,0:T(8,128)S(1)}, f32[256,128]{1,0:T(8,128)S(1)}, u32[]{:S(2)}, u32[]{:S(2)}) collective-permute-start(f32[256,128]{1,0:T(8,128)S(1)} %get-tuple-element.25), channel_id=1, source_target_pairs={{0,7},{1,6},{2,5},{3,4},{4,3},{5,2},{6,1},{7,0},{8,15},{9,14},{10,... | collective-permute-start | bytes 393224 | tf_op jit(solution)/shard_map/ppermute | solution.py:198
  75.5 0.0 all-to-all-done.recv_ref
  75.5 0.8 slice.20
  76.3 3.3 %rotate_inner.1.rest_8_ = f32[16,16,4,256]{3,2,1,0:T(4,128)} custom-call(f32[8,64]{1,0:T(8,128)S(1)} %bitcast.6, f32[8,264,128]{2,1,0:T(8,128)} %all-to-all-done.recv_ref), custom_call_target="tpu_custom_call" | custom-call | flops 8000000 | bytes 1600000 | tf_op jit(solution)/shard_map/rotate_inner/pallas_call | solution.py:264
  79.5 0.0 collective-permute-done.4.rest_3_
  79.5 3.4 %collective-permute-done.5.rest_4_ = f32[256,128]{1,0:T(8,128)S(1)} collective-permute-done((f32[256,128]{1,0:T(8,128)S(1)}, f32[256,128]{1,0:T(8,128)S(1)}, u32[]{:S(2)}, u32[]{:S(2)}) %collective-permute-start.5) | collective-permute-done | bytes 131104 | tf_op jit(solution)/shard_map/ppermute | solution.py:198
  82.9 2.8 %collective-permute-done.6.rest_5_ = f32[256,128]{1,0:T(8,128)S(1)} collective-permute-done((f32[256,128]{1,0:T(8,128)S(1)}, f32[256,128]{1,0:T(8,128)S(1)}, u32[]{:S(2)}, u32[]{:S(2)}) %collective-permute-start.6) | collective-permute-done | bytes 131104 | tf_op jit(solution)/shard_map/ppermute | solution.py:198
  85.7 6.7 %collective-permute-done.7.rest_6_ = f32[256,128]{1,0:T(8,128)S(1)} collective-permute-done((f32[256,128]{1,0:T(8,128)S(1)}, f32[256,128]{1,0:T(8,128)S(1)}, u32[]{:S(2)}, u32[]{:S(2)}) %collective-permute-start.7) | collective-permute-done | bytes 131104 | tf_op jit(solution)/shard_map/ppermute | solution.py:198
  92.4 2.8 %collective-permute-done.8.rest_7_ = f32[256,128]{1,0:T(8,128)S(1)} collective-permute-done((f32[256,128]{1,0:T(8,128)S(1)}, f32[256,128]{1,0:T(8,128)S(1)}, u32[]{:S(2)}, u32[]{:S(2)}) %collective-permute-start.8) | collective-permute-done | bytes 131104 | tf_op jit(solution)/shard_map/ppermute | solution.py:198
  95.2 2.6 %rotate_outer.1 = f32[16,16,4,256]{3,2,1,0:T(4,128)} custom-call(s32[1]{0:T(128)} %bitcast.mine_ref, f32[8,64]{1,0:T(8,128)S(1)} %bitcast.7, f32[256,128]{1,0:T(8,128)S(1)} %get-tuple-element.18.rest_0_, f32[256,128]{1,0:T(8,128)S(1)} %collective-permute-done.2.rest_1_, ...), custom_call_target="tpu_custom_call", output_to_operand_aliasing={{}: (10, {})} | custom-call | flops 8000000 | bytes 1600000 | tf_op jit(solution)/shard_map/rotate_outer/pallas_call | solution.py:274
  (3 shorter events, 0.1 us)
Async XLA Ops:
  1.5 21.0 %copy-start = (f32[4,16]{1,0:T(4,128)S(1)}, f32[4,16]{1,0:T(4,128)}, u32[]{:S(2)}) copy-start(f32[4,16]{1,0:T(4,128)} %param.9) | copy-start | bytes 772
  2.9 42.3 %collective-permute-start = (f32[18,32,256]{2,1,0:T(8,128)S(1)}, f32[18,32,256]{2,1,0:T(8,128)S(1)}, u32[]{:S(2)}, u32[]{:S(2)}) collective-permute-start(f32[18,32,256]{2,1,0:T(8,128)S(1)} %pad_maximum_fusion), channel_id=1, source_target_pairs={{0,8},{8,16},{16,24},{24,32},{32,40},{40,48},{48,56},{56,64},{64,7... | collective-permute-start | bytes 1769480 | tf_op jit(solution)/shard_map/ppermute | solution.py:186
  7.0 38.3 %collective-permute-start.1 = (f32[18,32,256]{2,1,0:T(8,128)S(1)}, f32[18,32,256]{2,1,0:T(8,128)S(1)}, u32[]{:S(2)}, u32[]{:S(2)}) collective-permute-start(f32[18,32,256]{2,1,0:T(8,128)S(1)} %pad_maximum_fusion.1), channel_id=1, source_target_pairs={{8,0},{16,8},{24,16},{32,24},{40,32},{48,40},{56,48},{64,56},{72,6... | collective-permute-start | bytes 1769480 | tf_op jit(solution)/shard_map/ppermute | solution.py:187
  30.1 45.4 %all-to-all-start = ((f32[8,264,128]{2,1,0:T(8,128)}), f32[8,264,128]{2,1,0:T(8,128)}, u32[]{:S(2)}, u32[]{:S(2)}) async-start(f32[8,264,128]{2,1,0:T(8,128)} %get-tuple-element.17), calls=%async_computation | async-start | bytes 2162688 | tf_op jit(solution)/shard_map/all_to_all | solution.py:226
  53.2 16.7 %collective-permute-start.2 = (f32[256,128]{1,0:T(8,128)S(1)}, f32[256,128]{1,0:T(8,128)S(1)}, u32[]{:S(2)}, u32[]{:S(2)}) collective-permute-start(f32[256,128]{1,0:T(8,128)S(1)} %get-tuple-element.19), channel_id=1, source_target_pairs={{0,1},{1,0},{2,3},{3,2},{4,5},{5,4},{6,7},{7,6},{8,9},{9,8},{10,11... | collective-permute-start | bytes 393224 | tf_op jit(solution)/shard_map/ppermute | solution.py:198
  57.8 15.3 %collective-permute-start.3 = (f32[256,128]{1,0:T(8,128)S(1)}, f32[256,128]{1,0:T(8,128)S(1)}, u32[]{:S(2)}, u32[]{:S(2)}) collective-permute-start(f32[256,128]{1,0:T(8,128)S(1)} %get-tuple-element.20), channel_id=1, source_target_pairs={{0,2},{1,3},{2,0},{3,1},{4,6},{5,7},{6,4},{7,5},{8,10},{9,11},{10,... | collective-permute-start | bytes 393224 | tf_op jit(solution)/shard_map/ppermute | solution.py:198
  59.8 19.8 %collective-permute-start.4 = (f32[256,128]{1,0:T(8,128)S(1)}, f32[256,128]{1,0:T(8,128)S(1)}, u32[]{:S(2)}, u32[]{:S(2)}) collective-permute-start(f32[256,128]{1,0:T(8,128)S(1)} %get-tuple-element.21), channel_id=1, source_target_pairs={{0,3},{1,2},{2,1},{3,0},{4,7},{5,6},{6,5},{7,4},{8,11},{9,10},{10,... | collective-permute-start | bytes 393224 | tf_op jit(solution)/shard_map/ppermute | solution.py:198
  63.3 19.6 %collective-permute-start.5 = (f32[256,128]{1,0:T(8,128)S(1)}, f32[256,128]{1,0:T(8,128)S(1)}, u32[]{:S(2)}, u32[]{:S(2)}) collective-permute-start(f32[256,128]{1,0:T(8,128)S(1)} %get-tuple-element.22), channel_id=1, source_target_pairs={{0,4},{1,5},{2,6},{3,7},{4,0},{5,1},{6,2},{7,3},{8,12},{9,13},{10,... | collective-permute-start | bytes 393224 | tf_op jit(solution)/shard_map/ppermute | solution.py:198
  67.6 18.1 %collective-permute-start.6 = (f32[256,128]{1,0:T(8,128)S(1)}, f32[256,128]{1,0:T(8,128)S(1)}, u32[]{:S(2)}, u32[]{:S(2)}) collective-permute-start(f32[256,128]{1,0:T(8,128)S(1)} %get-tuple-element.23), channel_id=1, source_target_pairs={{0,5},{1,4},{2,7},{3,6},{4,1},{5,0},{6,3},{7,2},{8,13},{9,12},{10,... | collective-permute-start | bytes 393224 | tf_op jit(solution)/shard_map/ppermute | solution.py:198
  69.9 22.5 %collective-permute-start.7 = (f32[256,128]{1,0:T(8,128)S(1)}, f32[256,128]{1,0:T(8,128)S(1)}, u32[]{:S(2)}, u32[]{:S(2)}) collective-permute-start(f32[256,128]{1,0:T(8,128)S(1)} %get-tuple-element.24), channel_id=1, source_target_pairs={{0,6},{1,7},{2,4},{3,5},{4,2},{5,3},{6,0},{7,1},{8,14},{9,15},{10,... | collective-permute-start | bytes 393224 | tf_op jit(solution)/shard_map/ppermute | solution.py:198
  73.1 22.1 %collective-permute-start.8 = (f32[256,128]{1,0:T(8,128)S(1)}, f32[256,128]{1,0:T(8,128)S(1)}, u32[]{:S(2)}, u32[]{:S(2)}) collective-permute-start(f32[256,128]{1,0:T(8,128)S(1)} %get-tuple-element.25), channel_id=1, source_target_pairs={{0,7},{1,6},{2,5},{3,4},{4,3},{5,2},{6,1},{7,0},{8,15},{9,14},{10,... | collective-permute-start | bytes 393224 | tf_op jit(solution)/shard_map/ppermute | solution.py:198

commit v2 on v1

--- a/solution.py
+++ b/solution.py
@@ -11,6 +11,7 @@
 REACH = 4
 PEERS, NCOL = 8, 16
 LIMIT = 48 * 1024 * 1024
+ORDER = (4, 5, 6, 7, 2, 3, 1, 0)
 
 
 def coefficients(lower_ref, upper_ref):
@@ -156,7 +157,7 @@
     rotate_tiles(
         pl.program_id(0),
         lambda slot, rows: received[slot][rows, :],
-        lambda slot, n: rot_ref[jnp.bitwise_xor(mine, slot), n],
+        lambda slot, n: rot_ref[jnp.bitwise_xor(mine, ORDER[slot]), n],
         out_ref,
     )
 
@@ -186,17 +187,15 @@
     low = lax.ppermute(packed(PLANES - REACH, PLANES - 2), "grid", forward)
     high = lax.ppermute(packed(0, 0), "grid", backward)
 
-    orb_hbm = pltpu.with_memory_space_constraint(orbitals, pltpu.HBM)
-    pot_hbm = pltpu.with_memory_space_constraint(potential, pltpu.HBM)
     rot_tile = jnp.pad(rotation.reshape(1, ORBS * NCOL), ((0, 7), (0, 128 - ORBS * NCOL)))
     mine = lax.axis_index("orb").astype(jnp.int32).reshape(1)
     filtered_shape = pltpu.HBM((ORBS, PLANES) + plane, F32)
 
     def regroup(sends):
-        got = [sends[0]] + [None] * (PEERS - 1)
-        for k in (4, 5, 6, 7, 2, 3, 1):
-            got[k] = lax.ppermute(sends[k], "orb", [(o, o ^ k) for o in range(PEERS)])
-        return got
+        return [
+            lax.ppermute(sends[k], "orb", [(o, o ^ k) for o in range(PEERS)]) if k else sends[k]
+            for k in ORDER
+        ]
 
     filtered, stored, send = pl.pallas_call(
         inner_kernel,
@@ -215,16 +214,15 @@
         ],
         out_shape=[
             filtered_shape,
-            pltpu.HBM((ORBS, 12) + plane, F32),
+            jax.ShapeDtypeStruct((ORBS, 12) + plane, F32),
             pltpu.HBM((PEERS, 264, 128), F32),
         ],
         scratch_shapes=[pltpu.VMEM((PEERS, 64, 128), F32)],
         compiler_params=params(),
         cost_estimate=cost(1_000_000, 1_000_000),
         name="filter_inner",
-    )(lower_cut, upper_bound, orb_hbm, pot_hbm, rot_tile)
+    )(lower_cut, upper_bound, orbitals, potential, rot_tile)
     received = lax.all_to_all(send, "orb", split_axis=0, concat_axis=0, tiled=True)
-    stored = pltpu.with_memory_space_constraint(stored, pltpu.HBM)
 
     filtered, *sends_outer = pl.pallas_call(
         outer_kernel,
@@ -255,7 +253,7 @@
         compiler_params=params(),
         cost_estimate=cost(400_000_000_000, 400_000_000),
         name="filter_outer",
-    )(mine, lower_cut, upper_bound, orb_hbm, pot_hbm, stored, low, low, high, high, filtered)
+    )(mine, lower_cut, upper_bound, orbitals, potential, stored, low, low, high, high, filtered)
     received_outer = regroup(sends_outer)
 
     weights = received[:, 256, : ORBS * NCOL]

time: 98.7 us -> 102 us (1.033)
  starting transfers between devices: 47.3 us -> 53.8 us
  waiting for transfers between devices: 24 us -> 19.1 us
  other arithmetic: 0.08 us -> 1.76 us
  Pallas kernels: 21.4 us -> 19.9 us
  local copies, waits for them, and re-layouts: 3.05 us -> 4.39 us
    ppermute x7, starting transfers between devices: 22.2 us -> 28.6 us  [regroup(): lax.ppermute(sends[k], 'orb', [(o, o ^ k) for o in range(PEERS)])]
    ppermute x7, waiting for transfers between devices: 15.7 us -> 11.5 us  [regroup(): lax.ppermute(sends[k], 'orb', [(o, o ^ k) for o in range(PEERS)])]
    concatenate x2, other arithmetic: 0.08 us -> 1.76 us  [packed(): jnp.concatenate([own, potential[first_local:first_local + 2]], axis=0)]
    unnamed x2 -> x10, local copies, waits for them, and re-layouts: 0.01 us -> 1.2 us
    pallas_call x1, Pallas kernels: 7.5 us -> 6.37 us  [body(): pl.pallas_call(inner_kernel, grid=(ORBS,), in_specs=[SMEM, SMEM, pl.Block...]
  transfers between devices with their start and end apart: 10 -> 10, of which waited for: 5 -> 3; matrix products, arithmetic and copies ran while one was open for 1% -> 2% of each run, Pallas kernels for 19% -> 17%
where the time goes in v2:
time: 102 us; the launch traced here: 101 us
  starting transfers between devices  53.8 us (53%)
  Pallas kernels  19.9 us (20%)
  waiting for transfers between devices  19.1 us (19%)
  local copies, waits for them, and re-layouts  4.39 us (4%)
  between operations  2.09 us (2%)
  other arithmetic  1.76 us (2%)
    ppermute x7, starting transfers between devices, regroup(): lax.ppermute(sends[k], 'orb', [(o, o ^ k) for o in range(PEERS)])  28.6 us
    ppermute x1, starting transfers between devices, body(): high = lax.ppermute(packed(0, 0), 'grid', backward)  14.2 us
    ppermute x7, waiting for transfers between devices, regroup(): lax.ppermute(sends[k], 'orb', [(o, o ^ k) for o in range(PEERS)])  11.5 us
    pallas_call x1, Pallas kernels, body(): pl.pallas_call(outer_kernel, grid=(ORBS, 2), in_specs=[SMEM, SMEM, SMEM,...  7.57 us
    ppermute x1, waiting for transfers between devices, body(): low = lax.ppermute(packed(PLANES - REACH, PLANES - 2), 'grid', forward)  7.31 us
    all_to_all x1, starting transfers between devices, body(): lax.all_to_all(send, 'orb', split_axis=0, concat_axis=0, tiled=True)  7 us
    pallas_call x1, Pallas kernels, body(): pl.pallas_call(inner_kernel, grid=(ORBS,), in_specs=[SMEM, SMEM, pl.Block...  6.37 us
    ppermute x1, starting transfers between devices, body(): low = lax.ppermute(packed(PLANES - REACH, PLANES - 2), 'grid', forward)  3.99 us
  transfers between devices with their start and end apart: 10, of which 3 were waited for; matrix products, arithmetic and copies ran while one was open for 2% of the time, Pallas kernels for 17%

profile of v2, /device:TPU:17, one launch (start us, length us, event | category | flops | bytes accessed | tf_op | source)
XLA Modules:
  0.0 101.1 jit_solution(14813788960833046201)
XLA Ops:
  0.6 0.9 fusion.1
  1.5 0.0 copy-start.4
  1.5 0.0 copy-start
  1.5 0.0 copy-start.1
  1.6 1.5 %fusion = (f32[4,4,32,256]{3,2,1,0:T(8,128)S(1)}, f32[4,4,32,256]{3,2,1,0:T(8,128)S(1)}) fusion(f32[4,16,32,256]{3,2,1,0:T(8,128)} %orb_ref.3), kind=kLoop, calls=%fused_computation.2 | loop fusion | bytes 2097152 | tf_op jit(solution)/shard_map/slice | solution.py:184
  3.0 0.9 pad_maximum_fusion
  3.9 4.0 %collective-permute-start = (f32[18,32,256]{2,1,0:T(8,128)}, f32[18,32,256]{2,1,0:T(8,128)S(1)}, u32[]{:S(2)}, u32[]{:S(2)}) collective-permute-start(f32[18,32,256]{2,1,0:T(8,128)} %pad_maximum_fusion), channel_id=1, source_target_pairs={{0,8},{8,16},{16,24},{24,32},{32,40},{40,48},{48,56},{56,64},{64,7... | collective-permute-start | bytes 1769480 | tf_op jit(solution)/shard_map/ppermute | solution.py:187
  7.9 0.9 pad_maximum_fusion.1
  8.8 14.2 %collective-permute-start.1 = (f32[18,32,256]{2,1,0:T(8,128)}, f32[18,32,256]{2,1,0:T(8,128)}, u32[]{:S(2)}, u32[]{:S(2)}) collective-permute-start(f32[18,32,256]{2,1,0:T(8,128)} %pad_maximum_fusion.1), channel_id=1, source_target_pairs={{8,0},{16,8},{24,16},{32,24},{40,32},{48,40},{56,48},{64,56},{72,6... | collective-permute-start | bytes 1769480 | tf_op jit(solution)/shard_map/ppermute | solution.py:188
  24.3 0.0 copy-done.4
  24.3 0.1 reshape.17
  24.4 0.0 copy-done
  24.4 0.0 copy-done.1
  24.4 6.4 %filter_inner.1 = (f32[4,16,32,256]{3,2,1,0:T(8,128)}, f32[4,12,32,256]{3,2,1,0:T(8,128)S(1)}, f32[8,264,128]{2,1,0:T(8,128)}) custom-call(f32[1]{0:T(128)S(6)} %copy.15.lower_ref, f32[1]{0:T(128)S(6)} %copy.16.upper_ref, f32[4,16,32,256]{3,2,1,0:T(8,128)S(1)} %copy-done, f32[16,32,256]{2,1,0:T(8,128)S(1)} %copy-done.1, f32[8,128]{1,0:T(8,128)S(1)} %pad.4.rot_ref), custom_call_target="tpu_custom_call" | custom-call | flops 1000000 | bytes 1000000 | tf_op jit(solution)/shard_map/filter_inner/pallas_call | solution.py:200
  30.8 0.0 copy-start.2
  30.8 1.2 %copy-done.2 = f32[4,12,32,256]{3,2,1,0:T(8,128)} copy-done((f32[4,12,32,256]{3,2,1,0:T(8,128)}, f32[4,12,32,256]{3,2,1,0:T(8,128)S(1)}, u32[]{:S(2)}) %copy-start.2) | copy-done | bytes 1572888
  32.0 0.0 copy-start.3
  32.0 7.0 %all-to-all-start = ((f32[8,264,128]{2,1,0:T(8,128)}), f32[8,264,128]{2,1,0:T(8,128)}, u32[]{:S(2)}, u32[]{:S(2)}) async-start(f32[8,264,128]{2,1,0:T(8,128)} %get-tuple-element.17), calls=%async_computation | async-start | bytes 2162688 | tf_op jit(solution)/shard_map/all_to_all | solution.py:225
  39.0 7.3 %collective-permute-done.low_ref.low_pot_ref = f32[18,32,256]{2,1,0:T(8,128)S(1)} collective-permute-done((f32[18,32,256]{2,1,0:T(8,128)}, f32[18,32,256]{2,1,0:T(8,128)S(1)}, u32[]{:S(2)}, u32[]{:S(2)}) %collective-permute-start) | collective-permute-done | bytes 589856 | tf_op jit(solution)/shard_map/ppermute | solution.py:187
  46.3 0.3 collective-permute-done.1.high_ref.high_pot_ref
  46.6 0.0 copy-done.3
  46.6 7.6 %filter_outer.1 = (f32[4,16,32,256]{3,2,1,0:T(8,128)}, f32[256,128]{1,0:T(8,128)S(1)}, f32[256,128]{1,0:T(8,128)S(1)}, f32[256,128]{1,0:T(8,128)S(1)}, f32[256,1...) custom-call(s32[1]{0:T(128)} %bitcast.mine_ref, ...), custom_call_target="tpu_custom_call", output_to_operand_aliasing={{0}: (10, {})} | custom-call | flops 399999991808 | bytes 400000000 | tf_op jit(solution)/shard_map/filter_outer/pallas_call | solution.py:227
  54.2 1.9 %collective-permute-start.2 = (f32[256,128]{1,0:T(8,128)S(1)}, f32[256,128]{1,0:T(8,128)S(1)}, u32[]{:S(2)}, u32[]{:S(2)}) collective-permute-start(f32[256,128]{1,0:T(8,128)S(1)} %get-tuple-element.18), channel_id=1, source_target_pairs={{0,4},{1,5},{2,6},{3,7},{4,0},{5,1},{6,2},{7,3},{8,12},{9,13},{10,... | collective-permute-start | bytes 393224 | tf_op jit(solution)/shard_map/ppermute | solution.py:196
  56.1 7.9 %collective-permute-start.3 = (f32[256,128]{1,0:T(8,128)S(1)}, f32[256,128]{1,0:T(8,128)S(1)}, u32[]{:S(2)}, u32[]{:S(2)}) collective-permute-start(f32[256,128]{1,0:T(8,128)S(1)} %get-tuple-element.19), channel_id=1, source_target_pairs={{0,5},{1,4},{2,7},{3,6},{4,1},{5,0},{6,3},{7,2},{8,13},{9,12},{10,... | collective-permute-start | bytes 393224 | tf_op jit(solution)/shard_map/ppermute | solution.py:196
  64.0 3.2 %collective-permute-start.4 = (f32[256,128]{1,0:T(8,128)S(1)}, f32[256,128]{1,0:T(8,128)S(1)}, u32[]{:S(2)}, u32[]{:S(2)}) collective-permute-start(f32[256,128]{1,0:T(8,128)S(1)} %get-tuple-element.20), channel_id=1, source_target_pairs={{0,6},{1,7},{2,4},{3,5},{4,2},{5,3},{6,0},{7,1},{8,14},{9,15},{10,... | collective-permute-start | bytes 393224 | tf_op jit(solution)/shard_map/ppermute | solution.py:196
  67.2 2.5 %collective-permute-start.5 = (f32[256,128]{1,0:T(8,128)S(1)}, f32[256,128]{1,0:T(8,128)S(1)}, u32[]{:S(2)}, u32[]{:S(2)}) collective-permute-start(f32[256,128]{1,0:T(8,128)S(1)} %get-tuple-element.21), channel_id=1, source_target_pairs={{0,7},{1,6},{2,5},{3,4},{4,3},{5,2},{6,1},{7,0},{8,15},{9,14},{10,... | collective-permute-start | bytes 393224 | tf_op jit(solution)/shard_map/ppermute | solution.py:196
  69.7 3.7 %collective-permute-start.6 = (f32[256,128]{1,0:T(8,128)S(1)}, f32[256,128]{1,0:T(8,128)S(1)}, u32[]{:S(2)}, u32[]{:S(2)}) collective-permute-start(f32[256,128]{1,0:T(8,128)S(1)} %get-tuple-element.22), channel_id=1, source_target_pairs={{0,2},{1,3},{2,0},{3,1},{4,6},{5,7},{6,4},{7,5},{8,10},{9,11},{10,... | collective-permute-start | bytes 393224 | tf_op jit(solution)/shard_map/ppermute | solution.py:196
  73.4 11.5 %collective-permute-done.2.rest_0_ = f32[256,128]{1,0:T(8,128)S(1)} collective-permute-done((f32[256,128]{1,0:T(8,128)S(1)}, f32[256,128]{1,0:T(8,128)S(1)}, u32[]{:S(2)}, u32[]{:S(2)}) %collective-permute-start.2) | collective-permute-done | bytes 131104 | tf_op jit(solution)/shard_map/ppermute | solution.py:196
  84.9 7.5 %collective-permute-start.7 = (f32[256,128]{1,0:T(8,128)S(1)}, f32[256,128]{1,0:T(8,128)S(1)}, u32[]{:S(2)}, u32[]{:S(2)}) collective-permute-start(f32[256,128]{1,0:T(8,128)S(1)} %get-tuple-element.23), channel_id=1, source_target_pairs={{0,3},{1,2},{2,1},{3,0},{4,7},{5,6},{6,5},{7,4},{8,11},{9,10},{10,... | collective-permute-start | bytes 393224 | tf_op jit(solution)/shard_map/ppermute | solution.py:196
  92.4 0.0 collective-permute-done.3.rest_1_
  92.4 1.9 %collective-permute-start.8 = (f32[256,128]{1,0:T(8,128)S(1)}, f32[256,128]{1,0:T(8,128)S(1)}, u32[]{:S(2)}, u32[]{:S(2)}) collective-permute-start(f32[256,128]{1,0:T(8,128)S(1)} %get-tuple-element.24), channel_id=1, source_target_pairs={{0,1},{1,0},{2,3},{3,2},{4,5},{5,4},{6,7},{7,6},{8,9},{9,8},{10,11... | collective-permute-start | bytes 393224 | tf_op jit(solution)/shard_map/ppermute | solution.py:196
  94.3 0.0 all-to-all-done.recv_ref
  94.3 0.8 slice.20
  95.1 3.3 %rotate_inner.1.rest_8_ = f32[16,16,4,256]{3,2,1,0:T(4,128)} custom-call(f32[8,64]{1,0:T(8,128)S(1)} %bitcast.6, f32[8,264,128]{2,1,0:T(8,128)} %all-to-all-done.recv_ref), custom_call_target="tpu_custom_call" | custom-call | flops 8000000 | bytes 1600000 | tf_op jit(solution)/shard_map/rotate_inner/pallas_call | solution.py:262
  98.4 0.0 collective-permute-done.4.rest_2_
  98.4 0.0 collective-permute-done.5.rest_3_
  98.4 0.0 collective-permute-done.6.rest_4_
  98.4 0.0 collective-permute-done.7.rest_5_
  98.4 0.0 collective-permute-done.8.rest_6_
  98.4 2.7 %rotate_outer.1 = f32[16,16,4,256]{3,2,1,0:T(4,128)} custom-call(s32[1]{0:T(128)} %bitcast.mine_ref, f32[8,64]{1,0:T(8,128)S(1)} %bitcast.7, f32[256,128]{1,0:T(8,128)S(1)} %collective-permute-done.2.rest_0_, f32[256,128]{1,0:T(8,128)S(1)} %collective-permute-done.3.rest_1_, ...), custom_call_target="tpu_custom_call", output_to_operand_aliasing={{}: (10, {})} | custom-call | flops 8000000 | bytes 1600000 | tf_op jit(solution)/shard_map/rotate_outer/pallas_call | solution.py:272
  (1 shorter events, 0.0 us)
Async XLA Ops:
  1.5 22.8 %copy-start.4 = (f32[4,16]{1,0:T(4,128)S(1)}, f32[4,16]{1,0:T(4,128)}, u32[]{:S(2)}) copy-start(f32[4,16]{1,0:T(4,128)} %param.9) | copy-start | bytes 772
  1.5 22.9 %copy-start = (f32[4,16,32,256]{3,2,1,0:T(8,128)S(1)}, f32[4,16,32,256]{3,2,1,0:T(8,128)}, u32[]{:S(2)}) copy-start(f32[4,16,32,256]{3,2,1,0:T(8,128)} %orb_ref.3) | copy-start | bytes 6291460
  1.5 22.9 %copy-start.1 = (f32[16,32,256]{2,1,0:T(8,128)S(1)}, f32[16,32,256]{2,1,0:T(8,128)}, u32[]{:S(2)}) copy-start(f32[16,32,256]{2,1,0:T(8,128)} %pot_ref.3) | copy-start | bytes 1572868
  3.9 42.4 %collective-permute-start = (f32[18,32,256]{2,1,0:T(8,128)}, f32[18,32,256]{2,1,0:T(8,128)S(1)}, u32[]{:S(2)}, u32[]{:S(2)}) collective-permute-start(f32[18,32,256]{2,1,0:T(8,128)} %pad_maximum_fusion), channel_id=1, source_target_pairs={{0,8},{8,16},{16,24},{24,32},{32,40},{40,48},{48,56},{56,64},{64,7... | collective-permute-start | bytes 1769480 | tf_op jit(solution)/shard_map/ppermute | solution.py:187
  8.8 37.8 %collective-permute-start.1 = (f32[18,32,256]{2,1,0:T(8,128)}, f32[18,32,256]{2,1,0:T(8,128)}, u32[]{:S(2)}, u32[]{:S(2)}) collective-permute-start(f32[18,32,256]{2,1,0:T(8,128)} %pad_maximum_fusion.1), channel_id=1, source_target_pairs={{8,0},{16,8},{24,16},{32,24},{40,32},{48,40},{56,48},{64,56},{72,6... | collective-permute-start | bytes 1769480 | tf_op jit(solution)/shard_map/ppermute | solution.py:188
  30.8 1.2 %copy-start.2 = (f32[4,12,32,256]{3,2,1,0:T(8,128)}, f32[4,12,32,256]{3,2,1,0:T(8,128)S(1)}, u32[]{:S(2)}) copy-start(f32[4,12,32,256]{3,2,1,0:T(8,128)S(1)} %get-tuple-element.14.stored_ref) | copy-start | bytes 4718596
  32.0 14.6 %copy-start.3 = (f32[4,12,32,256]{3,2,1,0:T(8,128)S(1)}, f32[4,12,32,256]{3,2,1,0:T(8,128)}, u32[]{:S(2)}) copy-start(f32[4,12,32,256]{3,2,1,0:T(8,128)} %copy-done.2) | copy-start | bytes 4718596
  32.0 62.4 %all-to-all-start = ((f32[8,264,128]{2,1,0:T(8,128)}), f32[8,264,128]{2,1,0:T(8,128)}, u32[]{:S(2)}, u32[]{:S(2)}) async-start(f32[8,264,128]{2,1,0:T(8,128)} %get-tuple-element.17), calls=%async_computation | async-start | bytes 2162688 | tf_op jit(solution)/shard_map/all_to_all | solution.py:225
  54.2 30.7 %collective-permute-start.2 = (f32[256,128]{1,0:T(8,128)S(1)}, f32[256,128]{1,0:T(8,128)S(1)}, u32[]{:S(2)}, u32[]{:S(2)}) collective-permute-start(f32[256,128]{1,0:T(8,128)S(1)} %get-tuple-element.18), channel_id=1, source_target_pairs={{0,4},{1,5},{2,6},{3,7},{4,0},{5,1},{6,2},{7,3},{8,12},{9,13},{10,... | collective-permute-start | bytes 393224 | tf_op jit(solution)/shard_map/ppermute | solution.py:196
  56.1 36.3 %collective-permute-start.3 = (f32[256,128]{1,0:T(8,128)S(1)}, f32[256,128]{1,0:T(8,128)S(1)}, u32[]{:S(2)}, u32[]{:S(2)}) collective-permute-start(f32[256,128]{1,0:T(8,128)S(1)} %get-tuple-element.19), channel_id=1, source_target_pairs={{0,5},{1,4},{2,7},{3,6},{4,1},{5,0},{6,3},{7,2},{8,13},{9,12},{10,... | collective-permute-start | bytes 393224 | tf_op jit(solution)/shard_map/ppermute | solution.py:196
  64.0 34.4 %collective-permute-start.4 = (f32[256,128]{1,0:T(8,128)S(1)}, f32[256,128]{1,0:T(8,128)S(1)}, u32[]{:S(2)}, u32[]{:S(2)}) collective-permute-start(f32[256,128]{1,0:T(8,128)S(1)} %get-tuple-element.20), channel_id=1, source_target_pairs={{0,6},{1,7},{2,4},{3,5},{4,2},{5,3},{6,0},{7,1},{8,14},{9,15},{10,... | collective-permute-start | bytes 393224 | tf_op jit(solution)/shard_map/ppermute | solution.py:196
  67.2 31.2 %collective-permute-start.5 = (f32[256,128]{1,0:T(8,128)S(1)}, f32[256,128]{1,0:T(8,128)S(1)}, u32[]{:S(2)}, u32[]{:S(2)}) collective-permute-start(f32[256,128]{1,0:T(8,128)S(1)} %get-tuple-element.21), channel_id=1, source_target_pairs={{0,7},{1,6},{2,5},{3,4},{4,3},{5,2},{6,1},{7,0},{8,15},{9,14},{10,... | collective-permute-start | bytes 393224 | tf_op jit(solution)/shard_map/ppermute | solution.py:196
  69.7 28.7 %collective-permute-start.6 = (f32[256,128]{1,0:T(8,128)S(1)}, f32[256,128]{1,0:T(8,128)S(1)}, u32[]{:S(2)}, u32[]{:S(2)}) collective-permute-start(f32[256,128]{1,0:T(8,128)S(1)} %get-tuple-element.22), channel_id=1, source_target_pairs={{0,2},{1,3},{2,0},{3,1},{4,6},{5,7},{6,4},{7,5},{8,10},{9,11},{10,... | collective-permute-start | bytes 393224 | tf_op jit(solution)/shard_map/ppermute | solution.py:196
  84.9 13.5 %collective-permute-start.7 = (f32[256,128]{1,0:T(8,128)S(1)}, f32[256,128]{1,0:T(8,128)S(1)}, u32[]{:S(2)}, u32[]{:S(2)}) collective-permute-start(f32[256,128]{1,0:T(8,128)S(1)} %get-tuple-element.23), channel_id=1, source_target_pairs={{0,3},{1,2},{2,1},{3,0},{4,7},{5,6},{6,5},{7,4},{8,11},{9,10},{10,... | collective-permute-start | bytes 393224 | tf_op jit(solution)/shard_map/ppermute | solution.py:196
  92.4 6.0 %collective-permute-start.8 = (f32[256,128]{1,0:T(8,128)S(1)}, f32[256,128]{1,0:T(8,128)S(1)}, u32[]{:S(2)}, u32[]{:S(2)}) collective-permute-start(f32[256,128]{1,0:T(8,128)S(1)} %get-tuple-element.24), channel_id=1, source_target_pairs={{0,1},{1,0},{2,3},{3,2},{4,5},{5,4},{6,7},{7,6},{8,9},{9,8},{10,11... | collective-permute-start | bytes 393224 | tf_op jit(solution)/shard_map/ppermute | solution.py:196

commit v3 on v2

--- a/solution.py
+++ b/solution.py
@@ -10,8 +10,8 @@
 ORBS, PLANES, ROWS, COLS = 4, 16, 32, 256
 REACH = 4
 PEERS, NCOL = 8, 16
-LIMIT = 48 * 1024 * 1024
-ORDER = (4, 5, 6, 7, 2, 3, 1, 0)
+LIMIT = 20 * 1024 * 1024
+ORDER = (1, 2, 4, 5, 6, 7, 3, 0)
 
 
 def coefficients(lower_ref, upper_ref):
@@ -65,14 +65,14 @@
     orbital = pl.program_id(0)
 
     def store(p, value):
-        first_ref[0, p] = value
-
-    first_planes(12, lambda p: orb_ref[0, p], lambda p: pot_ref[p + 2], store, coef)
+        first_ref[orbital, p] = value
+
+    first_planes(12, lambda p: orb_ref[orbital, p], lambda p: pot_ref[p + 2], store, coef)
     for t in range(4):
         pair = []
         for q in (2 * t, 2 * t + 1):
             g = filtered_plane(
-                q, lambda p: first_ref[0, p], orb_ref[0, q + 4], pot_ref[q + 4], coef
+                q, lambda p: first_ref[orbital, p], orb_ref[orbital, q + 4], pot_ref[q + 4], coef
             )
             out_ref[0, q + 4] = g
             pair.append(g)
@@ -83,44 +83,47 @@
 
 
 def outer_kernel(
-    mine_ref, lower_ref, upper_ref, orb_ref, pot_ref, stored_ref, low_ref, low_pot_ref,
-    high_ref, high_pot_ref, _, *rest,
+    mine_ref, lower_ref, upper_ref, orb_ref, pot_ref, stored_ref, low_ref, high_ref, _, *rest
 ):
-    out_ref, sends, (ext_ref, local_ref, first_ref, slots_ref) = rest[0], rest[1:-4], rest[-4:]
+    out_ref, sends, (fresh_ref, slots_ref) = rest[0], rest[1:-2], rest[-2:]
     coef = coefficients(lower_ref, upper_ref)
-    mine, side = mine_ref[0], pl.program_id(1)
+    mine, i, side = mine_ref[0], pl.program_id(0), pl.program_id(1)
+    halo = REACH * i
+
+    def filter_side(raw, local, first, original, own_local):
+        for p in range(4):
+            fresh_ref[p] = scaled_hamilton([raw(p + d) for d in range(5)], local(p), coef)
+        for t in range(2):
+            pair = []
+            for q in (2 * t, 2 * t + 1):
+                g = filtered_plane(q, first, original(q), own_local(q), coef)
+                out_ref[0, q] = g
+                pair.append(g)
+            pack_pair(mine, slots_ref, t * 16, *pair)
 
     @pl.when(side == 0)
     def _():
-        ext_ref[0:4] = low_ref[...]
-        ext_ref[4:8] = orb_ref[0]
-        local_ref[0:2] = low_pot_ref[...]
-        local_ref[2:4] = pot_ref[0:2]
-        first_ref[4:8] = stored_ref[0]
+        filter_side(
+            lambda p: low_ref[halo + p] if p < 4 else orb_ref[i, p - 4],
+            lambda p: low_ref[ORBS * REACH + p] if p < 2 else pot_ref[p - 2],
+            lambda p: fresh_ref[p] if p < 4 else stored_ref[i, p - 4],
+            lambda q: orb_ref[i, q],
+            lambda q: pot_ref[q],
+        )
 
     @pl.when(side == 1)
     def _():
-        ext_ref[0:4] = orb_ref[0]
-        ext_ref[4:8] = high_ref[...]
-        local_ref[0:2] = pot_ref[14:16]
-        local_ref[2:4] = high_pot_ref[...]
-        first_ref[0:4] = stored_ref[0]
-
-    def store(p, value):
-        first_ref[4 * side + p] = value
-
-    first_planes(4, lambda p: ext_ref[p], lambda p: local_ref[p], store, coef)
-    for t in range(2):
-        pair = []
-        for q in (2 * t, 2 * t + 1):
-            g = filtered_plane(
-                q, lambda p: first_ref[p], ext_ref[q + 4 - 4 * side], pot_ref[q + 12 * side], coef
-            )
-            out_ref[0, q] = g
-            pair.append(g)
-        pack_pair(mine, slots_ref, t * 16, *pair)
+        filter_side(
+            lambda p: orb_ref[i, 12 + p] if p < 4 else high_ref[halo + p - 4],
+            lambda p: pot_ref[14 + p] if p < 2 else high_ref[ORBS * REACH + p - 2],
+            lambda p: stored_ref[i, 8 + p] if p < 4 else fresh_ref[p - 4],
+            lambda q: orb_ref[i, 12 + q],
+            lambda q: pot_ref[12 + q],
+        )
+
+    rows = pl.ds(pl.multiple_of((2 * i + side) * 32, 32), 32)
     for slot, send_ref in enumerate(sends):
-        send_ref[...] = slots_ref[slot]
+        send_ref[rows, :] = slots_ref[slot]
 
 
 def rotate_tiles(u, tile, weight, out_ref):
@@ -163,6 +166,7 @@
 
 
 SMEM = pl.BlockSpec(memory_space=pltpu.SMEM)
+VMEM = pl.BlockSpec(memory_space=pltpu.VMEM)
 ANY = pl.BlockSpec(memory_space=pl.ANY)
 
 
@@ -203,13 +207,13 @@
         in_specs=[
             SMEM,
             SMEM,
-            pl.BlockSpec((1, PLANES) + plane, lambda i: (i, 0, 0, 0)),
-            pl.BlockSpec((PLANES,) + plane, lambda i: (0, 0, 0)),
-            pl.BlockSpec((8, 128), lambda i: (0, 0)),
+            VMEM,
+            VMEM,
+            VMEM,
         ],
         out_specs=[
             pl.BlockSpec((1, PLANES) + plane, lambda i: (i, 0, 0, 0)),
-            pl.BlockSpec((1, 12) + plane, lambda i: (i, 0, 0, 0)),
+            VMEM,
             pl.BlockSpec((PEERS, 264, 128), lambda i: (0, 0, 0)),
         ],
         out_shape=[
@@ -227,42 +231,26 @@
     filtered, *sends_outer = pl.pallas_call(
         outer_kernel,
         grid=(ORBS, 2),
-        in_specs=[
-            SMEM,
-            SMEM,
-            SMEM,
-            pl.BlockSpec((1, 4) + plane, lambda i, s: (i, 3 * s, 0, 0)),
-            pl.BlockSpec((PLANES,) + plane, lambda i, s: (0, 0, 0)),
-            pl.BlockSpec((1, 4) + plane, lambda i, s: (i, 2 * s, 0, 0)),
-            pl.BlockSpec((4,) + plane, lambda i, s: (i, 0, 0)),
-            pl.BlockSpec((2,) + plane, lambda i, s: (8, 0, 0)),
-            pl.BlockSpec((4,) + plane, lambda i, s: (i, 0, 0)),
-            pl.BlockSpec((2,) + plane, lambda i, s: (8, 0, 0)),
-            ANY,
-        ],
-        out_specs=[pl.BlockSpec((1, 4) + plane, lambda i, s: (i, 3 * s, 0, 0))]
-        + [pl.BlockSpec((32, 128), lambda i, s: (2 * i + s, 0))] * PEERS,
+        in_specs=[SMEM] * 3 + [VMEM] * 5 + [ANY],
+        out_specs=[pl.BlockSpec((1, 4) + plane, lambda i, s: (i, 3 * s, 0, 0))] + [VMEM] * PEERS,
         out_shape=[filtered_shape] + [jax.ShapeDtypeStruct((256, 128), F32)] * PEERS,
         scratch_shapes=[
-            pltpu.VMEM((8,) + plane, F32),
             pltpu.VMEM((4,) + plane, F32),
-            pltpu.VMEM((8,) + plane, F32),
             pltpu.VMEM((PEERS, 32, 128), F32),
         ],
-        input_output_aliases={10: 0},
+        input_output_aliases={8: 0},
         compiler_params=params(),
         cost_estimate=cost(400_000_000_000, 400_000_000),
         name="filter_outer",
-    )(mine, lower_cut, upper_bound, orbitals, potential, stored, low, low, high, high, filtered)
+    )(mine, lower_cut, upper_bound, orbitals, potential, stored, low, high, filtered)
     received_outer = regroup(sends_outer)
 
     weights = received[:, 256, : ORBS * NCOL]
     rotated_shape = jax.ShapeDtypeStruct((NCOL, PLANES, 4, COLS), F32)
-    vmem = pl.BlockSpec(memory_space=pltpu.VMEM)
     rotated = pl.pallas_call(
         rotate_inner_kernel,
         grid=(2,),
-        in_specs=[SMEM, vmem],
+        in_specs=[SMEM, VMEM],
         out_specs=pl.BlockSpec((NCOL, 4, 4, COLS), lambda u: (0, 1 + u, 0, 0)),
         out_shape=rotated_shape,
         compiler_params=params(),
@@ -272,7 +260,7 @@
     rotated = pl.pallas_call(
         rotate_outer_kernel,
         grid=(2,),
-        in_specs=[SMEM, SMEM] + [vmem] * PEERS + [ANY],
+        in_specs=[SMEM, SMEM] + [VMEM] * PEERS + [ANY],
         out_specs=pl.BlockSpec((NCOL, 4, 4, COLS), lambda u: (0, 3 * u, 0, 0)),
         out_shape=rotated_shape,
         input_output_aliases={PEERS + 2: 0},

time: 102 us -> 101 us (level)
  starting transfers between devices: 53.8 us -> 49.8 us
  waiting for transfers between devices: 19.1 us -> 22.1 us
  Pallas kernels: 19.9 us -> 18.4 us
  local copies, waits for them, and re-layouts: 4.39 us -> 5.8 us
    ppermute x7, starting transfers between devices: 28.6 us -> 24.7 us  [regroup(): lax.ppermute(sends[k], 'orb', [(o, o ^ k) for o in range(PEERS)])]
    all_to_all x1, waiting for transfers between devices: 0.01 us -> 3.42 us  [body(): lax.all_to_all(send, 'orb', split_axis=0, concat_axis=0, tiled=True)]
    pallas_call x4, Pallas kernels: 19.9 us -> 18.4 us  [the longest x1 6.37 us: body(): pl.pallas_call(inner_kernel, grid=(ORBS,), in_specs=[SMEM, SMEM, VMEM, VM...]
    unnamed x10, local copies, waits for them, and re-layouts: 1.2 us -> 2.61 us
  transfers between devices with their start and end apart: 10 -> 10, of which waited for: 3 -> 6; matrix products, arithmetic and copies ran while one was open for 2% -> 2% of each run, Pallas kernels for 17% -> 16%
where the time goes in v3:
time: 101 us; the launch traced here: 99.9 us
  starting transfers between devices  49.8 us (49%)
  waiting for transfers between devices  22.1 us (22%)
  Pallas kernels  18.4 us (18%)
  local copies, waits for them, and re-layouts  5.8 us (6%)
  between operations  2.07 us (2%)
  other arithmetic  1.76 us (2%)
    ppermute x7, starting transfers between devices, regroup(): lax.ppermute(sends[k], 'orb', [(o, o ^ k) for o in range(PEERS)])  24.7 us
    ppermute x1, starting transfers between devices, body(): high = lax.ppermute(packed(0, 0), 'grid', backward)  14.2 us
    ppermute x7, waiting for transfers between devices, regroup(): lax.ppermute(sends[k], 'orb', [(o, o ^ k) for o in range(PEERS)])  11 us
    ppermute x1, waiting for transfers between devices, body(): low = lax.ppermute(packed(PLANES - REACH, PLANES - 2), 'grid', forward)  7.44 us
    all_to_all x1, starting transfers between devices, body(): lax.all_to_all(send, 'orb', split_axis=0, concat_axis=0, tiled=True)  6.87 us
    pallas_call x1, Pallas kernels, body(): pl.pallas_call(inner_kernel, grid=(ORBS,), in_specs=[SMEM, SMEM, VMEM, VM...  6.37 us
    pallas_call x1, Pallas kernels, body(): pl.pallas_call(outer_kernel, grid=(ORBS, 2), in_specs=[SMEM] * 3 + [VMEM]...  6.13 us
    ppermute x1, starting transfers between devices, body(): low = lax.ppermute(packed(PLANES - REACH, PLANES - 2), 'grid', forward)  3.99 us
  transfers between devices with their start and end apart: 10, of which 6 were waited for; matrix products, arithmetic and copies ran while one was open for 2% of the time, Pallas kernels for 16%

profile of v3, /device:TPU:17, one launch (start us, length us, event | category | flops | bytes accessed | tf_op | source)
XLA Modules:
  0.0 99.9 jit_solution(11252959192302218216)
XLA Ops:
  0.6 0.9 fusion.1
  1.5 0.0 copy-start.4
  1.5 0.0 copy-start
  1.5 0.0 copy-start.1
  1.6 1.5 %fusion = (f32[4,4,32,256]{3,2,1,0:T(8,128)S(1)}, f32[4,4,32,256]{3,2,1,0:T(8,128)S(1)}) fusion(f32[4,16,32,256]{3,2,1,0:T(8,128)} %orb_ref.3), kind=kLoop, calls=%fused_computation.2 | loop fusion | bytes 2097152 | tf_op jit(solution)/shard_map/slice | solution.py:188
  3.0 0.9 pad_maximum_fusion
  3.9 4.0 %collective-permute-start = (f32[18,32,256]{2,1,0:T(8,128)}, f32[18,32,256]{2,1,0:T(8,128)S(1)}, u32[]{:S(2)}, u32[]{:S(2)}) collective-permute-start(f32[18,32,256]{2,1,0:T(8,128)} %pad_maximum_fusion), channel_id=1, source_target_pairs={{0,8},{8,16},{16,24},{24,32},{32,40},{40,48},{48,56},{56,64},{64,7... | collective-permute-start | bytes 1769480 | tf_op jit(solution)/shard_map/ppermute | solution.py:191
  7.9 0.9 pad_maximum_fusion.1
  8.8 14.2 %collective-permute-start.1 = (f32[18,32,256]{2,1,0:T(8,128)}, f32[18,32,256]{2,1,0:T(8,128)}, u32[]{:S(2)}, u32[]{:S(2)}) collective-permute-start(f32[18,32,256]{2,1,0:T(8,128)} %pad_maximum_fusion.1), channel_id=1, source_target_pairs={{8,0},{16,8},{24,16},{32,24},{40,32},{48,40},{56,48},{64,56},{72,6... | collective-permute-start | bytes 1769480 | tf_op jit(solution)/shard_map/ppermute | solution.py:192
  24.3 0.0 copy-done.4
  24.3 0.1 reshape.17
  24.4 0.0 copy-done
  24.4 0.0 copy-done.1
  24.4 6.4 %filter_inner.1 = (f32[4,16,32,256]{3,2,1,0:T(8,128)}, f32[4,12,32,256]{3,2,1,0:T(8,128)S(1)}, f32[8,264,128]{2,1,0:T(8,128)}) custom-call(f32[1]{0:T(128)S(6)} %copy.15.lower_ref, f32[1]{0:T(128)S(6)} %copy.16.upper_ref, f32[4,16,32,256]{3,2,1,0:T(8,128)S(1)} %copy-done, f32[16,32,256]{2,1,0:T(8,128)S(1)} %copy-done.1, f32[8,128]{1,0:T(8,128)S(1)} %pad.4.rot_ref), custom_call_target="tpu_custom_call" | custom-call | flops 1000000 | bytes 1000000 | tf_op jit(solution)/shard_map/filter_inner/pallas_call | solution.py:204
  30.8 0.0 copy-start.2
  30.8 1.2 %copy-done.2 = f32[4,12,32,256]{3,2,1,0:T(8,128)} copy-done((f32[4,12,32,256]{3,2,1,0:T(8,128)}, f32[4,12,32,256]{3,2,1,0:T(8,128)S(1)}, u32[]{:S(2)}) %copy-start.2) | copy-done | bytes 1572888
  32.0 6.9 %all-to-all-start = ((f32[8,264,128]{2,1,0:T(8,128)}), f32[8,264,128]{2,1,0:T(8,128)}, u32[]{:S(2)}, u32[]{:S(2)}) async-start(f32[8,264,128]{2,1,0:T(8,128)} %get-tuple-element.17), calls=%async_computation | async-start | bytes 2162688 | tf_op jit(solution)/shard_map/all_to_all | solution.py:229
  38.8 7.4 %collective-permute-done.low_ref = f32[18,32,256]{2,1,0:T(8,128)S(1)} collective-permute-done((f32[18,32,256]{2,1,0:T(8,128)}, f32[18,32,256]{2,1,0:T(8,128)S(1)}, u32[]{:S(2)}, u32[]{:S(2)}) %collective-permute-start) | collective-permute-done | bytes 589856 | tf_op jit(solution)/shard_map/ppermute | solution.py:191
  46.3 0.3 collective-permute-done.1.high_ref
  46.6 0.0 copy-start.3
  46.6 1.4 %copy-done.3 = f32[4,12,32,256]{3,2,1,0:T(8,128)S(1)} copy-done((f32[4,12,32,256]{3,2,1,0:T(8,128)S(1)}, f32[4,12,32,256]{3,2,1,0:T(8,128)}, u32[]{:S(2)}) %copy-start.3) | copy-done | bytes 1572888
  48.0 6.1 %filter_outer.1 = (f32[4,16,32,256]{3,2,1,0:T(8,128)}, f32[256,128]{1,0:T(8,128)S(1)}, f32[256,128]{1,0:T(8,128)S(1)}, f32[256,128]{1,0:T(8,128)S(1)}, f32[256,1...) custom-call(s32[1]{0:T(128)} %bitcast.mine_ref, ...), custom_call_target="tpu_custom_call", output_to_operand_aliasing={{0}: (8, {})} | custom-call | flops 399999991808 | bytes 400000000 | tf_op jit(solution)/shard_map/filter_outer/pallas_call | solution.py:231
  54.1 5.4 %collective-permute-start.2 = (f32[256,128]{1,0:T(8,128)S(1)}, f32[256,128]{1,0:T(8,128)S(1)}, u32[]{:S(2)}, u32[]{:S(2)}) collective-permute-start(f32[256,128]{1,0:T(8,128)S(1)} %get-tuple-element.18), channel_id=1, source_target_pairs={{0,1},{1,0},{2,3},{3,2},{4,5},{5,4},{6,7},{7,6},{8,9},{9,8},{10,11... | collective-permute-start | bytes 393224 | tf_op jit(solution)/shard_map/ppermute | solution.py:200
  59.5 1.9 %collective-permute-start.3 = (f32[256,128]{1,0:T(8,128)S(1)}, f32[256,128]{1,0:T(8,128)S(1)}, u32[]{:S(2)}, u32[]{:S(2)}) collective-permute-start(f32[256,128]{1,0:T(8,128)S(1)} %get-tuple-element.19), channel_id=1, source_target_pairs={{0,2},{1,3},{2,0},{3,1},{4,6},{5,7},{6,4},{7,5},{8,10},{9,11},{10,... | collective-permute-start | bytes 393224 | tf_op jit(solution)/shard_map/ppermute | solution.py:200
  61.4 4.4 %collective-permute-start.4 = (f32[256,128]{1,0:T(8,128)}, f32[256,128]{1,0:T(8,128)S(1)}, u32[]{:S(2)}, u32[]{:S(2)}) collective-permute-start(f32[256,128]{1,0:T(8,128)} %get-tuple-element.20), channel_id=1, source_target_pairs={{0,4},{1,5},{2,6},{3,7},{4,0},{5,1},{6,2},{7,3},{8,12},{9,13},{10,... | collective-permute-start | bytes 393224 | tf_op jit(solution)/shard_map/ppermute | solution.py:200
  65.9 2.1 %collective-permute-start.5 = (f32[256,128]{1,0:T(8,128)}, f32[256,128]{1,0:T(8,128)S(1)}, u32[]{:S(2)}, u32[]{:S(2)}) collective-permute-start(f32[256,128]{1,0:T(8,128)} %get-tuple-element.21), channel_id=1, source_target_pairs={{0,5},{1,4},{2,7},{3,6},{4,1},{5,0},{6,3},{7,2},{8,13},{9,12},{10,... | collective-permute-start | bytes 393224 | tf_op jit(solution)/shard_map/ppermute | solution.py:200
  67.9 4.9 %collective-permute-start.6 = (f32[256,128]{1,0:T(8,128)}, f32[256,128]{1,0:T(8,128)S(1)}, u32[]{:S(2)}, u32[]{:S(2)}) collective-permute-start(f32[256,128]{1,0:T(8,128)} %get-tuple-element.22), channel_id=1, source_target_pairs={{0,6},{1,7},{2,4},{3,5},{4,2},{5,3},{6,0},{7,1},{8,14},{9,15},{10,... | collective-permute-start | bytes 393224 | tf_op jit(solution)/shard_map/ppermute | solution.py:200
  72.8 0.0 collective-permute-done.2.rest_0_
  72.8 1.9 %collective-permute-start.7 = (f32[256,128]{1,0:T(8,128)}, f32[256,128]{1,0:T(8,128)S(1)}, u32[]{:S(2)}, u32[]{:S(2)}) collective-permute-start(f32[256,128]{1,0:T(8,128)} %get-tuple-element.23), channel_id=1, source_target_pairs={{0,7},{1,6},{2,5},{3,4},{4,3},{5,2},{6,1},{7,0},{8,15},{9,14},{10,... | collective-permute-start | bytes 393224 | tf_op jit(solution)/shard_map/ppermute | solution.py:200
  74.7 0.0 collective-permute-done.3.rest_1_
  74.7 4.1 %collective-permute-start.8 = (f32[256,128]{1,0:T(8,128)S(1)}, f32[256,128]{1,0:T(8,128)S(1)}, u32[]{:S(2)}, u32[]{:S(2)}) collective-permute-start(f32[256,128]{1,0:T(8,128)S(1)} %get-tuple-element.24), channel_id=1, source_target_pairs={{0,3},{1,2},{2,1},{3,0},{4,7},{5,6},{6,5},{7,4},{8,11},{9,10},{10,... | collective-permute-start | bytes 393224 | tf_op jit(solution)/shard_map/ppermute | solution.py:200
  78.9 3.4 %all-to-all-done.recv_ref = f32[8,264,128]{2,1,0:T(8,128)} async-done(((f32[8,264,128]{2,1,0:T(8,128)}), f32[8,264,128]{2,1,0:T(8,128)}, u32[]{:S(2)}, u32[]{:S(2)}) %all-to-all-start) | async-done | bytes 1081376 | tf_op jit(solution)/shard_map/all_to_all | solution.py:229
  82.3 0.8 slice.20
  83.1 3.3 %rotate_inner.1.rest_8_ = f32[16,16,4,256]{3,2,1,0:T(4,128)} custom-call(f32[8,64]{1,0:T(8,128)S(1)} %bitcast.6, f32[8,264,128]{2,1,0:T(8,128)} %all-to-all-done.recv_ref), custom_call_target="tpu_custom_call" | custom-call | flops 8000000 | bytes 1600000 | tf_op jit(solution)/shard_map/rotate_inner/pallas_call | solution.py:250
  86.3 0.0 collective-permute-done.4.rest_2_
  86.3 1.6 %collective-permute-done.5.rest_3_ = f32[256,128]{1,0:T(8,128)S(1)} collective-permute-done((f32[256,128]{1,0:T(8,128)}, f32[256,128]{1,0:T(8,128)S(1)}, u32[]{:S(2)}, u32[]{:S(2)}) %collective-permute-start.5) | collective-permute-done | bytes 131104 | tf_op jit(solution)/shard_map/ppermute | solution.py:200
  87.9 6.6 %collective-permute-done.6.rest_4_ = f32[256,128]{1,0:T(8,128)S(1)} collective-permute-done((f32[256,128]{1,0:T(8,128)}, f32[256,128]{1,0:T(8,128)S(1)}, u32[]{:S(2)}, u32[]{:S(2)}) %collective-permute-start.6) | collective-permute-done | bytes 131104 | tf_op jit(solution)/shard_map/ppermute | solution.py:200
  94.5 2.8 %collective-permute-done.7.rest_5_ = f32[256,128]{1,0:T(8,128)S(1)} collective-permute-done((f32[256,128]{1,0:T(8,128)}, f32[256,128]{1,0:T(8,128)S(1)}, u32[]{:S(2)}, u32[]{:S(2)}) %collective-permute-start.7) | collective-permute-done | bytes 131104 | tf_op jit(solution)/shard_map/ppermute | solution.py:200
  97.3 0.0 collective-permute-done.8.rest_6_
  97.3 2.6 %rotate_outer.1 = f32[16,16,4,256]{3,2,1,0:T(4,128)} custom-call(s32[1]{0:T(128)} %bitcast.mine_ref, f32[8,64]{1,0:T(8,128)S(1)} %bitcast.7, f32[256,128]{1,0:T(8,128)S(1)} %collective-permute-done.2.rest_0_, f32[256,128]{1,0:T(8,128)S(1)} %collective-permute-done.3.rest_1_, ...), custom_call_target="tpu_custom_call", output_to_operand_aliasing={{}: (10, {})} | custom-call | flops 8000000 | bytes 1600000 | tf_op jit(solution)/shard_map/rotate_outer/pallas_call | solution.py:260
  (1 shorter events, 0.0 us)
Async XLA Ops:
  1.5 22.8 %copy-start.4 = (f32[4,16]{1,0:T(4,128)S(1)}, f32[4,16]{1,0:T(4,128)}, u32[]{:S(2)}) copy-start(f32[4,16]{1,0:T(4,128)} %param.9) | copy-start | bytes 772
  1.5 22.9 %copy-start = (f32[4,16,32,256]{3,2,1,0:T(8,128)S(1)}, f32[4,16,32,256]{3,2,1,0:T(8,128)}, u32[]{:S(2)}) copy-start(f32[4,16,32,256]{3,2,1,0:T(8,128)} %orb_ref.3) | copy-start | bytes 6291460
  1.5 22.9 %copy-start.1 = (f32[16,32,256]{2,1,0:T(8,128)S(1)}, f32[16,32,256]{2,1,0:T(8,128)}, u32[]{:S(2)}) copy-start(f32[16,32,256]{2,1,0:T(8,128)} %pot_ref.3) | copy-start | bytes 1572868
  3.9 42.4 %collective-permute-start = (f32[18,32,256]{2,1,0:T(8,128)}, f32[18,32,256]{2,1,0:T(8,128)S(1)}, u32[]{:S(2)}, u32[]{:S(2)}) collective-permute-start(f32[18,32,256]{2,1,0:T(8,128)} %pad_maximum_fusion), channel_id=1, source_target_pairs={{0,8},{8,16},{16,24},{24,32},{32,40},{40,48},{48,56},{56,64},{64,7... | collective-permute-start | bytes 1769480 | tf_op jit(solution)/shard_map/ppermute | solution.py:191
  8.8 37.8 %collective-permute-start.1 = (f32[18,32,256]{2,1,0:T(8,128)}, f32[18,32,256]{2,1,0:T(8,128)}, u32[]{:S(2)}, u32[]{:S(2)}) collective-permute-start(f32[18,32,256]{2,1,0:T(8,128)} %pad_maximum_fusion.1), channel_id=1, source_target_pairs={{8,0},{16,8},{24,16},{32,24},{40,32},{48,40},{56,48},{64,56},{72,6... | collective-permute-start | bytes 1769480 | tf_op jit(solution)/shard_map/ppermute | solution.py:192
  30.8 1.2 %copy-start.2 = (f32[4,12,32,256]{3,2,1,0:T(8,128)}, f32[4,12,32,256]{3,2,1,0:T(8,128)S(1)}, u32[]{:S(2)}) copy-start(f32[4,12,32,256]{3,2,1,0:T(8,128)S(1)} %get-tuple-element.14.stored_ref) | copy-start | bytes 4718596
  32.0 50.3 %all-to-all-start = ((f32[8,264,128]{2,1,0:T(8,128)}), f32[8,264,128]{2,1,0:T(8,128)}, u32[]{:S(2)}, u32[]{:S(2)}) async-start(f32[8,264,128]{2,1,0:T(8,128)} %get-tuple-element.17), calls=%async_computation | async-start | bytes 2162688 | tf_op jit(solution)/shard_map/all_to_all | solution.py:229
  46.6 1.4 %copy-start.3 = (f32[4,12,32,256]{3,2,1,0:T(8,128)S(1)}, f32[4,12,32,256]{3,2,1,0:T(8,128)}, u32[]{:S(2)}) copy-start(f32[4,12,32,256]{3,2,1,0:T(8,128)} %copy-done.2) | copy-start | bytes 4718596
  54.1 18.7 %collective-permute-start.2 = (f32[256,128]{1,0:T(8,128)S(1)}, f32[256,128]{1,0:T(8,128)S(1)}, u32[]{:S(2)}, u32[]{:S(2)}) collective-permute-start(f32[256,128]{1,0:T(8,128)S(1)} %get-tuple-element.18), channel_id=1, source_target_pairs={{0,1},{1,0},{2,3},{3,2},{4,5},{5,4},{6,7},{7,6},{8,9},{9,8},{10,11... | collective-permute-start | bytes 393224 | tf_op jit(solution)/shard_map/ppermute | solution.py:200
  59.5 15.2 %collective-permute-start.3 = (f32[256,128]{1,0:T(8,128)S(1)}, f32[256,128]{1,0:T(8,128)S(1)}, u32[]{:S(2)}, u32[]{:S(2)}) collective-permute-start(f32[256,128]{1,0:T(8,128)S(1)} %get-tuple-element.19), channel_id=1, source_target_pairs={{0,2},{1,3},{2,0},{3,1},{4,6},{5,7},{6,4},{7,5},{8,10},{9,11},{10,... | collective-permute-start | bytes 393224 | tf_op jit(solution)/shard_map/ppermute | solution.py:200
  61.4 24.9 %collective-permute-start.4 = (f32[256,128]{1,0:T(8,128)}, f32[256,128]{1,0:T(8,128)S(1)}, u32[]{:S(2)}, u32[]{:S(2)}) collective-permute-start(f32[256,128]{1,0:T(8,128)} %get-tuple-element.20), channel_id=1, source_target_pairs={{0,4},{1,5},{2,6},{3,7},{4,0},{5,1},{6,2},{7,3},{8,12},{9,13},{10,... | collective-permute-start | bytes 393224 | tf_op jit(solution)/shard_map/ppermute | solution.py:200
  65.9 22.1 %collective-permute-start.5 = (f32[256,128]{1,0:T(8,128)}, f32[256,128]{1,0:T(8,128)S(1)}, u32[]{:S(2)}, u32[]{:S(2)}) collective-permute-start(f32[256,128]{1,0:T(8,128)} %get-tuple-element.21), channel_id=1, source_target_pairs={{0,5},{1,4},{2,7},{3,6},{4,1},{5,0},{6,3},{7,2},{8,13},{9,12},{10,... | collective-permute-start | bytes 393224 | tf_op jit(solution)/shard_map/ppermute | solution.py:200
  67.9 26.6 %collective-permute-start.6 = (f32[256,128]{1,0:T(8,128)}, f32[256,128]{1,0:T(8,128)S(1)}, u32[]{:S(2)}, u32[]{:S(2)}) collective-permute-start(f32[256,128]{1,0:T(8,128)} %get-tuple-element.22), channel_id=1, source_target_pairs={{0,6},{1,7},{2,4},{3,5},{4,2},{5,3},{6,0},{7,1},{8,14},{9,15},{10,... | collective-permute-start | bytes 393224 | tf_op jit(solution)/shard_map/ppermute | solution.py:200
  72.8 24.5 %collective-permute-start.7 = (f32[256,128]{1,0:T(8,128)}, f32[256,128]{1,0:T(8,128)S(1)}, u32[]{:S(2)}, u32[]{:S(2)}) collective-permute-start(f32[256,128]{1,0:T(8,128)} %get-tuple-element.23), channel_id=1, source_target_pairs={{0,7},{1,6},{2,5},{3,4},{4,3},{5,2},{6,1},{7,0},{8,15},{9,14},{10,... | collective-permute-start | bytes 393224 | tf_op jit(solution)/shard_map/ppermute | solution.py:200
  74.7 22.6 %collective-permute-start.8 = (f32[256,128]{1,0:T(8,128)S(1)}, f32[256,128]{1,0:T(8,128)S(1)}, u32[]{:S(2)}, u32[]{:S(2)}) collective-permute-start(f32[256,128]{1,0:T(8,128)S(1)} %get-tuple-element.24), channel_id=1, source_target_pairs={{0,3},{1,2},{2,1},{3,0},{4,7},{5,6},{6,5},{7,4},{8,11},{9,10},{10,... | collective-permute-start | bytes 393224 | tf_op jit(solution)/shard_map/ppermute | solution.py:200

commit v4 on v3

--- a/solution.py
+++ b/solution.py
@@ -10,6 +10,8 @@
 ORBS, PLANES, ROWS, COLS = 4, 16, 32, 256
 REACH = 4
 PEERS, NCOL = 8, 16
+RUN = 8
+DIRECT = 2
 LIMIT = 20 * 1024 * 1024
 ORDER = (1, 2, 4, 5, 6, 7, 3, 0)
 
@@ -65,14 +67,14 @@
     orbital = pl.program_id(0)
 
     def store(p, value):
-        first_ref[orbital, p] = value
-
-    first_planes(12, lambda p: orb_ref[orbital, p], lambda p: pot_ref[p + 2], store, coef)
+        first_ref[0, p] = value
+
+    first_planes(12, lambda p: orb_ref[0, p], lambda p: pot_ref[p + 2], store, coef)
     for t in range(4):
         pair = []
         for q in (2 * t, 2 * t + 1):
             g = filtered_plane(
-                q, lambda p: first_ref[orbital, p], orb_ref[orbital, q + 4], pot_ref[q + 4], coef
+                q, lambda p: first_ref[0, p], orb_ref[0, q + 4], pot_ref[q + 4], coef
             )
             out_ref[0, q + 4] = g
             pair.append(g)
@@ -83,12 +85,33 @@
 
 
 def outer_kernel(
-    mine_ref, lower_ref, upper_ref, orb_ref, pot_ref, stored_ref, low_ref, high_ref, _, *rest
+    mine_ref, position_ref, lower_ref, upper_ref, orb_ref, pot_ref, stored_ref, low_ref, high_ref,
+    far_direct_ref, far_relayed_ref, _, *rest,
 ):
-    out_ref, sends, (fresh_ref, slots_ref) = rest[0], rest[1:-2], rest[-2:]
+    out_ref, sends, (halo_ref, halo_pot_ref, fresh_ref, slots_ref) = rest[0], rest[1:-4], rest[-4:]
     coef = coefficients(lower_ref, upper_ref)
-    mine, i, side = mine_ref[0], pl.program_id(0), pl.program_id(1)
-    halo = REACH * i
+    mine, position = mine_ref[0], position_ref[0]
+    i, side = pl.program_id(0), pl.program_id(1)
+    far = ((side == 0) & (position == 0)) | ((side == 1) & (position == RUN - 1))
+    at = REACH * i + jnp.where(i < DIRECT, 0, 2)
+
+    def take(condition, ref, start):
+        @pl.when(condition)
+        def _():
+            halo_ref[...] = ref[pl.ds(start, REACH)]
+
+    def take_pot(condition, ref, start):
+        @pl.when(condition)
+        def _():
+            halo_pot_ref[...] = ref[start : start + 2]
+
+    take(~far & (side == 0), low_ref, at)
+    take(~far & (side == 1), high_ref, at)
+    take(far & (i < DIRECT), far_direct_ref, jnp.minimum(at, REACH * (DIRECT - 1)))
+    take(far & (i >= DIRECT), far_relayed_ref, jnp.maximum(at - REACH * DIRECT, 0))
+    take_pot(~far & (side == 0), low_ref, REACH * DIRECT)
+    take_pot(~far & (side == 1), high_ref, REACH * DIRECT)
+    take_pot(far, far_relayed_ref, 0)
 
     def filter_side(raw, local, first, original, own_local):
         for p in range(4):
@@ -104,20 +127,20 @@
     @pl.when(side == 0)
     def _():
         filter_side(
-            lambda p: low_ref[halo + p] if p < 4 else orb_ref[i, p - 4],
-            lambda p: low_ref[ORBS * REACH + p] if p < 2 else pot_ref[p - 2],
-            lambda p: fresh_ref[p] if p < 4 else stored_ref[i, p - 4],
-            lambda q: orb_ref[i, q],
+            lambda p: halo_ref[p] if p < 4 else orb_ref[0, p - 4],
+            lambda p: halo_pot_ref[p] if p < 2 else pot_ref[p - 2],
+            lambda p: fresh_ref[p] if p < 4 else stored_ref[0, p - 4],
+            lambda q: orb_ref[0, q],
             lambda q: pot_ref[q],
         )
 
     @pl.when(side == 1)
     def _():
         filter_side(
-            lambda p: orb_ref[i, 12 + p] if p < 4 else high_ref[halo + p - 4],
-            lambda p: pot_ref[14 + p] if p < 2 else high_ref[ORBS * REACH + p - 2],
-            lambda p: stored_ref[i, 8 + p] if p < 4 else fresh_ref[p - 4],
-            lambda q: orb_ref[i, 12 + q],
+            lambda p: orb_ref[0, p] if p < 4 else halo_ref[p - 4],
+            lambda p: pot_ref[14 + p] if p < 2 else halo_pot_ref[p - 2],
+            lambda p: stored_ref[0, p] if p < 4 else fresh_ref[p - 4],
+            lambda q: orb_ref[0, q],
             lambda q: pot_ref[12 + q],
         )
 
@@ -180,17 +203,34 @@
 
 def body(orbitals, potential, lower_cut, upper_bound, rotation):
     count = lax.axis_size("grid")
-    forward = [(i, (i + 1) % count) for i in range(count)]
-    backward = [(target, source) for source, target in forward]
     plane = (ROWS, COLS)
+    position = lax.axis_index("grid").astype(jnp.int32) % RUN
+    ring = [(g, (g + 1) % count) for g in range(count)]
+    near = [(g, h) for g, h in ring if g % RUN != RUN - 1]
+    ends = [(g, h) for g, h in ring if g % RUN == RUN - 1]
+    inwards = [(g, g - 1) for g, _ in ends] + [(h, h + 1) for _, h in ends]
+    across = [(g - 1, h) for g, h in ends] + [(h + 1, g) for g, h in ends]
+
+    def swapped(pairs):
+        return [(target, source) for source, target in pairs]
 
     def packed(first_plane, first_local):
         own = orbitals[:, first_plane : first_plane + REACH].reshape((ORBS * REACH,) + plane)
-        return jnp.concatenate([own, potential[first_local : first_local + 2]], axis=0)
-
-    low = lax.ppermute(packed(PLANES - REACH, PLANES - 2), "grid", forward)
-    high = lax.ppermute(packed(0, 0), "grid", backward)
-
+        local = potential[first_local : first_local + 2]
+        half = REACH * DIRECT
+        return jnp.concatenate([own[:half], local, own[half:]], axis=0)
+
+    top, bottom = packed(PLANES - REACH, PLANES - 2), packed(0, 0)
+    to_far = jnp.where(position == RUN - 1, top, bottom)
+    direct = REACH * DIRECT
+    relay = lax.ppermute(to_far[direct:], "grid", inwards)
+    far_relayed = lax.ppermute(relay, "grid", across)
+    far_direct = lax.ppermute(to_far[:direct], "grid", ends + swapped(ends))
+    low = lax.ppermute(top, "grid", near)
+    high = lax.ppermute(bottom, "grid", swapped(near))
+
+    orb_hbm = pltpu.with_memory_space_constraint(orbitals, pltpu.HBM)
+    pot_hbm = pltpu.with_memory_space_constraint(potential, pltpu.HBM)
     rot_tile = jnp.pad(rotation.reshape(1, ORBS * NCOL), ((0, 7), (0, 128 - ORBS * NCOL)))
     mine = lax.axis_index("orb").astype(jnp.int32).reshape(1)
     filtered_shape = pltpu.HBM((ORBS, PLANES) + plane, F32)
@@ -207,42 +247,55 @@
         in_specs=[
             SMEM,
             SMEM,
-            VMEM,
-            VMEM,
-            VMEM,
+            pl.BlockSpec((1, PLANES) + plane, lambda i: (i, 0, 0, 0)),
+            pl.BlockSpec((PLANES,) + plane, lambda i: (0, 0, 0)),
+            pl.BlockSpec((8, 128), lambda i: (0, 0)),
         ],
         out_specs=[
             pl.BlockSpec((1, PLANES) + plane, lambda i: (i, 0, 0, 0)),
-            VMEM,
+            pl.BlockSpec((1, 12) + plane, lambda i: (i, 0, 0, 0)),
             pl.BlockSpec((PEERS, 264, 128), lambda i: (0, 0, 0)),
         ],
         out_shape=[
             filtered_shape,
-            jax.ShapeDtypeStruct((ORBS, 12) + plane, F32),
+            pltpu.HBM((ORBS, 12) + plane, F32),
             pltpu.HBM((PEERS, 264, 128), F32),
         ],
         scratch_shapes=[pltpu.VMEM((PEERS, 64, 128), F32)],
         compiler_params=params(),
         cost_estimate=cost(1_000_000, 1_000_000),
         name="filter_inner",
-    )(lower_cut, upper_bound, orbitals, potential, rot_tile)
+    )(lower_cut, upper_bound, orb_hbm, pot_hbm, rot_tile)
     received = lax.all_to_all(send, "orb", split_axis=0, concat_axis=0, tiled=True)
+    stored = pltpu.with_memory_space_constraint(stored, pltpu.HBM)
 
     filtered, *sends_outer = pl.pallas_call(
         outer_kernel,
         grid=(ORBS, 2),
-        in_specs=[SMEM] * 3 + [VMEM] * 5 + [ANY],
+        in_specs=[SMEM] * 4
+        + [
+            pl.BlockSpec((1, 4) + plane, lambda i, s: (i, 3 * s, 0, 0)),
+            pl.BlockSpec((PLANES,) + plane, lambda i, s: (0, 0, 0)),
+            pl.BlockSpec((1, 4) + plane, lambda i, s: (i, 2 * s, 0, 0)),
+        ]
+        + [VMEM] * 4
+        + [ANY],
         out_specs=[pl.BlockSpec((1, 4) + plane, lambda i, s: (i, 3 * s, 0, 0))] + [VMEM] * PEERS,
         out_shape=[filtered_shape] + [jax.ShapeDtypeStruct((256, 128), F32)] * PEERS,
         scratch_shapes=[
             pltpu.VMEM((4,) + plane, F32),
+            pltpu.VMEM((2,) + plane, F32),
+            pltpu.VMEM((4,) + plane, F32),
             pltpu.VMEM((PEERS, 32, 128), F32),
         ],
-        input_output_aliases={8: 0},
+        input_output_aliases={11: 0},
         compiler_params=params(),
         cost_estimate=cost(400_000_000_000, 400_000_000),
         name="filter_outer",
-    )(mine, lower_cut, upper_bound, orbitals, potential, stored, low, high, filtered)
+    )(
+        mine, position.reshape(1), lower_cut, upper_bound, orb_hbm, pot_hbm, stored,
+        low, high, far_direct, far_relayed, filtered,
+    )
     received_outer = regroup(sends_outer)
 
     weights = received[:, 256, : ORBS * NCOL]

time: 101 us -> 99.4 us (0.984)
  the two profiles are of different devices: /device:TPU:17 before, /device:TPU:9 now
where the time goes in v4:
time: 99.4 us; the launch traced here: 98.6 us
  starting transfers between devices  53.1 us (53%)
  Pallas kernels  21 us (21%)
  waiting for transfers between devices  18.3 us (18%)
  local copies, waits for them, and re-layouts  3.05 us (3%)
  between operations  2.11 us (2%)
    ppermute x7, starting transfers between devices, regroup(): lax.ppermute(sends[k], 'orb', [(o, o ^ k) for o in range(PEERS)])  21.7 us
    ppermute x1, starting transfers between devices, body(): far_direct = lax.ppermute(to_far[:direct], 'grid', ends + swapped(ends))  15.4 us
    ppermute x7, waiting for transfers between devices, regroup(): lax.ppermute(sends[k], 'orb', [(o, o ^ k) for o in range(PEERS)])  8.99 us
    all_to_all x1, starting transfers between devices, body(): lax.all_to_all(send, 'orb', split_axis=0, concat_axis=0, tiled=True)  8.09 us
    pallas_call x1, Pallas kernels, body(): pl.pallas_call(outer_kernel, grid=(ORBS, 2), in_specs=[SMEM] * 4 + [pl.Bl...  7.61 us
    pallas_call x1, Pallas kernels, body(): pl.pallas_call(inner_kernel, grid=(ORBS,), in_specs=[SMEM, SMEM, pl.Block...  7.52 us
    all_to_all x1, waiting for transfers between devices, body(): lax.all_to_all(send, 'orb', split_axis=0, concat_axis=0, tiled=True)  5.61 us
    ppermute x1, starting transfers between devices, body(): relay = lax.ppermute(to_far[direct:], 'grid', inwards)  4.02 us
  transfers between devices with their start and end apart: 13, of which 5 were waited for; matrix products, arithmetic and copies ran while one was open for 1% of the time, Pallas kernels for 19%

profile of v4, /device:TPU:9, one launch (start us, length us, event | category | flops | bytes accessed | tf_op | source)
XLA Modules:
  0.0 98.6 jit_solution(9561825166841908922)
XLA Ops:
  0.6 0.9 fusion.1
  1.5 1.3 %fusion = (f32[2,4,32,256]{3,2,1,0:T(8,128)S(1)}, f32[2,4,32,256]{3,2,1,0:T(8,128)S(1)}, f32[2,4,32,256]{3,2,1,0:T(8,128)S(1)}, f32[2,4,32,256]{3,2,1,0:T(8,128)S(1)}) fusion(f32[4,16,32,256]{3,2,1,0:T(8,128)} %orb_ref.3), kind=kLoop, calls=%fused_computation.3 | loop fusion | bytes 2097152 | tf_op jit(solution)/shard_map/slice | solution.py:221
  2.8 0.0 copy-start
  2.8 1.0 broadcast_select_fusion
  3.8 4.0 %collective-permute-start.3 = (f32[10,32,256]{2,1,0:T(8,128)S(1)}, f32[10,32,256]{2,1,0:T(8,128)S(1)}, u32[]{:S(2)}, u32[]{:S(2)}) collective-permute-start(f32[10,32,256]{2,1,0:T(8,128)S(1)} %slice.59), channel_id=1, source_target_pairs={{56,48},{120,112},{184,176},{248,240},{312,304},{376,368},{440,432... | collective-permute-start | bytes 983048 | tf_op jit(solution)/shard_map/ppermute | solution.py:226
  7.8 1.3 %collective-permute-start = (f32[18,32,256]{2,1,0:T(8,128)}, f32[18,32,256]{2,1,0:T(8,128)S(1)}, u32[]{:S(2)}, u32[]{:S(2)}) collective-permute-start(f32[18,32,256]{2,1,0:T(8,128)} %get-tuple-element.31), channel_id=1, source_target_pairs={{0,8},{8,16},{16,24},{24,32},{32,40},{40,48},{48,56},{64,72},{72,8... | collective-permute-start | bytes 1769480 | tf_op jit(solution)/shard_map/ppermute | solution.py:229
  9.2 1.3 %collective-permute-start.1 = (f32[18,32,256]{2,1,0:T(8,128)S(1)}, f32[18,32,256]{2,1,0:T(8,128)S(1)}, u32[]{:S(2)}, u32[]{:S(2)}) collective-permute-start(f32[18,32,256]{2,1,0:T(8,128)S(1)} %get-tuple-element.32), channel_id=1, source_target_pairs={{8,0},{16,8},{24,16},{32,24},{40,32},{48,40},{56,48},{72,64},{80,7... | collective-permute-start | bytes 1769480 | tf_op jit(solution)/shard_map/ppermute | solution.py:230
  10.5 3.7 %collective-permute-done.3 = f32[10,32,256]{2,1,0:T(8,128)S(1)} collective-permute-done((f32[10,32,256]{2,1,0:T(8,128)S(1)}, f32[10,32,256]{2,1,0:T(8,128)S(1)}, u32[]{:S(2)}, u32[]{:S(2)}) %collective-permute-start.3) | collective-permute-done | bytes 327712 | tf_op jit(solution)/shard_map/ppermute | solution.py:226
  14.2 1.3 %collective-permute-start.4 = (f32[10,32,256]{2,1,0:T(8,128)S(1)}, f32[10,32,256]{2,1,0:T(8,128)S(1)}, u32[]{:S(2)}, u32[]{:S(2)}) collective-permute-start(f32[10,32,256]{2,1,0:T(8,128)S(1)} %collective-permute-done.3), channel_id=1, source_target_pairs={{48,64},{112,128},{176,192},{240,256},{304,320},{368,384},{432,448... | collective-permute-start | bytes 983048 | tf_op jit(solution)/shard_map/ppermute | solution.py:227
  15.5 15.4 %collective-permute-start.2 = (f32[8,32,256]{2,1,0:T(8,128)S(1)}, f32[8,32,256]{2,1,0:T(8,128)S(1)}, u32[]{:S(2)}, u32[]{:S(2)}) collective-permute-start(f32[8,32,256]{2,1,0:T(8,128)S(1)} %slice.58), channel_id=1, source_target_pairs={{56,64},{120,128},{184,192},{248,256},{312,320},{376,384},{440,448... | collective-permute-start | bytes 786440 | tf_op jit(solution)/shard_map/ppermute | solution.py:228
  32.2 0.0 copy-done
  32.2 0.1 reshape.21
  32.3 7.5 %filter_inner.1 = (f32[4,16,32,256]{3,2,1,0:T(8,128)}, f32[4,12,32,256]{3,2,1,0:T(8,128)}, f32[8,264,128]{2,1,0:T(8,128)}) custom-call(f32[1]{0:T(128)S(6)} %copy.15.lower_ref, f32[1]{0:T(128)S(6)} %copy.16.upper_ref, f32[4,16,32,256]{3,2,1,0:T(8,128)} %orb_ref.3, f32[16,32,256]{2,1,0:T(8,128)} %pot_ref.3, f32[8,128]{1,0:T(8,128)S(1)} %pad.4.rot_ref), custom_call_target="tpu_custom_call" | custom-call | flops 1000000 | bytes 1000000 | tf_op jit(solution)/shard_map/filter_inner/pallas_call | solution.py:244
  39.8 8.1 %all-to-all-start = ((f32[8,264,128]{2,1,0:T(8,128)}), f32[8,264,128]{2,1,0:T(8,128)}, u32[]{:S(2)}, u32[]{:S(2)}) async-start(f32[8,264,128]{2,1,0:T(8,128)} %get-tuple-element.17), calls=%async_computation | async-start | bytes 2162688 | tf_op jit(solution)/shard_map/all_to_all | solution.py:269
  47.9 0.0 collective-permute-done.2.far_direct_ref
  47.9 0.0 collective-permute-done.low_ref
  47.9 0.0 collective-permute-done.1.high_ref
  47.9 0.0 collective-permute-done.4.far_relayed_ref
  48.0 7.6 %filter_outer.1 = (f32[4,16,32,256]{3,2,1,0:T(8,128)}, f32[256,128]{1,0:T(8,128)S(1)}, f32[256,128]{1,0:T(8,128)S(1)}, f32[256,128]{1,0:T(8,128)S(1)}, f32[256,1...) custom-call(s32[1]{0:T(128)} %bitcast.mine_ref, ...), custom_call_target="tpu_custom_call", output_to_operand_aliasing={{0}: (11, {})} | custom-call | flops 399999991808 | bytes 400000000 | tf_op jit(solution)/shard_map/filter_outer/pallas_call | solution.py:272
  55.6 2.3 %collective-permute-start.5 = (f32[256,128]{1,0:T(8,128)S(1)}, f32[256,128]{1,0:T(8,128)S(1)}, u32[]{:S(2)}, u32[]{:S(2)}) collective-permute-start(f32[256,128]{1,0:T(8,128)S(1)} %get-tuple-element.18), channel_id=1, source_target_pairs={{0,1},{1,0},{2,3},{3,2},{4,5},{5,4},{6,7},{7,6},{8,9},{9,8},{10,11... | collective-permute-start | bytes 393224 | tf_op jit(solution)/shard_map/ppermute | solution.py:240
  57.8 1.9 %collective-permute-start.6 = (f32[256,128]{1,0:T(8,128)S(1)}, f32[256,128]{1,0:T(8,128)S(1)}, u32[]{:S(2)}, u32[]{:S(2)}) collective-permute-start(f32[256,128]{1,0:T(8,128)S(1)} %get-tuple-element.19), channel_id=1, source_target_pairs={{0,2},{1,3},{2,0},{3,1},{4,6},{5,7},{6,4},{7,5},{8,10},{9,11},{10,... | collective-permute-start | bytes 393224 | tf_op jit(solution)/shard_map/ppermute | solution.py:240
  59.8 4.3 %collective-permute-start.7 = (f32[256,128]{1,0:T(8,128)S(1)}, f32[256,128]{1,0:T(8,128)S(1)}, u32[]{:S(2)}, u32[]{:S(2)}) collective-permute-start(f32[256,128]{1,0:T(8,128)S(1)} %get-tuple-element.20), channel_id=1, source_target_pairs={{0,4},{1,5},{2,6},{3,7},{4,0},{5,1},{6,2},{7,3},{8,12},{9,13},{10,... | collective-permute-start | bytes 393224 | tf_op jit(solution)/shard_map/ppermute | solution.py:240
  64.0 2.6 %collective-permute-start.8 = (f32[256,128]{1,0:T(8,128)S(1)}, f32[256,128]{1,0:T(8,128)S(1)}, u32[]{:S(2)}, u32[]{:S(2)}) collective-permute-start(f32[256,128]{1,0:T(8,128)S(1)} %get-tuple-element.21), channel_id=1, source_target_pairs={{0,5},{1,4},{2,7},{3,6},{4,1},{5,0},{6,3},{7,2},{8,13},{9,12},{10,... | collective-permute-start | bytes 393224 | tf_op jit(solution)/shard_map/ppermute | solution.py:240
  66.6 4.2 %collective-permute-start.9 = (f32[256,128]{1,0:T(8,128)S(1)}, f32[256,128]{1,0:T(8,128)S(1)}, u32[]{:S(2)}, u32[]{:S(2)}) collective-permute-start(f32[256,128]{1,0:T(8,128)S(1)} %get-tuple-element.22), channel_id=1, source_target_pairs={{0,6},{1,7},{2,4},{3,5},{4,2},{5,3},{6,0},{7,1},{8,14},{9,15},{10,... | collective-permute-start | bytes 393224 | tf_op jit(solution)/shard_map/ppermute | solution.py:240
  70.9 0.0 collective-permute-done.5.rest_0_
  70.9 1.9 %collective-permute-start.10 = (f32[256,128]{1,0:T(8,128)S(1)}, f32[256,128]{1,0:T(8,128)S(1)}, u32[]{:S(2)}, u32[]{:S(2)}) collective-permute-start(f32[256,128]{1,0:T(8,128)S(1)} %get-tuple-element.23), channel_id=1, source_target_pairs={{0,7},{1,6},{2,5},{3,4},{4,3},{5,2},{6,1},{7,0},{8,15},{9,14},{10,... | collective-permute-start | bytes 393224 | tf_op jit(solution)/shard_map/ppermute | solution.py:240
  72.8 0.0 collective-permute-done.6.rest_1_
  72.8 4.5 %collective-permute-start.11 = (f32[256,128]{1,0:T(8,128)S(1)}, f32[256,128]{1,0:T(8,128)S(1)}, u32[]{:S(2)}, u32[]{:S(2)}) collective-permute-start(f32[256,128]{1,0:T(8,128)S(1)} %get-tuple-element.24), channel_id=1, source_target_pairs={{0,3},{1,2},{2,1},{3,0},{4,7},{5,6},{6,5},{7,4},{8,11},{9,10},{10,... | collective-permute-start | bytes 393224 | tf_op jit(solution)/shard_map/ppermute | solution.py:240
  77.3 5.6 %all-to-all-done.recv_ref = f32[8,264,128]{2,1,0:T(8,128)} async-done(((f32[8,264,128]{2,1,0:T(8,128)}), f32[8,264,128]{2,1,0:T(8,128)}, u32[]{:S(2)}, u32[]{:S(2)}) %all-to-all-start) | async-done | bytes 1081376 | tf_op jit(solution)/shard_map/all_to_all | solution.py:269
  82.9 0.8 slice.60
  83.7 3.3 %rotate_inner.1.rest_8_ = f32[16,16,4,256]{3,2,1,0:T(4,128)} custom-call(f32[8,64]{1,0:T(8,128)S(1)} %bitcast.9, f32[8,264,128]{2,1,0:T(8,128)} %all-to-all-done.recv_ref), custom_call_target="tpu_custom_call" | custom-call | flops 8000000 | bytes 1600000 | tf_op jit(solution)/shard_map/rotate_inner/pallas_call | solution.py:303
  87.0 0.0 collective-permute-done.7.rest_2_
  87.0 1.5 %collective-permute-done.8.rest_3_ = f32[256,128]{1,0:T(8,128)S(1)} collective-permute-done((f32[256,128]{1,0:T(8,128)S(1)}, f32[256,128]{1,0:T(8,128)S(1)}, u32[]{:S(2)}, u32[]{:S(2)}) %collective-permute-start.8) | collective-permute-done | bytes 131104 | tf_op jit(solution)/shard_map/ppermute | solution.py:240
  88.4 4.5 %collective-permute-done.9.rest_4_ = f32[256,128]{1,0:T(8,128)S(1)} collective-permute-done((f32[256,128]{1,0:T(8,128)S(1)}, f32[256,128]{1,0:T(8,128)S(1)}, u32[]{:S(2)}, u32[]{:S(2)}) %collective-permute-start.9) | collective-permute-done | bytes 131104 | tf_op jit(solution)/shard_map/ppermute | solution.py:240
  93.0 3.0 %collective-permute-done.10.rest_5_ = f32[256,128]{1,0:T(8,128)S(1)} collective-permute-done((f32[256,128]{1,0:T(8,128)S(1)}, f32[256,128]{1,0:T(8,128)S(1)}, u32[]{:S(2)}, u32[]{:S(2)}) %collective-permute-start.10) | collective-permute-done | bytes 131104 | tf_op jit(solution)/shard_map/ppermute | solution.py:240
  96.0 0.0 collective-permute-done.11.rest_6_
  96.0 2.6 %rotate_outer.1 = f32[16,16,4,256]{3,2,1,0:T(4,128)} custom-call(s32[1]{0:T(128)} %bitcast.mine_ref, f32[8,64]{1,0:T(8,128)S(1)} %bitcast.10, f32[256,128]{1,0:T(8,128)S(1)} %collective-permute-done.5.rest_0_, f32[256,128]{1,0:T(8,128)S(1)} %collective-permute-done.6.rest_1_, ...), custom_call_target="tpu_custom_call", output_to_operand_aliasing={{}: (10, {})} | custom-call | flops 8000000 | bytes 1600000 | tf_op jit(solution)/shard_map/rotate_outer/pallas_call | solution.py:313
  (3 shorter events, 0.0 us)
Async XLA Ops:
  2.8 29.4 %copy-start = (f32[4,16]{1,0:T(4,128)S(1)}, f32[4,16]{1,0:T(4,128)}, u32[]{:S(2)}) copy-start(f32[4,16]{1,0:T(4,128)} %param.9) | copy-start | bytes 772
  3.8 10.4 %collective-permute-start.3 = (f32[10,32,256]{2,1,0:T(8,128)S(1)}, f32[10,32,256]{2,1,0:T(8,128)S(1)}, u32[]{:S(2)}, u32[]{:S(2)}) collective-permute-start(f32[10,32,256]{2,1,0:T(8,128)S(1)} %slice.59), channel_id=1, source_target_pairs={{56,48},{120,112},{184,176},{248,240},{312,304},{376,368},{440,432... | collective-permute-start | bytes 983048 | tf_op jit(solution)/shard_map/ppermute | solution.py:226
  7.8 40.1 %collective-permute-start = (f32[18,32,256]{2,1,0:T(8,128)}, f32[18,32,256]{2,1,0:T(8,128)S(1)}, u32[]{:S(2)}, u32[]{:S(2)}) collective-permute-start(f32[18,32,256]{2,1,0:T(8,128)} %get-tuple-element.31), channel_id=1, source_target_pairs={{0,8},{8,16},{16,24},{24,32},{32,40},{40,48},{48,56},{64,72},{72,8... | collective-permute-start | bytes 1769480 | tf_op jit(solution)/shard_map/ppermute | solution.py:229
  9.2 38.8 %collective-permute-start.1 = (f32[18,32,256]{2,1,0:T(8,128)S(1)}, f32[18,32,256]{2,1,0:T(8,128)S(1)}, u32[]{:S(2)}, u32[]{:S(2)}) collective-permute-start(f32[18,32,256]{2,1,0:T(8,128)S(1)} %get-tuple-element.32), channel_id=1, source_target_pairs={{8,0},{16,8},{24,16},{32,24},{40,32},{48,40},{56,48},{72,64},{80,7... | collective-permute-start | bytes 1769480 | tf_op jit(solution)/shard_map/ppermute | solution.py:230
  14.2 33.8 %collective-permute-start.4 = (f32[10,32,256]{2,1,0:T(8,128)S(1)}, f32[10,32,256]{2,1,0:T(8,128)S(1)}, u32[]{:S(2)}, u32[]{:S(2)}) collective-permute-start(f32[10,32,256]{2,1,0:T(8,128)S(1)} %collective-permute-done.3), channel_id=1, source_target_pairs={{48,64},{112,128},{176,192},{240,256},{304,320},{368,384},{432,448... | collective-permute-start | bytes 983048 | tf_op jit(solution)/shard_map/ppermute | solution.py:227
  15.5 32.4 %collective-permute-start.2 = (f32[8,32,256]{2,1,0:T(8,128)S(1)}, f32[8,32,256]{2,1,0:T(8,128)S(1)}, u32[]{:S(2)}, u32[]{:S(2)}) collective-permute-start(f32[8,32,256]{2,1,0:T(8,128)S(1)} %slice.58), channel_id=1, source_target_pairs={{56,64},{120,128},{184,192},{248,256},{312,320},{376,384},{440,448... | collective-permute-start | bytes 786440 | tf_op jit(solution)/shard_map/ppermute | solution.py:228
  39.8 43.1 %all-to-all-start = ((f32[8,264,128]{2,1,0:T(8,128)}), f32[8,264,128]{2,1,0:T(8,128)}, u32[]{:S(2)}, u32[]{:S(2)}) async-start(f32[8,264,128]{2,1,0:T(8,128)} %get-tuple-element.17), calls=%async_computation | async-start | bytes 2162688 | tf_op jit(solution)/shard_map/all_to_all | solution.py:269
  55.6 15.3 %collective-permute-start.5 = (f32[256,128]{1,0:T(8,128)S(1)}, f32[256,128]{1,0:T(8,128)S(1)}, u32[]{:S(2)}, u32[]{:S(2)}) collective-permute-start(f32[256,128]{1,0:T(8,128)S(1)} %get-tuple-element.18), channel_id=1, source_target_pairs={{0,1},{1,0},{2,3},{3,2},{4,5},{5,4},{6,7},{7,6},{8,9},{9,8},{10,11... | collective-permute-start | bytes 393224 | tf_op jit(solution)/shard_map/ppermute | solution.py:240
  57.8 15.0 %collective-permute-start.6 = (f32[256,128]{1,0:T(8,128)S(1)}, f32[256,128]{1,0:T(8,128)S(1)}, u32[]{:S(2)}, u32[]{:S(2)}) collective-permute-start(f32[256,128]{1,0:T(8,128)S(1)} %get-tuple-element.19), channel_id=1, source_target_pairs={{0,2},{1,3},{2,0},{3,1},{4,6},{5,7},{6,4},{7,5},{8,10},{9,11},{10,... | collective-permute-start | bytes 393224 | tf_op jit(solution)/shard_map/ppermute | solution.py:240
  59.8 27.2 %collective-permute-start.7 = (f32[256,128]{1,0:T(8,128)S(1)}, f32[256,128]{1,0:T(8,128)S(1)}, u32[]{:S(2)}, u32[]{:S(2)}) collective-permute-start(f32[256,128]{1,0:T(8,128)S(1)} %get-tuple-element.20), channel_id=1, source_target_pairs={{0,4},{1,5},{2,6},{3,7},{4,0},{5,1},{6,2},{7,3},{8,12},{9,13},{10,... | collective-permute-start | bytes 393224 | tf_op jit(solution)/shard_map/ppermute | solution.py:240
  64.0 24.4 %collective-permute-start.8 = (f32[256,128]{1,0:T(8,128)S(1)}, f32[256,128]{1,0:T(8,128)S(1)}, u32[]{:S(2)}, u32[]{:S(2)}) collective-permute-start(f32[256,128]{1,0:T(8,128)S(1)} %get-tuple-element.21), channel_id=1, source_target_pairs={{0,5},{1,4},{2,7},{3,6},{4,1},{5,0},{6,3},{7,2},{8,13},{9,12},{10,... | collective-permute-start | bytes 393224 | tf_op jit(solution)/shard_map/ppermute | solution.py:240
  66.6 26.4 %collective-permute-start.9 = (f32[256,128]{1,0:T(8,128)S(1)}, f32[256,128]{1,0:T(8,128)S(1)}, u32[]{:S(2)}, u32[]{:S(2)}) collective-permute-start(f32[256,128]{1,0:T(8,128)S(1)} %get-tuple-element.22), channel_id=1, source_target_pairs={{0,6},{1,7},{2,4},{3,5},{4,2},{5,3},{6,0},{7,1},{8,14},{9,15},{10,... | collective-permute-start | bytes 393224 | tf_op jit(solution)/shard_map/ppermute | solution.py:240
  70.9 25.1 %collective-permute-start.10 = (f32[256,128]{1,0:T(8,128)S(1)}, f32[256,128]{1,0:T(8,128)S(1)}, u32[]{:S(2)}, u32[]{:S(2)}) collective-permute-start(f32[256,128]{1,0:T(8,128)S(1)} %get-tuple-element.23), channel_id=1, source_target_pairs={{0,7},{1,6},{2,5},{3,4},{4,3},{5,2},{6,1},{7,0},{8,15},{9,14},{10,... | collective-permute-start | bytes 393224 | tf_op jit(solution)/shard_map/ppermute | solution.py:240
  72.8 23.2 %collective-permute-start.11 = (f32[256,128]{1,0:T(8,128)S(1)}, f32[256,128]{1,0:T(8,128)S(1)}, u32[]{:S(2)}, u32[]{:S(2)}) collective-permute-start(f32[256,128]{1,0:T(8,128)S(1)} %get-tuple-element.24), channel_id=1, source_target_pairs={{0,3},{1,2},{2,1},{3,0},{4,7},{5,6},{6,5},{7,4},{8,11},{9,10},{10,... | collective-permute-start | bytes 393224 | tf_op jit(solution)/shard_map/ppermute | solution.py:240

commit v5 on v3

--- a/solution.py
+++ b/solution.py
@@ -11,12 +11,12 @@
 REACH = 4
 PEERS, NCOL = 8, 16
 LIMIT = 20 * 1024 * 1024
-ORDER = (1, 2, 4, 5, 6, 7, 3, 0)
-
-
-def coefficients(lower_ref, upper_ref):
-    middle = (upper_ref[0] + lower_ref[0]) * 0.5
-    inverse = 1.0 / ((upper_ref[0] - lower_ref[0]) * 0.5)
+SOON, LAST = (1, 2, 4, 5, 0), (6, 7, 3)
+
+
+def coefficients(lower, upper):
+    middle = (upper + lower) * 0.5
+    inverse = 1.0 / ((upper - lower) * 0.5)
     return (-1.5 * W0 - middle) * inverse, inverse, -0.5 * W1 * inverse
 
 
@@ -61,18 +61,18 @@
 def inner_kernel(
     lower_ref, upper_ref, orb_ref, pot_ref, rot_ref, out_ref, first_ref, send_ref, slots_ref
 ):
-    coef = coefficients(lower_ref, upper_ref)
+    coef = coefficients(lower_ref[0], upper_ref[0])
     orbital = pl.program_id(0)
 
     def store(p, value):
-        first_ref[orbital, p] = value
-
-    first_planes(12, lambda p: orb_ref[orbital, p], lambda p: pot_ref[p + 2], store, coef)
+        first_ref[0, p] = value
+
+    first_planes(12, lambda p: orb_ref[0, p], lambda p: pot_ref[p + 2], store, coef)
     for t in range(4):
         pair = []
         for q in (2 * t, 2 * t + 1):
             g = filtered_plane(
-                q, lambda p: first_ref[orbital, p], orb_ref[orbital, q + 4], pot_ref[q + 4], coef
+                q, lambda p: first_ref[0, p], orb_ref[0, q + 4], pot_ref[q + 4], coef
             )
             out_ref[0, q + 4] = g
             pair.append(g)
@@ -86,7 +86,7 @@
     mine_ref, lower_ref, upper_ref, orb_ref, pot_ref, stored_ref, low_ref, high_ref, _, *rest
 ):
     out_ref, sends, (fresh_ref, slots_ref) = rest[0], rest[1:-2], rest[-2:]
-    coef = coefficients(lower_ref, upper_ref)
+    coef = coefficients(lower_ref[0], upper_ref[0])
     mine, i, side = mine_ref[0], pl.program_id(0), pl.program_id(1)
     halo = REACH * i
 
@@ -104,20 +104,20 @@
     @pl.when(side == 0)
     def _():
         filter_side(
-            lambda p: low_ref[halo + p] if p < 4 else orb_ref[i, p - 4],
+            lambda p: low_ref[halo + p] if p < 4 else orb_ref[0, p - 4],
             lambda p: low_ref[ORBS * REACH + p] if p < 2 else pot_ref[p - 2],
-            lambda p: fresh_ref[p] if p < 4 else stored_ref[i, p - 4],
-            lambda q: orb_ref[i, q],
+            lambda p: fresh_ref[p] if p < 4 else stored_ref[0, p - 4],
+            lambda q: orb_ref[0, q],
             lambda q: pot_ref[q],
         )
 
     @pl.when(side == 1)
     def _():
         filter_side(
-            lambda p: orb_ref[i, 12 + p] if p < 4 else high_ref[halo + p - 4],
+            lambda p: orb_ref[0, p] if p < 4 else high_ref[halo + p - 4],
             lambda p: pot_ref[14 + p] if p < 2 else high_ref[ORBS * REACH + p - 2],
-            lambda p: stored_ref[i, 8 + p] if p < 4 else fresh_ref[p - 4],
-            lambda q: orb_ref[i, 12 + q],
+            lambda p: stored_ref[0, p] if p < 4 else fresh_ref[p - 4],
+            lambda q: orb_ref[0, q],
             lambda q: pot_ref[12 + q],
         )
 
@@ -126,11 +126,11 @@
         send_ref[rows, :] = slots_ref[slot]
 
 
-def rotate_tiles(u, tile, weight, out_ref):
+def rotate_tiles(u, slots, tile, weight, start, finish):
     width = 8
     for first in range(0, NCOL, width):
-        sums = [jnp.zeros((8, 128), F32)] * (4 * width)
-        for slot in range(PEERS):
+        sums = [start(first + m // 4, m % 4) for m in range(4 * width)]
+        for slot in slots:
             for i in range(ORBS):
                 rows = [pl.multiple_of(i * 64 + u * 32 + 8 * n, 8) for n in range(4)]
                 values = [tile(slot, pl.ds(row, 8)) for row in rows]
@@ -138,30 +138,60 @@
                     factor = weight(slot, i * NCOL + first + j)
                     for n in range(4):
                         sums[4 * j + n] = sums[4 * j + n] + factor * values[n]
-        for j in range(width):
-            for n in range(4):
-                t, h = divmod(n, 2)
-                columns = slice(128 * h, 128 * h + 128)
-                out_ref[first + j, 2 * t, :, columns] = sums[4 * j + n][0:4]
-                out_ref[first + j, 2 * t + 1, :, columns] = sums[4 * j + n][4:8]
+        for m in range(4 * width):
+            finish(first + m // 4, m % 4, sums[m])
+
+
+def zero_start(j, n):
+    return jnp.zeros((8, 128), F32)
+
+
+def write_to(out_ref):
+    def finish(j, n, value):
+        t, h = divmod(n, 2)
+        columns = slice(128 * h, 128 * h + 128)
+        out_ref[j, 2 * t, :, columns] = value[0:4]
+        out_ref[j, 2 * t + 1, :, columns] = value[4:8]
+
+    return finish
 
 
 def rotate_inner_kernel(rot_ref, recv_ref, out_ref):
     rotate_tiles(
         pl.program_id(0),
+        range(PEERS),
         lambda slot, rows: recv_ref[slot, rows, :],
         lambda slot, n: rot_ref[slot, n],
-        out_ref,
+        zero_start,
+        write_to(out_ref),
     )
 
 
-def rotate_outer_kernel(mine_ref, rot_ref, *rest):
-    received, out_ref, mine = rest[:PEERS], rest[-1], mine_ref[0]
+def rotate_soon_kernel(mine_ref, rot_ref, *rest):
+    received, sums_ref, mine, u = rest[:-1], rest[-1], mine_ref[0], pl.program_id(0)
+
+    def finish(j, n, value):
+        sums_ref[u, 4 * j + n] = value
+
     rotate_tiles(
-        pl.program_id(0),
+        u,
+        range(len(SOON)),
         lambda slot, rows: received[slot][rows, :],
-        lambda slot, n: rot_ref[jnp.bitwise_xor(mine, ORDER[slot]), n],
-        out_ref,
+        lambda slot, n: rot_ref[jnp.bitwise_xor(mine, SOON[slot]), n],
+        zero_start,
+        finish,
+    )
+
+
+def rotate_last_kernel(mine_ref, rot_ref, sums_ref, *rest):
+    received, out_ref, mine, u = rest[:-2], rest[-1], mine_ref[0], pl.program_id(0)
+    rotate_tiles(
+        u,
+        range(len(LAST)),
+        lambda slot, rows: received[slot][rows, :],
+        lambda slot, n: rot_ref[jnp.bitwise_xor(mine, LAST[slot]), n],
+        lambda j, n: sums_ref[u, 4 * j + n],
+        write_to(out_ref),
     )
 
 
@@ -191,6 +221,9 @@
     low = lax.ppermute(packed(PLANES - REACH, PLANES - 2), "grid", forward)
     high = lax.ppermute(packed(0, 0), "grid", backward)
 
+    orb_hbm = pltpu.with_memory_space_constraint(orbitals, pltpu.HBM)
+    pot_hbm = pltpu.with_memory_space_constraint(potential, pltpu.HBM)
+    lower, upper = lower_cut, upper_bound
     rot_tile = jnp.pad(rotation.reshape(1, ORBS * NCOL), ((0, 7), (0, 128 - ORBS * NCOL)))
     mine = lax.axis_index("orb").astype(jnp.int32).reshape(1)
     filtered_shape = pltpu.HBM((ORBS, PLANES) + plane, F32)
@@ -198,40 +231,48 @@
     def regroup(sends):
         return [
             lax.ppermute(sends[k], "orb", [(o, o ^ k) for o in range(PEERS)]) if k else sends[k]
-            for k in ORDER
+            for k in SOON + LAST
         ]
 
     filtered, stored, send = pl.pallas_call(
         inner_kernel,
         grid=(ORBS,),
         in_specs=[
-            SMEM,
-            SMEM,
             VMEM,
             VMEM,
-            VMEM,
+            pl.BlockSpec((1, PLANES) + plane, lambda i: (i, 0, 0, 0)),
+            pl.BlockSpec((PLANES,) + plane, lambda i: (0, 0, 0)),
+            pl.BlockSpec((8, 128), lambda i: (0, 0)),
         ],
         out_specs=[
             pl.BlockSpec((1, PLANES) + plane, lambda i: (i, 0, 0, 0)),
-            VMEM,
+            pl.BlockSpec((1, 12) + plane, lambda i: (i, 0, 0, 0)),
             pl.BlockSpec((PEERS, 264, 128), lambda i: (0, 0, 0)),
         ],
         out_shape=[
             filtered_shape,
-            jax.ShapeDtypeStruct((ORBS, 12) + plane, F32),
+            pltpu.HBM((ORBS, 12) + plane, F32),
             pltpu.HBM((PEERS, 264, 128), F32),
         ],
         scratch_shapes=[pltpu.VMEM((PEERS, 64, 128), F32)],
         compiler_params=params(),
         cost_estimate=cost(1_000_000, 1_000_000),
         name="filter_inner",
-    )(lower_cut, upper_bound, orbitals, potential, rot_tile)
+    )(lower, upper, orb_hbm, pot_hbm, rot_tile)
     received = lax.all_to_all(send, "orb", split_axis=0, concat_axis=0, tiled=True)
+    stored = pltpu.with_memory_space_constraint(stored, pltpu.HBM)
 
     filtered, *sends_outer = pl.pallas_call(
         outer_kernel,
         grid=(ORBS, 2),
-        in_specs=[SMEM] * 3 + [VMEM] * 5 + [ANY],
+        in_specs=[SMEM, VMEM, VMEM]
+        + [
+            pl.BlockSpec((1, 4) + plane, lambda i, s: (i, 3 * s, 0, 0)),
+            pl.BlockSpec((PLANES,) + plane, lambda i, s: (0, 0, 0)),
+            pl.BlockSpec((1, 4) + plane, lambda i, s: (i, 2 * s, 0, 0)),
+        ]
+        + [VMEM] * 2
+        + [ANY],
         out_specs=[pl.BlockSpec((1, 4) + plane, lambda i, s: (i, 3 * s, 0, 0))] + [VMEM] * PEERS,
         out_shape=[filtered_shape] + [jax.ShapeDtypeStruct((256, 128), F32)] * PEERS,
         scratch_shapes=[
@@ -242,7 +283,7 @@
         compiler_params=params(),
         cost_estimate=cost(400_000_000_000, 400_000_000),
         name="filter_outer",
-    )(mine, lower_cut, upper_bound, orbitals, potential, stored, low, high, filtered)
+    )(mine, lower, upper, orb_hbm, pot_hbm, stored, low, high, filtered)
     received_outer = regroup(sends_outer)
 
     weights = received[:, 256, : ORBS * NCOL]
@@ -257,17 +298,27 @@
         cost_estimate=cost(8_000_000, 1_600_000),
         name="rotate_inner",
     )(weights, received)
+    sums = pl.pallas_call(
+        rotate_soon_kernel,
+        grid=(2,),
+        in_specs=[SMEM, SMEM] + [VMEM] * len(SOON),
+        out_specs=VMEM,
+        out_shape=jax.ShapeDtypeStruct((2, 4 * NCOL, 8, 128), F32),
+        compiler_params=params(),
+        cost_estimate=cost(5_000_000, 1_100_000),
+        name="rotate_soon",
+    )(mine, weights, *received_outer[: len(SOON)])
     rotated = pl.pallas_call(
-        rotate_outer_kernel,
+        rotate_last_kernel,
         grid=(2,),
-        in_specs=[SMEM, SMEM] + [VMEM] * PEERS + [ANY],
+        in_specs=[SMEM, SMEM, VMEM] + [VMEM] * len(LAST) + [ANY],
         out_specs=pl.BlockSpec((NCOL, 4, 4, COLS), lambda u: (0, 3 * u, 0, 0)),
         out_shape=rotated_shape,
-        input_output_aliases={PEERS + 2: 0},
-        compiler_params=params(),
-        cost_estimate=cost(8_000_000, 1_600_000),
-        name="rotate_outer",
-    )(mine, weights, *received_outer, rotated)
+        input_output_aliases={len(LAST) + 3: 0},
+        compiler_params=params(),
+        cost_estimate=cost(3_000_000, 1_100_000),
+        name="rotate_last",
+    )(mine, weights, sums, *received_outer[len(SOON) :], rotated)
     return (filtered, rotated)
 
 

time: 101 us -> 97.9 us (0.969)
  Pallas kernels: 18.4 us -> 21.7 us
  local copies, waits for them, and re-layouts: 5.8 us -> 3.05 us
  other arithmetic: 1.76 us -> 0.08 us
    pallas_call x3 -> x4, Pallas kernels: 15.1 us -> 18.4 us  [the longest x1 7.64 us: body(): pl.pallas_call(inner_kernel, grid=(ORBS,), in_specs=[VMEM, VMEM, pl.Block...]
    unnamed x10 -> x2, local copies, waits for them, and re-layouts: 2.61 us -> 0.01 us
    concatenate x2, other arithmetic: 1.76 us -> 0.08 us  [packed(): jnp.concatenate([own, potential[first_local:first_local + 2]], axis=0)]
    ppermute x7, waiting for transfers between devices: 11 us -> 9.66 us  [regroup(): lax.ppermute(sends[k], 'orb', [(o, o ^ k) for o in range(PEERS)])]
  transfers between devices with their start and end apart: 10 -> 10, of which waited for: 6 -> 6; matrix products, arithmetic and copies ran while one was open for 2% -> 1% of each run, Pallas kernels for 16% -> 20%
where the time goes in v5:
time: 97.9 us; the launch traced here: 97.1 us
  starting transfers between devices  49.1 us (50%)
  Pallas kernels  21.7 us (22%)
  waiting for transfers between devices  21.1 us (22%)
  local copies, waits for them, and re-layouts  3.05 us (3%)
  between operations  2.07 us (2%)
    ppermute x7, starting transfers between devices, regroup(): lax.ppermute(sends[k], 'orb', [(o, o ^ k) for o in range(PEERS)])  24 us
    ppermute x1, starting transfers between devices, body(): high = lax.ppermute(packed(0, 0), 'grid', backward)  14.2 us
    ppermute x7, waiting for transfers between devices, regroup(): lax.ppermute(sends[k], 'orb', [(o, o ^ k) for o in range(PEERS)])  9.66 us
    ppermute x1, waiting for transfers between devices, body(): low = lax.ppermute(packed(PLANES - REACH, PLANES - 2), 'grid', forward)  8.08 us
    pallas_call x1, Pallas kernels, body(): pl.pallas_call(inner_kernel, grid=(ORBS,), in_specs=[VMEM, VMEM, pl.Block...  7.64 us
    pallas_call x1, Pallas kernels, body(): pl.pallas_call(outer_kernel, grid=(ORBS, 2), in_specs=[SMEM, VMEM, VMEM]...  7.55 us
    all_to_all x1, starting transfers between devices, body(): lax.all_to_all(send, 'orb', split_axis=0, concat_axis=0, tiled=True)  6.88 us
    ppermute x1, starting transfers between devices, body(): low = lax.ppermute(packed(PLANES - REACH, PLANES - 2), 'grid', forward)  4 us
  transfers between devices with their start and end apart: 10, of which 6 were waited for; matrix products, arithmetic and copies ran while one was open for 1% of the time, Pallas kernels for 20%

profile of v5, /device:TPU:17, one launch (start us, length us, event | category | flops | bytes accessed | tf_op | source)
XLA Modules:
  0.0 97.1 jit_solution(15919358714152618945)
XLA Ops:
  0.6 0.9 fusion.1
  1.5 0.0 copy-start
  1.5 1.3 %fusion = (f32[4,4,32,256]{3,2,1,0:T(8,128)S(1)}, f32[4,4,32,256]{3,2,1,0:T(8,128)S(1)}) fusion(f32[4,16,32,256]{3,2,1,0:T(8,128)} %orb_ref.3), kind=kLoop, calls=%fused_computation.2 | loop fusion | bytes 2097152 | tf_op jit(solution)/shard_map/slice | solution.py:218
  2.9 4.0 %collective-permute-start = (f32[18,32,256]{2,1,0:T(8,128)S(1)}, f32[18,32,256]{2,1,0:T(8,128)S(1)}, u32[]{:S(2)}, u32[]{:S(2)}) collective-permute-start(f32[18,32,256]{2,1,0:T(8,128)S(1)} %pad_maximum_fusion), channel_id=1, source_target_pairs={{0,8},{8,16},{16,24},{24,32},{32,40},{40,48},{48,56},{56,64},{64,7... | collective-permute-start | bytes 1769480 | tf_op jit(solution)/shard_map/ppermute | solution.py:221
  7.0 14.2 %collective-permute-start.1 = (f32[18,32,256]{2,1,0:T(8,128)S(1)}, f32[18,32,256]{2,1,0:T(8,128)S(1)}, u32[]{:S(2)}, u32[]{:S(2)}) collective-permute-start(f32[18,32,256]{2,1,0:T(8,128)S(1)} %pad_maximum_fusion.1), channel_id=1, source_target_pairs={{8,0},{16,8},{24,16},{32,24},{40,32},{48,40},{56,48},{64,56},{72,6... | collective-permute-start | bytes 1769480 | tf_op jit(solution)/shard_map/ppermute | solution.py:222
  22.5 0.0 copy-done
  22.5 0.1 reshape.17
  22.6 7.6 %filter_inner.1 = (f32[4,16,32,256]{3,2,1,0:T(8,128)}, f32[4,12,32,256]{3,2,1,0:T(8,128)}, f32[8,264,128]{2,1,0:T(8,128)}) custom-call(f32[1]{0:T(128)S(6)} %copy.15.lower_ref, f32[1]{0:T(128)S(6)} %copy.16.upper_ref, f32[4,16,32,256]{3,2,1,0:T(8,128)} %orb_ref.3, f32[16,32,256]{2,1,0:T(8,128)} %pot_ref.3, f32[8,128]{1,0:T(8,128)S(1)} %pad.4.rot_ref), custom_call_target="tpu_custom_call" | custom-call | flops 1000000 | bytes 1000000 | tf_op jit(solution)/shard_map/filter_inner/pallas_call | solution.py:237
  30.2 6.9 %all-to-all-start = ((f32[8,264,128]{2,1,0:T(8,128)}), f32[8,264,128]{2,1,0:T(8,128)}, u32[]{:S(2)}, u32[]{:S(2)}) async-start(f32[8,264,128]{2,1,0:T(8,128)} %get-tuple-element.17), calls=%async_computation | async-start | bytes 2162688 | tf_op jit(solution)/shard_map/all_to_all | solution.py:262
  37.1 8.1 %collective-permute-done.low_ref = f32[18,32,256]{2,1,0:T(8,128)S(1)} collective-permute-done((f32[18,32,256]{2,1,0:T(8,128)S(1)}, f32[18,32,256]{2,1,0:T(8,128)S(1)}, u32[]{:S(2)}, u32[]{:S(2)}) %collective-permute-start) | collective-permute-done | bytes 589856 | tf_op jit(solution)/shard_map/ppermute | solution.py:221
  45.2 0.0 collective-permute-done.1.high_ref
  45.2 7.5 %filter_outer.1 = (f32[4,16,32,256]{3,2,1,0:T(8,128)}, f32[256,128]{1,0:T(8,128)S(1)}, f32[256,128]{1,0:T(8,128)S(1)}, f32[256,128]{1,0:T(8,128)S(1)}, f32[256,1...) custom-call(s32[1]{0:T(128)} %bitcast.mine_ref, ...), custom_call_target="tpu_custom_call", output_to_operand_aliasing={{0}: (8, {})} | custom-call | flops 399999991808 | bytes 400000000 | tf_op jit(solution)/shard_map/filter_outer/pallas_call | solution.py:265
  52.7 4.6 %collective-permute-start.2 = (f32[256,128]{1,0:T(8,128)S(1)}, f32[256,128]{1,0:T(8,128)S(1)}, u32[]{:S(2)}, u32[]{:S(2)}) collective-permute-start(f32[256,128]{1,0:T(8,128)S(1)} %get-tuple-element.18), channel_id=1, source_target_pairs={{0,1},{1,0},{2,3},{3,2},{4,5},{5,4},{6,7},{7,6},{8,9},{9,8},{10,11... | collective-permute-start | bytes 393224 | tf_op jit(solution)/shard_map/ppermute | solution.py:233
  57.4 1.9 %collective-permute-start.3 = (f32[256,128]{1,0:T(8,128)S(1)}, f32[256,128]{1,0:T(8,128)S(1)}, u32[]{:S(2)}, u32[]{:S(2)}) collective-permute-start(f32[256,128]{1,0:T(8,128)S(1)} %get-tuple-element.19), channel_id=1, source_target_pairs={{0,2},{1,3},{2,0},{3,1},{4,6},{5,7},{6,4},{7,5},{8,10},{9,11},{10,... | collective-permute-start | bytes 393224 | tf_op jit(solution)/shard_map/ppermute | solution.py:233
  59.3 4.4 %collective-permute-start.4 = (f32[256,128]{1,0:T(8,128)S(1)}, f32[256,128]{1,0:T(8,128)S(1)}, u32[]{:S(2)}, u32[]{:S(2)}) collective-permute-start(f32[256,128]{1,0:T(8,128)S(1)} %get-tuple-element.20), channel_id=1, source_target_pairs={{0,4},{1,5},{2,6},{3,7},{4,0},{5,1},{6,2},{7,3},{8,12},{9,13},{10,... | collective-permute-start | bytes 393224 | tf_op jit(solution)/shard_map/ppermute | solution.py:233
  63.7 2.1 %collective-permute-start.5 = (f32[256,128]{1,0:T(8,128)S(1)}, f32[256,128]{1,0:T(8,128)S(1)}, u32[]{:S(2)}, u32[]{:S(2)}) collective-permute-start(f32[256,128]{1,0:T(8,128)S(1)} %get-tuple-element.21), channel_id=1, source_target_pairs={{0,5},{1,4},{2,7},{3,6},{4,1},{5,0},{6,3},{7,2},{8,13},{9,12},{10,... | collective-permute-start | bytes 393224 | tf_op jit(solution)/shard_map/ppermute | solution.py:233
  65.8 4.7 %collective-permute-start.6 = (f32[256,128]{1,0:T(8,128)S(1)}, f32[256,128]{1,0:T(8,128)S(1)}, u32[]{:S(2)}, u32[]{:S(2)}) collective-permute-start(f32[256,128]{1,0:T(8,128)S(1)} %get-tuple-element.23), channel_id=1, source_target_pairs={{0,6},{1,7},{2,4},{3,5},{4,2},{5,3},{6,0},{7,1},{8,14},{9,15},{10,... | collective-permute-start | bytes 393224 | tf_op jit(solution)/shard_map/ppermute | solution.py:233
  70.5 0.0 collective-permute-done.2.rest_0_
  70.5 1.9 %collective-permute-start.7 = (f32[256,128]{1,0:T(8,128)S(1)}, f32[256,128]{1,0:T(8,128)S(1)}, u32[]{:S(2)}, u32[]{:S(2)}) collective-permute-start(f32[256,128]{1,0:T(8,128)S(1)} %get-tuple-element.24), channel_id=1, source_target_pairs={{0,7},{1,6},{2,5},{3,4},{4,3},{5,2},{6,1},{7,0},{8,15},{9,14},{10,... | collective-permute-start | bytes 393224 | tf_op jit(solution)/shard_map/ppermute | solution.py:233
  72.4 0.0 collective-permute-done.3.rest_1_
  72.4 4.3 %collective-permute-start.8 = (f32[256,128]{1,0:T(8,128)S(1)}, f32[256,128]{1,0:T(8,128)S(1)}, u32[]{:S(2)}, u32[]{:S(2)}) collective-permute-start(f32[256,128]{1,0:T(8,128)S(1)} %get-tuple-element.25), channel_id=1, source_target_pairs={{0,3},{1,2},{2,1},{3,0},{4,7},{5,6},{6,5},{7,4},{8,11},{9,10},{10,... | collective-permute-start | bytes 393224 | tf_op jit(solution)/shard_map/ppermute | solution.py:233
  76.8 3.4 %all-to-all-done.recv_ref = f32[8,264,128]{2,1,0:T(8,128)} async-done(((f32[8,264,128]{2,1,0:T(8,128)}), f32[8,264,128]{2,1,0:T(8,128)}, u32[]{:S(2)}, u32[]{:S(2)}) %all-to-all-start) | async-done | bytes 1081376 | tf_op jit(solution)/shard_map/all_to_all | solution.py:262
  80.1 0.8 slice.20
  80.9 1.9 %collective-permute-done.4.rest_2_ = f32[256,128]{1,0:T(8,128)S(1)} collective-permute-done((f32[256,128]{1,0:T(8,128)S(1)}, f32[256,128]{1,0:T(8,128)S(1)}, u32[]{:S(2)}, u32[]{:S(2)}) %collective-permute-start.4) | collective-permute-done | bytes 131104 | tf_op jit(solution)/shard_map/ppermute | solution.py:233
  82.8 2.8 %collective-permute-done.5.rest_3_ = f32[256,128]{1,0:T(8,128)S(1)} collective-permute-done((f32[256,128]{1,0:T(8,128)S(1)}, f32[256,128]{1,0:T(8,128)S(1)}, u32[]{:S(2)}, u32[]{:S(2)}) %collective-permute-start.5) | collective-permute-done | bytes 131104 | tf_op jit(solution)/shard_map/ppermute | solution.py:233
  85.7 1.4 %rotate_soon.1.sums_ref = f32[2,64,8,128]{3,2,1,0:T(8,128)S(1)} custom-call(s32[1]{0:T(128)} %bitcast.mine_ref, f32[8,64]{1,0:T(8,128)S(1)} %bitcast.6, f32[256,128]{1,0:T(8,128)S(1)} %collective-permute-done.2.rest_0_, f32[256,128]{1,0:T(8,128)S(1)} %collective-permute-done.3.rest_1_, f32[256,128]{1,0:T(8,128)S(1)} %collective-permute-done.4.rest_2_, ...), custom_call_target="tpu_custom_call" | custom-call | flops 5000000 | bytes 1100000 | tf_op jit(solution)/shard_map/rotate_soon/pallas_call | solution.py:301
  87.1 3.3 %rotate_inner.1.rest_3_ = f32[16,16,4,256]{3,2,1,0:T(4,128)} custom-call(f32[8,64]{1,0:T(8,128)S(1)} %bitcast.7, f32[8,264,128]{2,1,0:T(8,128)} %all-to-all-done.recv_ref), custom_call_target="tpu_custom_call" | custom-call | flops 8000000 | bytes 1600000 | tf_op jit(solution)/shard_map/rotate_inner/pallas_call | solution.py:291
  90.4 2.1 %collective-permute-done.6.rest_0_ = f32[256,128]{1,0:T(8,128)S(1)} collective-permute-done((f32[256,128]{1,0:T(8,128)S(1)}, f32[256,128]{1,0:T(8,128)S(1)}, u32[]{:S(2)}, u32[]{:S(2)}) %collective-permute-start.6) | collective-permute-done | bytes 131104 | tf_op jit(solution)/shard_map/ppermute | solution.py:233
  92.5 2.8 %collective-permute-done.7.rest_1_ = f32[256,128]{1,0:T(8,128)S(1)} collective-permute-done((f32[256,128]{1,0:T(8,128)S(1)}, f32[256,128]{1,0:T(8,128)S(1)}, u32[]{:S(2)}, u32[]{:S(2)}) %collective-permute-start.7) | collective-permute-done | bytes 131104 | tf_op jit(solution)/shard_map/ppermute | solution.py:233
  95.3 0.0 collective-permute-done.8.rest_2_
  95.3 1.8 %rotate_last.1 = f32[16,16,4,256]{3,2,1,0:T(4,128)} custom-call(s32[1]{0:T(128)} %bitcast.mine_ref, f32[8,64]{1,0:T(8,128)S(1)} %bitcast.8, f32[2,64,8,128]{3,2,1,0:T(8,128)S(1)} %rotate_soon.1.sums_ref, f32[256,128]{1,0:T(8,128)S(1)} %collective-permute-done.6.rest_0_, ...), custom_call_target="tpu_custom_call", output_to_operand_aliasing={{}: (6, {})} | custom-call | flops 3000000 | bytes 1100000 | tf_op jit(solution)/shard_map/rotate_last/pallas_call | solution.py:311
  (3 shorter events, 0.1 us)
Async XLA Ops:
  1.5 21.0 %copy-start = (f32[4,16]{1,0:T(4,128)S(1)}, f32[4,16]{1,0:T(4,128)}, u32[]{:S(2)}) copy-start(f32[4,16]{1,0:T(4,128)} %param.9) | copy-start | bytes 772
  2.9 42.3 %collective-permute-start = (f32[18,32,256]{2,1,0:T(8,128)S(1)}, f32[18,32,256]{2,1,0:T(8,128)S(1)}, u32[]{:S(2)}, u32[]{:S(2)}) collective-permute-start(f32[18,32,256]{2,1,0:T(8,128)S(1)} %pad_maximum_fusion), channel_id=1, source_target_pairs={{0,8},{8,16},{16,24},{24,32},{32,40},{40,48},{48,56},{56,64},{64,7... | collective-permute-start | bytes 1769480 | tf_op jit(solution)/shard_map/ppermute | solution.py:221
  7.0 38.2 %collective-permute-start.1 = (f32[18,32,256]{2,1,0:T(8,128)S(1)}, f32[18,32,256]{2,1,0:T(8,128)S(1)}, u32[]{:S(2)}, u32[]{:S(2)}) collective-permute-start(f32[18,32,256]{2,1,0:T(8,128)S(1)} %pad_maximum_fusion.1), channel_id=1, source_target_pairs={{8,0},{16,8},{24,16},{32,24},{40,32},{48,40},{56,48},{64,56},{72,6... | collective-permute-start | bytes 1769480 | tf_op jit(solution)/shard_map/ppermute | solution.py:222
  30.2 49.9 %all-to-all-start = ((f32[8,264,128]{2,1,0:T(8,128)}), f32[8,264,128]{2,1,0:T(8,128)}, u32[]{:S(2)}, u32[]{:S(2)}) async-start(f32[8,264,128]{2,1,0:T(8,128)} %get-tuple-element.17), calls=%async_computation | async-start | bytes 2162688 | tf_op jit(solution)/shard_map/all_to_all | solution.py:262
  52.7 17.8 %collective-permute-start.2 = (f32[256,128]{1,0:T(8,128)S(1)}, f32[256,128]{1,0:T(8,128)S(1)}, u32[]{:S(2)}, u32[]{:S(2)}) collective-permute-start(f32[256,128]{1,0:T(8,128)S(1)} %get-tuple-element.18), channel_id=1, source_target_pairs={{0,1},{1,0},{2,3},{3,2},{4,5},{5,4},{6,7},{7,6},{8,9},{9,8},{10,11... | collective-permute-start | bytes 393224 | tf_op jit(solution)/shard_map/ppermute | solution.py:233
  57.4 15.0 %collective-permute-start.3 = (f32[256,128]{1,0:T(8,128)S(1)}, f32[256,128]{1,0:T(8,128)S(1)}, u32[]{:S(2)}, u32[]{:S(2)}) collective-permute-start(f32[256,128]{1,0:T(8,128)S(1)} %get-tuple-element.19), channel_id=1, source_target_pairs={{0,2},{1,3},{2,0},{3,1},{4,6},{5,7},{6,4},{7,5},{8,10},{9,11},{10,... | collective-permute-start | bytes 393224 | tf_op jit(solution)/shard_map/ppermute | solution.py:233
  59.3 23.5 %collective-permute-start.4 = (f32[256,128]{1,0:T(8,128)S(1)}, f32[256,128]{1,0:T(8,128)S(1)}, u32[]{:S(2)}, u32[]{:S(2)}) collective-permute-start(f32[256,128]{1,0:T(8,128)S(1)} %get-tuple-element.20), channel_id=1, source_target_pairs={{0,4},{1,5},{2,6},{3,7},{4,0},{5,1},{6,2},{7,3},{8,12},{9,13},{10,... | collective-permute-start | bytes 393224 | tf_op jit(solution)/shard_map/ppermute | solution.py:233
  63.7 22.0 %collective-permute-start.5 = (f32[256,128]{1,0:T(8,128)S(1)}, f32[256,128]{1,0:T(8,128)S(1)}, u32[]{:S(2)}, u32[]{:S(2)}) collective-permute-start(f32[256,128]{1,0:T(8,128)S(1)} %get-tuple-element.21), channel_id=1, source_target_pairs={{0,5},{1,4},{2,7},{3,6},{4,1},{5,0},{6,3},{7,2},{8,13},{9,12},{10,... | collective-permute-start | bytes 393224 | tf_op jit(solution)/shard_map/ppermute | solution.py:233
  65.8 26.7 %collective-permute-start.6 = (f32[256,128]{1,0:T(8,128)S(1)}, f32[256,128]{1,0:T(8,128)S(1)}, u32[]{:S(2)}, u32[]{:S(2)}) collective-permute-start(f32[256,128]{1,0:T(8,128)S(1)} %get-tuple-element.23), channel_id=1, source_target_pairs={{0,6},{1,7},{2,4},{3,5},{4,2},{5,3},{6,0},{7,1},{8,14},{9,15},{10,... | collective-permute-start | bytes 393224 | tf_op jit(solution)/shard_map/ppermute | solution.py:233
  70.5 24.8 %collective-permute-start.7 = (f32[256,128]{1,0:T(8,128)S(1)}, f32[256,128]{1,0:T(8,128)S(1)}, u32[]{:S(2)}, u32[]{:S(2)}) collective-permute-start(f32[256,128]{1,0:T(8,128)S(1)} %get-tuple-element.24), channel_id=1, source_target_pairs={{0,7},{1,6},{2,5},{3,4},{4,3},{5,2},{6,1},{7,0},{8,15},{9,14},{10,... | collective-permute-start | bytes 393224 | tf_op jit(solution)/shard_map/ppermute | solution.py:233
  72.4 22.8 %collective-permute-start.8 = (f32[256,128]{1,0:T(8,128)S(1)}, f32[256,128]{1,0:T(8,128)S(1)}, u32[]{:S(2)}, u32[]{:S(2)}) collective-permute-start(f32[256,128]{1,0:T(8,128)S(1)} %get-tuple-element.25), channel_id=1, source_target_pairs={{0,3},{1,2},{2,1},{3,0},{4,7},{5,6},{6,5},{7,4},{8,11},{9,10},{10,... | collective-permute-start | bytes 393224 | tf_op jit(solution)/shard_map/ppermute | solution.py:233

commit v6 on v5

--- a/solution.py
+++ b/solution.py
@@ -37,7 +37,7 @@
         store(p, scaled_hamilton([source(p + d) for d in range(5)], local(p), coef))
         return carry
 
-    lax.fori_loop(0, count, step, 0, unroll=2)
+    lax.fori_loop(0, count, step, 0, unroll=4)
 
 
 def filtered_plane(q, first, original, local, coef):
@@ -168,7 +168,7 @@
 
 
 def rotate_soon_kernel(mine_ref, rot_ref, *rest):
-    received, sums_ref, mine, u = rest[:-1], rest[-1], mine_ref[0], pl.program_id(0)
+    received, sums_ref, mine, u = rest[:-2], rest[-1], mine_ref[0], pl.program_id(0)
 
     def finish(j, n, value):
         sums_ref[u, 4 * j + n] = value
@@ -287,7 +287,7 @@
     received_outer = regroup(sends_outer)
 
     weights = received[:, 256, : ORBS * NCOL]
-    rotated_shape = jax.ShapeDtypeStruct((NCOL, PLANES, 4, COLS), F32)
+    rotated_shape = pltpu.HBM((NCOL, PLANES, 4, COLS), F32)
     rotated = pl.pallas_call(
         rotate_inner_kernel,
         grid=(2,),
@@ -298,16 +298,17 @@
         cost_estimate=cost(8_000_000, 1_600_000),
         name="rotate_inner",
     )(weights, received)
+    rotated = pltpu.with_memory_space_constraint(rotated, pltpu.HBM)
     sums = pl.pallas_call(
         rotate_soon_kernel,
         grid=(2,),
-        in_specs=[SMEM, SMEM] + [VMEM] * len(SOON),
+        in_specs=[SMEM, SMEM] + [VMEM] * len(SOON) + [ANY],
         out_specs=VMEM,
         out_shape=jax.ShapeDtypeStruct((2, 4 * NCOL, 8, 128), F32),
         compiler_params=params(),
         cost_estimate=cost(5_000_000, 1_100_000),
         name="rotate_soon",
-    )(mine, weights, *received_outer[: len(SOON)])
+    )(mine, weights, *received_outer[: len(SOON)], rotated)
     rotated = pl.pallas_call(
         rotate_last_kernel,
         grid=(2,),

time: 97.9 us -> 97.9 us (level)
  transfers between devices with their start and end apart: 10 -> 10, of which waited for: 6 -> 5; matrix products, arithmetic and copies ran while one was open for 1% -> 1% of each run, Pallas kernels for 20% -> 20%
where the time goes in v6:
time: 97.9 us; the launch traced here: 97.1 us
  starting transfers between devices  49.1 us (50%)
  waiting for transfers between devices  21.9 us (22%)
  Pallas kernels  21 us (21%)
  local copies, waits for them, and re-layouts  3.05 us (3%)
  between operations  2.07 us (2%)
    ppermute x7, starting transfers between devices, regroup(): lax.ppermute(sends[k], 'orb', [(o, o ^ k) for o in range(PEERS)])  24 us
    ppermute x1, starting transfers between devices, body(): high = lax.ppermute(packed(0, 0), 'grid', backward)  14.2 us
    ppermute x7, waiting for transfers between devices, regroup(): lax.ppermute(sends[k], 'orb', [(o, o ^ k) for o in range(PEERS)])  9.57 us
    ppermute x1, waiting for transfers between devices, body(): low = lax.ppermute(packed(PLANES - REACH, PLANES - 2), 'grid', forward)  8.78 us
    pallas_call x1, Pallas kernels, body(): pl.pallas_call(outer_kernel, grid=(ORBS, 2), in_specs=[SMEM, VMEM, VMEM]...  7.55 us
    pallas_call x1, Pallas kernels, body(): pl.pallas_call(inner_kernel, grid=(ORBS,), in_specs=[VMEM, VMEM, pl.Block...  6.9 us
    all_to_all x1, starting transfers between devices, body(): lax.all_to_all(send, 'orb', split_axis=0, concat_axis=0, tiled=True)  6.88 us
    ppermute x1, starting transfers between devices, body(): low = lax.ppermute(packed(PLANES - REACH, PLANES - 2), 'grid', forward)  4 us
  transfers between devices with their start and end apart: 10, of which 5 were waited for; matrix products, arithmetic and copies ran while one was open for 1% of the time, Pallas kernels for 20%

profile of v6, /device:TPU:17, one launch (start us, length us, event | category | flops | bytes accessed | tf_op | source)
XLA Modules:
  0.0 97.1 jit_solution(4465867466836113177)
XLA Ops:
  0.6 0.9 fusion.1
  1.5 0.0 copy-start
  1.5 1.3 %fusion = (f32[4,4,32,256]{3,2,1,0:T(8,128)S(1)}, f32[4,4,32,256]{3,2,1,0:T(8,128)S(1)}) fusion(f32[4,16,32,256]{3,2,1,0:T(8,128)} %orb_ref.3), kind=kLoop, calls=%fused_computation.2 | loop fusion | bytes 2097152 | tf_op jit(solution)/shard_map/slice | solution.py:218
  2.9 4.0 %collective-permute-start = (f32[18,32,256]{2,1,0:T(8,128)S(1)}, f32[18,32,256]{2,1,0:T(8,128)S(1)}, u32[]{:S(2)}, u32[]{:S(2)}) collective-permute-start(f32[18,32,256]{2,1,0:T(8,128)S(1)} %pad_maximum_fusion), channel_id=1, source_target_pairs={{0,8},{8,16},{16,24},{24,32},{32,40},{40,48},{48,56},{56,64},{64,7... | collective-permute-start | bytes 1769480 | tf_op jit(solution)/shard_map/ppermute | solution.py:221
  7.0 14.2 %collective-permute-start.1 = (f32[18,32,256]{2,1,0:T(8,128)S(1)}, f32[18,32,256]{2,1,0:T(8,128)S(1)}, u32[]{:S(2)}, u32[]{:S(2)}) collective-permute-start(f32[18,32,256]{2,1,0:T(8,128)S(1)} %pad_maximum_fusion.1), channel_id=1, source_target_pairs={{8,0},{16,8},{24,16},{32,24},{40,32},{48,40},{56,48},{64,56},{72,6... | collective-permute-start | bytes 1769480 | tf_op jit(solution)/shard_map/ppermute | solution.py:222
  22.5 0.0 copy-done
  22.5 0.1 reshape.17
  22.6 6.9 %filter_inner.1 = (f32[4,16,32,256]{3,2,1,0:T(8,128)}, f32[4,12,32,256]{3,2,1,0:T(8,128)}, f32[8,264,128]{2,1,0:T(8,128)}) custom-call(f32[1]{0:T(128)S(6)} %copy.15.lower_ref, f32[1]{0:T(128)S(6)} %copy.16.upper_ref, f32[4,16,32,256]{3,2,1,0:T(8,128)} %orb_ref.3, f32[16,32,256]{2,1,0:T(8,128)} %pot_ref.3, f32[8,128]{1,0:T(8,128)S(1)} %pad.4.rot_ref), custom_call_target="tpu_custom_call" | custom-call | flops 1000000 | bytes 1000000 | tf_op jit(solution)/shard_map/filter_inner/pallas_call | solution.py:237
  29.5 6.9 %all-to-all-start = ((f32[8,264,128]{2,1,0:T(8,128)}), f32[8,264,128]{2,1,0:T(8,128)}, u32[]{:S(2)}, u32[]{:S(2)}) async-start(f32[8,264,128]{2,1,0:T(8,128)} %get-tuple-element.17), calls=%async_computation | async-start | bytes 2162688 | tf_op jit(solution)/shard_map/all_to_all | solution.py:262
  36.4 8.8 %collective-permute-done.low_ref = f32[18,32,256]{2,1,0:T(8,128)S(1)} collective-permute-done((f32[18,32,256]{2,1,0:T(8,128)S(1)}, f32[18,32,256]{2,1,0:T(8,128)S(1)}, u32[]{:S(2)}, u32[]{:S(2)}) %collective-permute-start) | collective-permute-done | bytes 589856 | tf_op jit(solution)/shard_map/ppermute | solution.py:221
  45.2 0.0 collective-permute-done.1.high_ref
  45.2 7.5 %filter_outer.1 = (f32[4,16,32,256]{3,2,1,0:T(8,128)}, f32[256,128]{1,0:T(8,128)S(1)}, f32[256,128]{1,0:T(8,128)S(1)}, f32[256,128]{1,0:T(8,128)S(1)}, f32[256,1...) custom-call(s32[1]{0:T(128)} %bitcast.mine_ref, ...), custom_call_target="tpu_custom_call", output_to_operand_aliasing={{0}: (8, {})} | custom-call | flops 399999991808 | bytes 400000000 | tf_op jit(solution)/shard_map/filter_outer/pallas_call | solution.py:265
  52.7 4.7 %collective-permute-start.2 = (f32[256,128]{1,0:T(8,128)S(1)}, f32[256,128]{1,0:T(8,128)S(1)}, u32[]{:S(2)}, u32[]{:S(2)}) collective-permute-start(f32[256,128]{1,0:T(8,128)S(1)} %get-tuple-element.18), channel_id=1, source_target_pairs={{0,1},{1,0},{2,3},{3,2},{4,5},{5,4},{6,7},{7,6},{8,9},{9,8},{10,11... | collective-permute-start | bytes 393224 | tf_op jit(solution)/shard_map/ppermute | solution.py:233
  57.4 1.9 %collective-permute-start.3 = (f32[256,128]{1,0:T(8,128)S(1)}, f32[256,128]{1,0:T(8,128)S(1)}, u32[]{:S(2)}, u32[]{:S(2)}) collective-permute-start(f32[256,128]{1,0:T(8,128)S(1)} %get-tuple-element.19), channel_id=1, source_target_pairs={{0,2},{1,3},{2,0},{3,1},{4,6},{5,7},{6,4},{7,5},{8,10},{9,11},{10,... | collective-permute-start | bytes 393224 | tf_op jit(solution)/shard_map/ppermute | solution.py:233
  59.3 4.4 %collective-permute-start.4 = (f32[256,128]{1,0:T(8,128)S(1)}, f32[256,128]{1,0:T(8,128)S(1)}, u32[]{:S(2)}, u32[]{:S(2)}) collective-permute-start(f32[256,128]{1,0:T(8,128)S(1)} %get-tuple-element.20), channel_id=1, source_target_pairs={{0,4},{1,5},{2,6},{3,7},{4,0},{5,1},{6,2},{7,3},{8,12},{9,13},{10,... | collective-permute-start | bytes 393224 | tf_op jit(solution)/shard_map/ppermute | solution.py:233
  63.7 2.1 %collective-permute-start.5 = (f32[256,128]{1,0:T(8,128)S(1)}, f32[256,128]{1,0:T(8,128)S(1)}, u32[]{:S(2)}, u32[]{:S(2)}) collective-permute-start(f32[256,128]{1,0:T(8,128)S(1)} %get-tuple-element.21), channel_id=1, source_target_pairs={{0,5},{1,4},{2,7},{3,6},{4,1},{5,0},{6,3},{7,2},{8,13},{9,12},{10,... | collective-permute-start | bytes 393224 | tf_op jit(solution)/shard_map/ppermute | solution.py:233
  65.8 4.8 %collective-permute-start.6 = (f32[256,128]{1,0:T(8,128)S(1)}, f32[256,128]{1,0:T(8,128)S(1)}, u32[]{:S(2)}, u32[]{:S(2)}) collective-permute-start(f32[256,128]{1,0:T(8,128)S(1)} %get-tuple-element.23), channel_id=1, source_target_pairs={{0,6},{1,7},{2,4},{3,5},{4,2},{5,3},{6,0},{7,1},{8,14},{9,15},{10,... | collective-permute-start | bytes 393224 | tf_op jit(solution)/shard_map/ppermute | solution.py:233
  70.6 0.0 collective-permute-done.2.rest_0_
  70.7 1.9 %collective-permute-start.7 = (f32[256,128]{1,0:T(8,128)S(1)}, f32[256,128]{1,0:T(8,128)S(1)}, u32[]{:S(2)}, u32[]{:S(2)}) collective-permute-start(f32[256,128]{1,0:T(8,128)S(1)} %get-tuple-element.24), channel_id=1, source_target_pairs={{0,7},{1,6},{2,5},{3,4},{4,3},{5,2},{6,1},{7,0},{8,15},{9,14},{10,... | collective-permute-start | bytes 393224 | tf_op jit(solution)/shard_map/ppermute | solution.py:233
  72.6 0.0 collective-permute-done.3.rest_1_
  72.6 4.1 %collective-permute-start.8 = (f32[256,128]{1,0:T(8,128)S(1)}, f32[256,128]{1,0:T(8,128)S(1)}, u32[]{:S(2)}, u32[]{:S(2)}) collective-permute-start(f32[256,128]{1,0:T(8,128)S(1)} %get-tuple-element.25), channel_id=1, source_target_pairs={{0,3},{1,2},{2,1},{3,0},{4,7},{5,6},{6,5},{7,4},{8,11},{9,10},{10,... | collective-permute-start | bytes 393224 | tf_op jit(solution)/shard_map/ppermute | solution.py:233
  76.7 3.5 %all-to-all-done.recv_ref = f32[8,264,128]{2,1,0:T(8,128)} async-done(((f32[8,264,128]{2,1,0:T(8,128)}), f32[8,264,128]{2,1,0:T(8,128)}, u32[]{:S(2)}, u32[]{:S(2)}) %all-to-all-start) | async-done | bytes 1081376 | tf_op jit(solution)/shard_map/all_to_all | solution.py:262
  80.3 0.8 slice.20
  81.0 3.3 %rotate_inner.1.rest_5_.rest_3_ = f32[16,16,4,256]{3,2,1,0:T(4,128)} custom-call(f32[8,64]{1,0:T(8,128)S(1)} %bitcast.6, f32[8,264,128]{2,1,0:T(8,128)} %all-to-all-done.recv_ref), custom_call_target="tpu_custom_call" | custom-call | flops 8000000 | bytes 1600000 | tf_op jit(solution)/shard_map/rotate_inner/pallas_call | solution.py:291
  84.3 0.0 collective-permute-done.4.rest_2_
  84.3 1.5 %collective-permute-done.5.rest_3_ = f32[256,128]{1,0:T(8,128)S(1)} collective-permute-done((f32[256,128]{1,0:T(8,128)S(1)}, f32[256,128]{1,0:T(8,128)S(1)}, u32[]{:S(2)}, u32[]{:S(2)}) %collective-permute-start.5) | collective-permute-done | bytes 131104 | tf_op jit(solution)/shard_map/ppermute | solution.py:233
  85.8 1.4 %rotate_soon.1.sums_ref = f32[2,64,8,128]{3,2,1,0:T(8,128)S(1)} custom-call(s32[1]{0:T(128)} %bitcast.mine_ref, f32[8,64]{1,0:T(8,128)S(1)} %bitcast.7, f32[256,128]{1,0:T(8,128)S(1)} %collective-permute-done.2.rest_0_, f32[256,128]{1,0:T(8,128)S(1)} %collective-permute-done.3.rest_1_, f32[256,128]{1,0:T(8,128)S(1)} %collective-permute-done.4.rest_2_, ...), custom_call_target="tpu_custom_call" | custom-call | flops 5000000 | bytes 1100000 | tf_op jit(solution)/shard_map/rotate_soon/pallas_call | solution.py:302
  87.2 5.3 %collective-permute-done.6.rest_0_ = f32[256,128]{1,0:T(8,128)S(1)} collective-permute-done((f32[256,128]{1,0:T(8,128)S(1)}, f32[256,128]{1,0:T(8,128)S(1)}, u32[]{:S(2)}, u32[]{:S(2)}) %collective-permute-start.6) | collective-permute-done | bytes 131104 | tf_op jit(solution)/shard_map/ppermute | solution.py:233
  92.5 2.8 %collective-permute-done.7.rest_1_ = f32[256,128]{1,0:T(8,128)S(1)} collective-permute-done((f32[256,128]{1,0:T(8,128)S(1)}, f32[256,128]{1,0:T(8,128)S(1)}, u32[]{:S(2)}, u32[]{:S(2)}) %collective-permute-start.7) | collective-permute-done | bytes 131104 | tf_op jit(solution)/shard_map/ppermute | solution.py:233
  95.3 0.0 collective-permute-done.8.rest_2_
  95.3 1.8 %rotate_last.1 = f32[16,16,4,256]{3,2,1,0:T(4,128)} custom-call(s32[1]{0:T(128)} %bitcast.mine_ref, f32[8,64]{1,0:T(8,128)S(1)} %bitcast.8, f32[2,64,8,128]{3,2,1,0:T(8,128)S(1)} %rotate_soon.1.sums_ref, f32[256,128]{1,0:T(8,128)S(1)} %collective-permute-done.6.rest_0_, ...), custom_call_target="tpu_custom_call", output_to_operand_aliasing={{}: (6, {})} | custom-call | flops 3000000 | bytes 1100000 | tf_op jit(solution)/shard_map/rotate_last/pallas_call | solution.py:312
  (3 shorter events, 0.1 us)
Async XLA Ops:
  1.5 21.0 %copy-start = (f32[4,16]{1,0:T(4,128)S(1)}, f32[4,16]{1,0:T(4,128)}, u32[]{:S(2)}) copy-start(f32[4,16]{1,0:T(4,128)} %param.9) | copy-start | bytes 772
  2.9 42.3 %collective-permute-start = (f32[18,32,256]{2,1,0:T(8,128)S(1)}, f32[18,32,256]{2,1,0:T(8,128)S(1)}, u32[]{:S(2)}, u32[]{:S(2)}) collective-permute-start(f32[18,32,256]{2,1,0:T(8,128)S(1)} %pad_maximum_fusion), channel_id=1, source_target_pairs={{0,8},{8,16},{16,24},{24,32},{32,40},{40,48},{48,56},{56,64},{64,7... | collective-permute-start | bytes 1769480 | tf_op jit(solution)/shard_map/ppermute | solution.py:221
  7.0 38.2 %collective-permute-start.1 = (f32[18,32,256]{2,1,0:T(8,128)S(1)}, f32[18,32,256]{2,1,0:T(8,128)S(1)}, u32[]{:S(2)}, u32[]{:S(2)}) collective-permute-start(f32[18,32,256]{2,1,0:T(8,128)S(1)} %pad_maximum_fusion.1), channel_id=1, source_target_pairs={{8,0},{16,8},{24,16},{32,24},{40,32},{48,40},{56,48},{64,56},{72,6... | collective-permute-start | bytes 1769480 | tf_op jit(solution)/shard_map/ppermute | solution.py:222
  29.5 50.8 %all-to-all-start = ((f32[8,264,128]{2,1,0:T(8,128)}), f32[8,264,128]{2,1,0:T(8,128)}, u32[]{:S(2)}, u32[]{:S(2)}) async-start(f32[8,264,128]{2,1,0:T(8,128)} %get-tuple-element.17), calls=%async_computation | async-start | bytes 2162688 | tf_op jit(solution)/shard_map/all_to_all | solution.py:262
  52.7 17.9 %collective-permute-start.2 = (f32[256,128]{1,0:T(8,128)S(1)}, f32[256,128]{1,0:T(8,128)S(1)}, u32[]{:S(2)}, u32[]{:S(2)}) collective-permute-start(f32[256,128]{1,0:T(8,128)S(1)} %get-tuple-element.18), channel_id=1, source_target_pairs={{0,1},{1,0},{2,3},{3,2},{4,5},{5,4},{6,7},{7,6},{8,9},{9,8},{10,11... | collective-permute-start | bytes 393224 | tf_op jit(solution)/shard_map/ppermute | solution.py:233
  57.4 15.2 %collective-permute-start.3 = (f32[256,128]{1,0:T(8,128)S(1)}, f32[256,128]{1,0:T(8,128)S(1)}, u32[]{:S(2)}, u32[]{:S(2)}) collective-permute-start(f32[256,128]{1,0:T(8,128)S(1)} %get-tuple-element.19), channel_id=1, source_target_pairs={{0,2},{1,3},{2,0},{3,1},{4,6},{5,7},{6,4},{7,5},{8,10},{9,11},{10,... | collective-permute-start | bytes 393224 | tf_op jit(solution)/shard_map/ppermute | solution.py:233
  59.3 25.0 %collective-permute-start.4 = (f32[256,128]{1,0:T(8,128)S(1)}, f32[256,128]{1,0:T(8,128)S(1)}, u32[]{:S(2)}, u32[]{:S(2)}) collective-permute-start(f32[256,128]{1,0:T(8,128)S(1)} %get-tuple-element.20), channel_id=1, source_target_pairs={{0,4},{1,5},{2,6},{3,7},{4,0},{5,1},{6,2},{7,3},{8,12},{9,13},{10,... | collective-permute-start | bytes 393224 | tf_op jit(solution)/shard_map/ppermute | solution.py:233
  63.7 22.0 %collective-permute-start.5 = (f32[256,128]{1,0:T(8,128)S(1)}, f32[256,128]{1,0:T(8,128)S(1)}, u32[]{:S(2)}, u32[]{:S(2)}) collective-permute-start(f32[256,128]{1,0:T(8,128)S(1)} %get-tuple-element.21), channel_id=1, source_target_pairs={{0,5},{1,4},{2,7},{3,6},{4,1},{5,0},{6,3},{7,2},{8,13},{9,12},{10,... | collective-permute-start | bytes 393224 | tf_op jit(solution)/shard_map/ppermute | solution.py:233
  65.8 26.7 %collective-permute-start.6 = (f32[256,128]{1,0:T(8,128)S(1)}, f32[256,128]{1,0:T(8,128)S(1)}, u32[]{:S(2)}, u32[]{:S(2)}) collective-permute-start(f32[256,128]{1,0:T(8,128)S(1)} %get-tuple-element.23), channel_id=1, source_target_pairs={{0,6},{1,7},{2,4},{3,5},{4,2},{5,3},{6,0},{7,1},{8,14},{9,15},{10,... | collective-permute-start | bytes 393224 | tf_op jit(solution)/shard_map/ppermute | solution.py:233
  70.7 24.6 %collective-permute-start.7 = (f32[256,128]{1,0:T(8,128)S(1)}, f32[256,128]{1,0:T(8,128)S(1)}, u32[]{:S(2)}, u32[]{:S(2)}) collective-permute-start(f32[256,128]{1,0:T(8,128)S(1)} %get-tuple-element.24), channel_id=1, source_target_pairs={{0,7},{1,6},{2,5},{3,4},{4,3},{5,2},{6,1},{7,0},{8,15},{9,14},{10,... | collective-permute-start | bytes 393224 | tf_op jit(solution)/shard_map/ppermute | solution.py:233
  72.6 22.7 %collective-permute-start.8 = (f32[256,128]{1,0:T(8,128)S(1)}, f32[256,128]{1,0:T(8,128)S(1)}, u32[]{:S(2)}, u32[]{:S(2)}) collective-permute-start(f32[256,128]{1,0:T(8,128)S(1)} %get-tuple-element.25), channel_id=1, source_target_pairs={{0,3},{1,2},{2,1},{3,0},{4,7},{5,6},{6,5},{7,4},{8,11},{9,10},{10,... | collective-permute-start | bytes 393224 | tf_op jit(solution)/shard_map/ppermute | solution.py:233

commit v7 on v6

--- a/solution.py
+++ b/solution.py
@@ -37,7 +37,7 @@
         store(p, scaled_hamilton([source(p + d) for d in range(5)], local(p), coef))
         return carry
 
-    lax.fori_loop(0, count, step, 0, unroll=4)
+    lax.fori_loop(0, count, step, 0, unroll=True)
 
 
 def filtered_plane(q, first, original, local, coef):

time: 97.9 us -> 97.9 us (level)
  transfers between devices with their start and end apart: 10 -> 10, of which waited for: 5 -> 5; matrix products, arithmetic and copies ran while one was open for 1% -> 1% of each run, Pallas kernels for 20% -> 19%
where the time goes in v7:
time: 97.9 us; the launch traced here: 97.1 us
  starting transfers between devices  49.2 us (50%)
  waiting for transfers between devices  22.5 us (23%)
  Pallas kernels  20.2 us (21%)
  local copies, waits for them, and re-layouts  3.05 us (3%)
  between operations  2.07 us (2%)
    ppermute x7, starting transfers between devices, regroup(): lax.ppermute(sends[k], 'orb', [(o, o ^ k) for o in range(PEERS)])  24.1 us
    ppermute x1, starting transfers between devices, body(): high = lax.ppermute(packed(0, 0), 'grid', backward)  14.2 us
    ppermute x7, waiting for transfers between devices, regroup(): lax.ppermute(sends[k], 'orb', [(o, o ^ k) for o in range(PEERS)])  10.1 us
    ppermute x1, waiting for transfers between devices, body(): low = lax.ppermute(packed(PLANES - REACH, PLANES - 2), 'grid', forward)  9.44 us
    pallas_call x1, Pallas kernels, body(): pl.pallas_call(outer_kernel, grid=(ORBS, 2), in_specs=[SMEM, VMEM, VMEM]...  7.55 us
    all_to_all x1, starting transfers between devices, body(): lax.all_to_all(send, 'orb', split_axis=0, concat_axis=0, tiled=True)  6.88 us
    pallas_call x1, Pallas kernels, body(): pl.pallas_call(inner_kernel, grid=(ORBS,), in_specs=[VMEM, VMEM, pl.Block...  6.16 us
    ppermute x1, starting transfers between devices, body(): low = lax.ppermute(packed(PLANES - REACH, PLANES - 2), 'grid', forward)  4 us
  transfers between devices with their start and end apart: 10, of which 5 were waited for; matrix products, arithmetic and copies ran while one was open for 1% of the time, Pallas kernels for 19%

profile of v7, /device:TPU:17, one launch (start us, length us, event | category | flops | bytes accessed | tf_op | source)
XLA Modules:
  0.0 97.1 jit_solution(9320983379631149268)
XLA Ops:
  0.6 0.9 fusion.1
  1.5 0.0 copy-start
  1.5 1.3 %fusion = (f32[4,4,32,256]{3,2,1,0:T(8,128)S(1)}, f32[4,4,32,256]{3,2,1,0:T(8,128)S(1)}) fusion(f32[4,16,32,256]{3,2,1,0:T(8,128)} %orb_ref.3), kind=kLoop, calls=%fused_computation.2 | loop fusion | bytes 2097152 | tf_op jit(solution)/shard_map/slice | solution.py:218
  2.9 4.0 %collective-permute-start = (f32[18,32,256]{2,1,0:T(8,128)S(1)}, f32[18,32,256]{2,1,0:T(8,128)S(1)}, u32[]{:S(2)}, u32[]{:S(2)}) collective-permute-start(f32[18,32,256]{2,1,0:T(8,128)S(1)} %pad_maximum_fusion), channel_id=1, source_target_pairs={{0,8},{8,16},{16,24},{24,32},{32,40},{40,48},{48,56},{56,64},{64,7... | collective-permute-start | bytes 1769480 | tf_op jit(solution)/shard_map/ppermute | solution.py:221
  7.0 14.2 %collective-permute-start.1 = (f32[18,32,256]{2,1,0:T(8,128)S(1)}, f32[18,32,256]{2,1,0:T(8,128)S(1)}, u32[]{:S(2)}, u32[]{:S(2)}) collective-permute-start(f32[18,32,256]{2,1,0:T(8,128)S(1)} %pad_maximum_fusion.1), channel_id=1, source_target_pairs={{8,0},{16,8},{24,16},{32,24},{40,32},{48,40},{56,48},{64,56},{72,6... | collective-permute-start | bytes 1769480 | tf_op jit(solution)/shard_map/ppermute | solution.py:222
  22.5 0.0 copy-done
  22.5 0.1 reshape.17
  22.6 6.2 %filter_inner.1 = (f32[4,16,32,256]{3,2,1,0:T(8,128)}, f32[4,12,32,256]{3,2,1,0:T(8,128)}, f32[8,264,128]{2,1,0:T(8,128)}) custom-call(f32[1]{0:T(128)S(6)} %copy.15.lower_ref, f32[1]{0:T(128)S(6)} %copy.16.upper_ref, f32[4,16,32,256]{3,2,1,0:T(8,128)} %orb_ref.3, f32[16,32,256]{2,1,0:T(8,128)} %pot_ref.3, f32[8,128]{1,0:T(8,128)S(1)} %pad.4.rot_ref), custom_call_target="tpu_custom_call" | custom-call | flops 1000000 | bytes 1000000 | tf_op jit(solution)/shard_map/filter_inner/pallas_call | solution.py:237
  28.8 6.9 %all-to-all-start = ((f32[8,264,128]{2,1,0:T(8,128)}), f32[8,264,128]{2,1,0:T(8,128)}, u32[]{:S(2)}, u32[]{:S(2)}) async-start(f32[8,264,128]{2,1,0:T(8,128)} %get-tuple-element.17), calls=%async_computation | async-start | bytes 2162688 | tf_op jit(solution)/shard_map/all_to_all | solution.py:262
  35.6 9.4 %collective-permute-done.low_ref = f32[18,32,256]{2,1,0:T(8,128)S(1)} collective-permute-done((f32[18,32,256]{2,1,0:T(8,128)S(1)}, f32[18,32,256]{2,1,0:T(8,128)S(1)}, u32[]{:S(2)}, u32[]{:S(2)}) %collective-permute-start) | collective-permute-done | bytes 589856 | tf_op jit(solution)/shard_map/ppermute | solution.py:221
  45.1 0.0 collective-permute-done.1.high_ref
  45.1 7.5 %filter_outer.1 = (f32[4,16,32,256]{3,2,1,0:T(8,128)}, f32[256,128]{1,0:T(8,128)S(1)}, f32[256,128]{1,0:T(8,128)S(1)}, f32[256,128]{1,0:T(8,128)S(1)}, f32[256,1...) custom-call(s32[1]{0:T(128)} %bitcast.mine_ref, ...), custom_call_target="tpu_custom_call", output_to_operand_aliasing={{0}: (8, {})} | custom-call | flops 399999991808 | bytes 400000000 | tf_op jit(solution)/shard_map/filter_outer/pallas_call | solution.py:265
  52.6 4.8 %collective-permute-start.2 = (f32[256,128]{1,0:T(8,128)S(1)}, f32[256,128]{1,0:T(8,128)S(1)}, u32[]{:S(2)}, u32[]{:S(2)}) collective-permute-start(f32[256,128]{1,0:T(8,128)S(1)} %get-tuple-element.18), channel_id=1, source_target_pairs={{0,1},{1,0},{2,3},{3,2},{4,5},{5,4},{6,7},{7,6},{8,9},{9,8},{10,11... | collective-permute-start | bytes 393224 | tf_op jit(solution)/shard_map/ppermute | solution.py:233
  57.4 1.9 %collective-permute-start.3 = (f32[256,128]{1,0:T(8,128)S(1)}, f32[256,128]{1,0:T(8,128)S(1)}, u32[]{:S(2)}, u32[]{:S(2)}) collective-permute-start(f32[256,128]{1,0:T(8,128)S(1)} %get-tuple-element.19), channel_id=1, source_target_pairs={{0,2},{1,3},{2,0},{3,1},{4,6},{5,7},{6,4},{7,5},{8,10},{9,11},{10,... | collective-permute-start | bytes 393224 | tf_op jit(solution)/shard_map/ppermute | solution.py:233
  59.3 4.5 %collective-permute-start.4 = (f32[256,128]{1,0:T(8,128)S(1)}, f32[256,128]{1,0:T(8,128)S(1)}, u32[]{:S(2)}, u32[]{:S(2)}) collective-permute-start(f32[256,128]{1,0:T(8,128)S(1)} %get-tuple-element.20), channel_id=1, source_target_pairs={{0,4},{1,5},{2,6},{3,7},{4,0},{5,1},{6,2},{7,3},{8,12},{9,13},{10,... | collective-permute-start | bytes 393224 | tf_op jit(solution)/shard_map/ppermute | solution.py:233
  63.9 2.1 %collective-permute-start.5 = (f32[256,128]{1,0:T(8,128)S(1)}, f32[256,128]{1,0:T(8,128)S(1)}, u32[]{:S(2)}, u32[]{:S(2)}) collective-permute-start(f32[256,128]{1,0:T(8,128)S(1)} %get-tuple-element.21), channel_id=1, source_target_pairs={{0,5},{1,4},{2,7},{3,6},{4,1},{5,0},{6,3},{7,2},{8,13},{9,12},{10,... | collective-permute-start | bytes 393224 | tf_op jit(solution)/shard_map/ppermute | solution.py:233
  66.0 4.7 %collective-permute-start.6 = (f32[256,128]{1,0:T(8,128)S(1)}, f32[256,128]{1,0:T(8,128)S(1)}, u32[]{:S(2)}, u32[]{:S(2)}) collective-permute-start(f32[256,128]{1,0:T(8,128)S(1)} %get-tuple-element.23), channel_id=1, source_target_pairs={{0,6},{1,7},{2,4},{3,5},{4,2},{5,3},{6,0},{7,1},{8,14},{9,15},{10,... | collective-permute-start | bytes 393224 | tf_op jit(solution)/shard_map/ppermute | solution.py:233
  70.6 0.0 collective-permute-done.2.rest_0_
  70.7 1.9 %collective-permute-start.7 = (f32[256,128]{1,0:T(8,128)S(1)}, f32[256,128]{1,0:T(8,128)S(1)}, u32[]{:S(2)}, u32[]{:S(2)}) collective-permute-start(f32[256,128]{1,0:T(8,128)S(1)} %get-tuple-element.24), channel_id=1, source_target_pairs={{0,7},{1,6},{2,5},{3,4},{4,3},{5,2},{6,1},{7,0},{8,15},{9,14},{10,... | collective-permute-start | bytes 393224 | tf_op jit(solution)/shard_map/ppermute | solution.py:233
  72.6 0.0 collective-permute-done.3.rest_1_
  72.6 4.2 %collective-permute-start.8 = (f32[256,128]{1,0:T(8,128)S(1)}, f32[256,128]{1,0:T(8,128)S(1)}, u32[]{:S(2)}, u32[]{:S(2)}) collective-permute-start(f32[256,128]{1,0:T(8,128)S(1)} %get-tuple-element.25), channel_id=1, source_target_pairs={{0,3},{1,2},{2,1},{3,0},{4,7},{5,6},{6,5},{7,4},{8,11},{9,10},{10,... | collective-permute-start | bytes 393224 | tf_op jit(solution)/shard_map/ppermute | solution.py:233
  76.8 3.0 %all-to-all-done.recv_ref = f32[8,264,128]{2,1,0:T(8,128)} async-done(((f32[8,264,128]{2,1,0:T(8,128)}), f32[8,264,128]{2,1,0:T(8,128)}, u32[]{:S(2)}, u32[]{:S(2)}) %all-to-all-start) | async-done | bytes 1081376 | tf_op jit(solution)/shard_map/all_to_all | solution.py:262
  79.8 0.8 slice.20
  80.5 3.3 %rotate_inner.1.rest_5_.rest_3_ = f32[16,16,4,256]{3,2,1,0:T(4,128)} custom-call(f32[8,64]{1,0:T(8,128)S(1)} %bitcast.6, f32[8,264,128]{2,1,0:T(8,128)} %all-to-all-done.recv_ref), custom_call_target="tpu_custom_call" | custom-call | flops 8000000 | bytes 1600000 | tf_op jit(solution)/shard_map/rotate_inner/pallas_call | solution.py:291
  83.8 0.0 collective-permute-done.4.rest_2_
  83.8 1.5 %collective-permute-done.5.rest_3_ = f32[256,128]{1,0:T(8,128)S(1)} collective-permute-done((f32[256,128]{1,0:T(8,128)S(1)}, f32[256,128]{1,0:T(8,128)S(1)}, u32[]{:S(2)}, u32[]{:S(2)}) %collective-permute-start.5) | collective-permute-done | bytes 131104 | tf_op jit(solution)/shard_map/ppermute | solution.py:233
  85.3 1.4 %rotate_soon.1.sums_ref = f32[2,64,8,128]{3,2,1,0:T(8,128)S(1)} custom-call(s32[1]{0:T(128)} %bitcast.mine_ref, f32[8,64]{1,0:T(8,128)S(1)} %bitcast.7, f32[256,128]{1,0:T(8,128)S(1)} %collective-permute-done.2.rest_0_, f32[256,128]{1,0:T(8,128)S(1)} %collective-permute-done.3.rest_1_, f32[256,128]{1,0:T(8,128)S(1)} %collective-permute-done.4.rest_2_, ...), custom_call_target="tpu_custom_call" | custom-call | flops 5000000 | bytes 1100000 | tf_op jit(solution)/shard_map/rotate_soon/pallas_call | solution.py:302
  86.7 5.8 %collective-permute-done.6.rest_0_ = f32[256,128]{1,0:T(8,128)S(1)} collective-permute-done((f32[256,128]{1,0:T(8,128)S(1)}, f32[256,128]{1,0:T(8,128)S(1)}, u32[]{:S(2)}, u32[]{:S(2)}) %collective-permute-start.6) | collective-permute-done | bytes 131104 | tf_op jit(solution)/shard_map/ppermute | solution.py:233
  92.5 2.8 %collective-permute-done.7.rest_1_ = f32[256,128]{1,0:T(8,128)S(1)} collective-permute-done((f32[256,128]{1,0:T(8,128)S(1)}, f32[256,128]{1,0:T(8,128)S(1)}, u32[]{:S(2)}, u32[]{:S(2)}) %collective-permute-start.7) | collective-permute-done | bytes 131104 | tf_op jit(solution)/shard_map/ppermute | solution.py:233
  95.3 0.0 collective-permute-done.8.rest_2_
  95.3 1.8 %rotate_last.1 = f32[16,16,4,256]{3,2,1,0:T(4,128)} custom-call(s32[1]{0:T(128)} %bitcast.mine_ref, f32[8,64]{1,0:T(8,128)S(1)} %bitcast.8, f32[2,64,8,128]{3,2,1,0:T(8,128)S(1)} %rotate_soon.1.sums_ref, f32[256,128]{1,0:T(8,128)S(1)} %collective-permute-done.6.rest_0_, ...), custom_call_target="tpu_custom_call", output_to_operand_aliasing={{}: (6, {})} | custom-call | flops 3000000 | bytes 1100000 | tf_op jit(solution)/shard_map/rotate_last/pallas_call | solution.py:312
  (3 shorter events, 0.1 us)
Async XLA Ops:
  1.5 21.0 %copy-start = (f32[4,16]{1,0:T(4,128)S(1)}, f32[4,16]{1,0:T(4,128)}, u32[]{:S(2)}) copy-start(f32[4,16]{1,0:T(4,128)} %param.9) | copy-start | bytes 772
  2.9 42.2 %collective-permute-start = (f32[18,32,256]{2,1,0:T(8,128)S(1)}, f32[18,32,256]{2,1,0:T(8,128)S(1)}, u32[]{:S(2)}, u32[]{:S(2)}) collective-permute-start(f32[18,32,256]{2,1,0:T(8,128)S(1)} %pad_maximum_fusion), channel_id=1, source_target_pairs={{0,8},{8,16},{16,24},{24,32},{32,40},{40,48},{48,56},{56,64},{64,7... | collective-permute-start | bytes 1769480 | tf_op jit(solution)/shard_map/ppermute | solution.py:221
  7.0 38.1 %collective-permute-start.1 = (f32[18,32,256]{2,1,0:T(8,128)S(1)}, f32[18,32,256]{2,1,0:T(8,128)S(1)}, u32[]{:S(2)}, u32[]{:S(2)}) collective-permute-start(f32[18,32,256]{2,1,0:T(8,128)S(1)} %pad_maximum_fusion.1), channel_id=1, source_target_pairs={{8,0},{16,8},{24,16},{32,24},{40,32},{48,40},{56,48},{64,56},{72,6... | collective-permute-start | bytes 1769480 | tf_op jit(solution)/shard_map/ppermute | solution.py:222
  28.8 51.0 %all-to-all-start = ((f32[8,264,128]{2,1,0:T(8,128)}), f32[8,264,128]{2,1,0:T(8,128)}, u32[]{:S(2)}, u32[]{:S(2)}) async-start(f32[8,264,128]{2,1,0:T(8,128)} %get-tuple-element.17), calls=%async_computation | async-start | bytes 2162688 | tf_op jit(solution)/shard_map/all_to_all | solution.py:262
  52.6 18.0 %collective-permute-start.2 = (f32[256,128]{1,0:T(8,128)S(1)}, f32[256,128]{1,0:T(8,128)S(1)}, u32[]{:S(2)}, u32[]{:S(2)}) collective-permute-start(f32[256,128]{1,0:T(8,128)S(1)} %get-tuple-element.18), channel_id=1, source_target_pairs={{0,1},{1,0},{2,3},{3,2},{4,5},{5,4},{6,7},{7,6},{8,9},{9,8},{10,11... | collective-permute-start | bytes 393224 | tf_op jit(solution)/shard_map/ppermute | solution.py:233
  57.4 15.2 %collective-permute-start.3 = (f32[256,128]{1,0:T(8,128)S(1)}, f32[256,128]{1,0:T(8,128)S(1)}, u32[]{:S(2)}, u32[]{:S(2)}) collective-permute-start(f32[256,128]{1,0:T(8,128)S(1)} %get-tuple-element.19), channel_id=1, source_target_pairs={{0,2},{1,3},{2,0},{3,1},{4,6},{5,7},{6,4},{7,5},{8,10},{9,11},{10,... | collective-permute-start | bytes 393224 | tf_op jit(solution)/shard_map/ppermute | solution.py:233
  59.3 24.5 %collective-permute-start.4 = (f32[256,128]{1,0:T(8,128)S(1)}, f32[256,128]{1,0:T(8,128)S(1)}, u32[]{:S(2)}, u32[]{:S(2)}) collective-permute-start(f32[256,128]{1,0:T(8,128)S(1)} %get-tuple-element.20), channel_id=1, source_target_pairs={{0,4},{1,5},{2,6},{3,7},{4,0},{5,1},{6,2},{7,3},{8,12},{9,13},{10,... | collective-permute-start | bytes 393224 | tf_op jit(solution)/shard_map/ppermute | solution.py:233
  63.9 21.4 %collective-permute-start.5 = (f32[256,128]{1,0:T(8,128)S(1)}, f32[256,128]{1,0:T(8,128)S(1)}, u32[]{:S(2)}, u32[]{:S(2)}) collective-permute-start(f32[256,128]{1,0:T(8,128)S(1)} %get-tuple-element.21), channel_id=1, source_target_pairs={{0,5},{1,4},{2,7},{3,6},{4,1},{5,0},{6,3},{7,2},{8,13},{9,12},{10,... | collective-permute-start | bytes 393224 | tf_op jit(solution)/shard_map/ppermute | solution.py:233
  66.0 26.5 %collective-permute-start.6 = (f32[256,128]{1,0:T(8,128)S(1)}, f32[256,128]{1,0:T(8,128)S(1)}, u32[]{:S(2)}, u32[]{:S(2)}) collective-permute-start(f32[256,128]{1,0:T(8,128)S(1)} %get-tuple-element.23), channel_id=1, source_target_pairs={{0,6},{1,7},{2,4},{3,5},{4,2},{5,3},{6,0},{7,1},{8,14},{9,15},{10,... | collective-permute-start | bytes 393224 | tf_op jit(solution)/shard_map/ppermute | solution.py:233
  70.7 24.6 %collective-permute-start.7 = (f32[256,128]{1,0:T(8,128)S(1)}, f32[256,128]{1,0:T(8,128)S(1)}, u32[]{:S(2)}, u32[]{:S(2)}) collective-permute-start(f32[256,128]{1,0:T(8,128)S(1)} %get-tuple-element.24), channel_id=1, source_target_pairs={{0,7},{1,6},{2,5},{3,4},{4,3},{5,2},{6,1},{7,0},{8,15},{9,14},{10,... | collective-permute-start | bytes 393224 | tf_op jit(solution)/shard_map/ppermute | solution.py:233
  72.6 22.7 %collective-permute-start.8 = (f32[256,128]{1,0:T(8,128)S(1)}, f32[256,128]{1,0:T(8,128)S(1)}, u32[]{:S(2)}, u32[]{:S(2)}) collective-permute-start(f32[256,128]{1,0:T(8,128)S(1)} %get-tuple-element.25), channel_id=1, source_target_pairs={{0,3},{1,2},{2,1},{3,0},{4,7},{5,6},{6,5},{7,4},{8,11},{9,10},{10,... | collective-permute-start | bytes 393224 | tf_op jit(solution)/shard_map/ppermute | solution.py:233
